TPU v7x, 32 devices: a whole 2x2x4 slice. The times are simulated.
32 devices in a mesh: groups: 2 (over x), row: 16 (over z, y, core).
Axes of the slice: x: 2, y: 2, z: 4, core: 2. Of those that a mesh axis runs over, the one named last changes fastest.
Arguments:
- homolog_features: bfloat16 [64, 512, 256], P(None, ('groups', 'row')), parts along dimension 1, may hold values from -6 to 6
- coverage_indicator: int32 [64, 512], P(None, ('groups', 'row')), parts along dimension 1, may hold values from 0 to 1, as said below
- couple_features: bfloat16 [512, 256, 128], P(('groups', 'row')), parts along dimension 0, may hold values from -6 to 6
- observed_indicator: int32 [512], P('groups'), parts along dimension 0, may hold values 0 or 1
- first_factor_matrix: bfloat16 [256, 32], replicated, may hold values from -0.375 to 0.375
- second_factor_matrix: bfloat16 [256, 32], replicated, may hold values from -0.375 to 0.375
- product_final_matrix: bfloat16 [1024, 128], replicated, may hold values from -0.5 to 0.5
- edge_projection_matrix: bfloat16 [128, 512], replicated, may hold values from -0.5 to 0.5
- sigmoid_filter_matrix: bfloat16 [128, 128], replicated, may hold values from -0.5 to 0.5
- multiplicative_final_matrix: bfloat16 [128, 128], replicated, may hold values from -0.5 to 0.5
Outputs:
- new_pair: bfloat16 [512, 256, 128], P(('groups', 'row')), parts along dimension 0
There are 2 independent parts, one for each index of `groups`. A program takes and returns all parts, laid end to end along the dimension named above; an argument that names none is the same for every part. Nothing has to cross between parts.
Inputs may be any that keep to these rules, and one draw needn't show every extreme that they name: `coverage_indicator`: each residue is covered by a leading run of sequences whose depth varies by residue, with gaps inside it; some residues have depth zero.
All inputs are finite; a program needn't handle non-finite values.
Results may differ from a plain program's by a relative error of at most 0.0064.
Values may be sent and summed in bfloat16 or wider, within the bound.
No kernel may reach another device: no remote copies, remote signals or barrier semaphores. Data moves between devices by JAX's collectives and lax.ppermute only.
A program may use at most 128 MiB of HBM per device.

v0:
```python
import jax
import jax.numpy as jnp
from jax import lax
from jax.sharding import PartitionSpec as P


def standardize_module(value):
    mean = jnp.mean(value, axis=-1, keepdims=True)
    centred = value - mean
    var = jnp.mean(centred * centred, axis=-1, keepdims=True)
    return centred * lax.rsqrt(var + 1e-05)


def triangle_product(whole_a, whole_b):
    return jnp.einsum(
        "uncik,umcjk->ucnimj", whole_a, whole_b, preferred_element_type=jnp.float32
    ).astype(jnp.bfloat16)


def body(
    homolog_features,
    coverage_indicator,
    couple_features,
    observed_indicator,
    first_factor_matrix,
    second_factor_matrix,
    product_final_matrix,
    edge_projection_matrix,
    sigmoid_filter_matrix,
    multiplicative_final_matrix,
):
    float_thirty_two = jnp.float32
    homolog_entries, local_amino_acids, homolog_feature_dim = homolog_features.shape
    proj_width = first_factor_matrix.shape[1]
    hidden = multiplicative_final_matrix.shape[0]
    total_res = observed_indicator.shape[0]
    n_dev = lax.axis_size("row")
    chan_local = hidden // n_dev
    rows_of_mask = coverage_indicator.T.astype(float_thirty_two)
    homolog_standardizer = standardize_module(homolog_features.astype(float_thirty_two)).astype(
        jnp.bfloat16
    )
    left_side = (
        jnp.einsum(
            "gwn,nd->wgd",
            homolog_standardizer,
            first_factor_matrix,
            preferred_element_type=float_thirty_two,
        )
        * rows_of_mask[..., None]
    ).astype(jnp.bfloat16)
    right_side = (
        jnp.einsum(
            "gwn,nd->wgd",
            homolog_standardizer,
            second_factor_matrix,
            preferred_element_type=float_thirty_two,
        )
        * rows_of_mask[..., None]
    ).astype(jnp.bfloat16)
    right_flat = right_side.reshape(local_amino_acids, homolog_entries * proj_width)
    mask_send = rows_of_mask.astype(jnp.bfloat16)
    right_piece = lax.all_gather(right_flat, "row", axis=0, tiled=True)
    mask_piece = lax.all_gather(mask_send, "row", axis=0, tiled=True)
    count_cols = mask_piece.shape[0]
    right_cols = right_piece.reshape(count_cols, homolog_entries, proj_width)

    def one_row(items):
        left_row, mask_row = items
        outer = jnp.einsum(
            "sp,jsq->jpq", left_row, right_cols, preferred_element_type=float_thirty_two
        ).astype(jnp.bfloat16)
        outer = outer.reshape(count_cols, proj_width * proj_width)
        update = jnp.dot(outer, product_final_matrix, preferred_element_type=float_thirty_two)
        count = jnp.dot(mask_piece, mask_row, preferred_element_type=float_thirty_two)
        return update / jnp.maximum(count, 1.0)[:, None]

    update = lax.map(one_row, (left_side, mask_send))
    pair_one = couple_features.astype(float_thirty_two) + update
    pair_norm = standardize_module(pair_one).astype(jnp.bfloat16)
    resid = observed_indicator.astype(float_thirty_two)
    row_start = lax.axis_index("row") * local_amino_acids
    resid_rows = lax.dynamic_slice_in_dim(resid, row_start, local_amino_acids)
    pair_mask = (resid_rows[:, None] * resid[None, :])[None]

    def make_side(offset):
        gate_part = jnp.einsum(
            "ijc,cd->dij",
            pair_norm,
            edge_projection_matrix[:, offset : offset + hidden],
            preferred_element_type=float_thirty_two,
        )
        value_part = jnp.einsum(
            "ijc,cd->dij",
            pair_norm,
            edge_projection_matrix[:, offset + hidden : offset + 2 * hidden],
            preferred_element_type=float_thirty_two,
        )
        side = (jax.nn.sigmoid(gate_part) * value_part * pair_mask).astype(jnp.bfloat16)
        return side.reshape(n_dev, 1, chan_local, local_amino_acids, total_res)

    side_a = make_side(0)
    side_b = make_side(2 * hidden)
    tri_cols = triangle_product(
        lax.all_to_all(side_a, "row", split_axis=0, concat_axis=1, tiled=True),
        lax.all_to_all(side_b, "row", split_axis=0, concat_axis=1, tiled=True),
    )
    tri_cols = tri_cols.reshape(1, chan_local, n_dev, local_amino_acids, total_res)
    tri_back = lax.all_to_all(tri_cols, "row", split_axis=2, concat_axis=0, tiled=True)
    tri = tri_back.reshape(hidden, local_amino_acids, total_res).transpose(1, 2, 0)
    tri_norm = standardize_module(tri.astype(float_thirty_two)).astype(jnp.bfloat16)
    gate = jax.nn.sigmoid(
        jnp.einsum(
            "ijc,cd->ijd", pair_norm, sigmoid_filter_matrix, preferred_element_type=float_thirty_two
        )
    )
    result = pair_one + gate * jnp.einsum(
        "ijh,hc->ijc",
        tri_norm,
        multiplicative_final_matrix,
        preferred_element_type=float_thirty_two,
    )
    return result.astype(jnp.bfloat16)


def solution(mesh):
    placed = (
        P(None, ("groups", "row"), None),
        P(None, ("groups", "row")),
        P(("groups", "row"), None, None),
        P("groups"),
        P(),
        P(),
        P(),
        P(),
        P(),
        P(),
    )
    return jax.shard_map(
        body,
        mesh=mesh,
        in_specs=placed,
        out_specs=P(("groups", "row"), None, None),
        check_vma=False,
    )
```

profile of v0, /device:TPU:0, one launch (start us, length us, event | category | flops | bytes accessed | tf_op | source)
XLA Modules:
  0.0 216.0 jit_solution(8441395237159149204)
XLA Ops:
  10.1 1.5 fusion.19
  13.5 23.3 %all_gather.7 = bf16[256,64]{1,0:T(8,128)(2,1)S(1)} all-gather(bf16[16,64]{1,0:T(8,128)(2,1)S(1)} %get-tuple-element.128), channel_id=1, replica_groups=mesh['groups'=2,'row'=16] {'row'}, dimensions={0}, use_global_device_ids=true | all-gather | bytes 34816 | tf_op jit(solution)/shard_map/all_gather | solution.py:64
  36.9 16.6 %all-gather.2.cloned.1.call-done = bf16[256,2048]{1,0:T(8,128)(2,1)} async-done(((bf16[16,2048]{1,0:T(8,128)(2,1)}), bf16[256,2048]{1,0:T(8,128)(2,1)}) %all-gather.2.cloned.1.call-update) | async-done | bytes 1048592 | tf_op jit(solution)/shard_map/all_gather | solution.py:63
  53.5 2.3 %copy.47 = bf16[256,2048]{0,1:T(8,128)(2,1)} copy(bf16[256,2048]{1,0:T(8,128)(2,1)} %all-gather.2.cloned.1.call-done) | data formatting | bytes 2097152 | tf_op jit(solution)/shard_map/all_gather | solution.py:63
  55.7 1.8 copy.49
  57.6 21.0 %while.10 = (s32[]{:T(128)}, f32[16,256,128]{2,1,0:T(8,128)S(1)}, bf16[16,64,32]{1,2,0:T(8,128)(2,1)S(1)}, bf16[256,64,32]{0,1,2:T(8,128)(2,1)S(1)}, bf16[1024,1...) while((s32[]{:T(128)}, f32[16,256,128]{2,1,0:T(8,128)S(1)}, ...), condition=%wide.region_3.4_spmd, body=%wide.region_2.3_spmd.sunk | while | flops 100991232 | bytes 4665981 | solution.py:78
  78.5 1.9 fusion.30
  83.5 1.7 fusion.13
  85.2 2.7 %copy.54 = bf16[128,16,256]{2,1,0:T(8,128)(2,1)} copy(bf16[128,16,256]{0,2,1:T(8,128)(2,1)} %fusion.13) | data formatting | bytes 2097152 | tf_op jit(solution)/shard_map/convert_element_type | solution.py:99
  87.9 4.4 %all-to-all-start = ((bf16[16,1,8,16,256]{4,3,2,1,0:T(8,128)(2,1)}), bf16[16,1,8,16,256]{4,3,2,1,0:T(8,128)(2,1)}, u32[]{:S(2)}, u32[]{:S(2)}) async-start(bf16[16,1,8,16,256]{4,3,2,1,0:T(8,128)(2,1)} %bitcast.139), calls=%async_computation | async-start | bytes 2097152 | tf_op jit(solution)/shard_map/all_to_all | solution.py:105
  92.7 1.7 fusion.14
  94.3 2.7 %copy.61 = bf16[128,16,256]{2,1,0:T(8,128)(2,1)} copy(bf16[128,16,256]{0,2,1:T(8,128)(2,1)} %fusion.14) | data formatting | bytes 2097152 | tf_op jit(solution)/shard_map/convert_element_type | solution.py:99
  97.0 18.2 %all-to-all-done = bf16[16,1,8,16,256]{4,3,2,1,0:T(8,128)(2,1)} async-done(((bf16[16,1,8,16,256]{4,3,2,1,0:T(8,128)(2,1)}), bf16[16,1,8,16,256]{4,3,2,1,0:T(8,128)(2,1)}, u32[]{:S(2)}, u32[]{:S(2)}) %all-to-all-start) | async-done | bytes 1048608 | tf_op jit(solution)/shard_map/all_to_all | solution.py:105
  115.2 31.7 %all_to_all.12 = bf16[16,1,8,16,256]{4,3,2,1,0:T(8,128)(2,1)S(1)} all-to-all(bf16[16,1,8,16,256]{4,3,2,1,0:T(8,128)(2,1)} %bitcast.140), channel_id=1, replica_groups=mesh['groups'=2,'row'=16] {'row'}, dimensions={0} | all-to-all | bytes 2097152 | tf_op jit(solution)/shard_map/all_to_all | solution.py:106
  146.8 5.8 %convolution_convert_fusion.1 = bf16[8,16,16,16,16]{4,2,3,1,0:T(8,128)(2,1)} fusion(bf16[16,1,8,16,256]{4,3,2,1,0:T(8,128)(2,1)S(1)} %all_to_all.12, bf16[16,1,8,16,256]{4,3,2,1,0:T(8,128)(2,1)} %all-to-all-done), kind=kOutput, calls=%fused_computation.12 | convolution fusion | flops 268959744 | bytes 3145728 | tf_op jit(solution)/shard_map/uncik,umcjk->ucnimj/dot_general | solution.py:15
  152.6 10.8 %copy.74 = bf16[8,16,16,16,16]{4,3,2,0,1:T(8,128)(2,1)} copy(bf16[8,16,16,16,16]{4,2,3,1,0:T(8,128)(2,1)} %convolution_convert_fusion.1) | data formatting | bytes 2097152 | tf_op jit(solution)/shard_map/reshape | solution.py:108
  163.4 11.0 %reshape.128 = bf16[1,8,16,16,256]{4,3,1,0,2:T(8,128)(2,1)} reshape(bf16[8,16,16,16,16]{4,3,2,0,1:T(8,128)(2,1)} %copy.74) | data formatting | bytes 2097152 | tf_op jit(solution)/shard_map/reshape | solution.py:108
  174.5 5.0 %all-to-all-start.2 = ((bf16[1,8,16,16,256]{4,3,1,0,2:T(8,128)(2,1)}), bf16[1,8,16,16,256]{4,3,1,0,2:T(8,128)(2,1)}, u32[]{:S(2)}, u32[]{:S(2)}) async-start(bf16[1,8,16,16,256]{4,3,1,0,2:T(8,128)(2,1)} %reshape.128), calls=%async_computation.2 | async-start | bytes 2097152 | tf_op jit(solution)/shard_map/all_to_all | solution.py:109
  179.5 1.8 fusion.38
  181.3 21.2 %all-to-all-done.2 = bf16[1,8,16,16,256]{4,3,1,0,2:T(8,128)(2,1)} async-done(((bf16[1,8,16,16,256]{4,3,1,0,2:T(8,128)(2,1)}), bf16[1,8,16,16,256]{4,3,1,0,2:T(8,128)(2,1)}, u32[]{:S(2)}, u32[]{:S(2)}) %all-to-all-start.2) | async-done | bytes 1048608 | tf_op jit(solution)/shard_map/all_to_all | solution.py:109
  202.5 1.6 bitcast_reduce_fusion
  204.1 1.6 fusion.11
  205.6 1.5 fusion.12
  207.2 2.0 add_convert_fusion
  (154 shorter events, 29.2 us)
Async XLA Ops:
  6.5 173.0 %copy-start = (bf16[128,128]{1,0:T(8,128)(2,1)S(1)}, bf16[128,128]{1,0:T(8,128)(2,1)}, u32[]{:S(2)}) copy-start(bf16[128,128]{1,0:T(8,128)(2,1)} %param.20) | copy-start | bytes 98308
  6.5 6.1 %copy-start.4 = (bf16[64,16,256]{2,1,0:T(8,128)(2,1)S(1)}, bf16[64,16,256]{2,1,0:T(8,128)(2,1)}, u32[]{:S(2)}) copy-start(bf16[64,16,256]{2,1,0:T(8,128)(2,1)} %param.12) | copy-start | bytes 1572868
  6.5 6.1 %copy-start.9 = (bf16[256,32]{0,1:T(8,128)(2,1)S(1)}, bf16[256,32]{0,1:T(8,128)(2,1)}, u32[]{:S(2)}) copy-start(bf16[256,32]{0,1:T(8,128)(2,1)} %param.16) | copy-start | bytes 49156
  6.5 46.9 %all-gather.2.cloned.1.call-start = ((), (), s32[]{:S(2)}) async-start(), calls=%async_computation.3 | async-start | bytes 1114112 | tf_op jit(solution)/shard_map/all_gather | solution.py:63
  10.1 3.4 %copy-start.6 = (s32[256]{0:T(256)S(1)}, s32[256]{0:T(256)}, u32[]{:S(2)}) copy-start(s32[256]{0:T(256)} %param.15) | copy-start | bytes 3076
  57.6 1.0 copy-start.7
  58.9 1.0 copy-start.7
  60.2 1.0 copy-start.7
  61.5 1.0 copy-start.7
  62.8 1.0 copy-start.7
  64.1 1.0 copy-start.7
  65.4 1.0 copy-start.7
  66.7 1.0 copy-start.7
  68.0 1.0 copy-start.7
  69.3 1.0 copy-start.7
  70.7 1.0 copy-start.7
  72.0 1.0 copy-start.7
  78.5 2.0 copy-start.1
  81.8 1.3 copy-start.5
  87.9 27.3 %all-to-all-start = ((bf16[16,1,8,16,256]{4,3,2,1,0:T(8,128)(2,1)}), bf16[16,1,8,16,256]{4,3,2,1,0:T(8,128)(2,1)}, u32[]{:S(2)}, u32[]{:S(2)}) async-start(bf16[16,1,8,16,256]{4,3,2,1,0:T(8,128)(2,1)} %bitcast.139), calls=%async_computation | async-start | bytes 2097152 | tf_op jit(solution)/shard_map/all_to_all | solution.py:105
  174.5 28.0 %all-to-all-start.2 = ((bf16[1,8,16,16,256]{4,3,1,0,2:T(8,128)(2,1)}), bf16[1,8,16,16,256]{4,3,1,0,2:T(8,128)(2,1)}, u32[]{:S(2)}, u32[]{:S(2)}) async-start(bf16[1,8,16,16,256]{4,3,1,0,2:T(8,128)(2,1)} %reshape.128), calls=%async_computation.2 | async-start | bytes 2097152 | tf_op jit(solution)/shard_map/all_to_all | solution.py:109
  181.3 25.9 %copy-start.2 = (bf16[16,256,128]{2,1,0:T(8,128)(2,1)S(1)}, bf16[16,256,128]{2,1,0:T(8,128)(2,1)}, u32[]{:S(2)}) copy-start(bf16[16,256,128]{2,1,0:T(8,128)(2,1)} %param.14) | copy-start | bytes 3145732
  181.3 25.9 %copy-start.8 = (bf16[128,128]{1,0:T(8,128)(2,1)S(1)}, bf16[128,128]{1,0:T(8,128)(2,1)}, u32[]{:S(2)}) copy-start(bf16[128,128]{1,0:T(8,128)(2,1)} %param.21) | copy-start | bytes 98308
  202.5 4.7 %copy-start.3 = (f32[16,256,128]{2,1,0:T(8,128)S(1)}, f32[16,256,128]{2,1,0:T(8,128)}, u32[]{:S(2)}) copy-start(f32[16,256,128]{2,1,0:T(8,128)} %fusion.38) | copy-start | bytes 6291460
  (4 other events, 3.8 us)
Sparse Core Ops, SparseCore 0:
  12.8 40.6 all-gather.1
where the time goes:
time: 219 us; the launch traced here: 216 us
  waiting for transfers between devices  56 us (26%)
  blocking collectives  54.9 us (25%)
  local copies, waits for them, and re-layouts  40.8 us (19%)
  matrix products  27.8 us (13%)
  between operations  13.6 us (6%)
  other arithmetic  12.8 us (6%)
  starting transfers between devices  9.4 us (4%)
    all_to_all x1, blocking collectives, body(): lax.all_to_all(side_b, 'row', split_axis=0, concat_axis=1, tiled=True)  31.7 us
    all_gather x1, blocking collectives, body(): mask_piece = lax.all_gather(mask_send, 'row', axis=0, tiled=True)  23.3 us
    reshape x2, local copies, waits for them, and re-layouts, body(): tri_cols.reshape(1, chan_local, n_dev, local_amino_acids, total_res)  21.8 us
    all_to_all x1, waiting for transfers between devices, body(): lax.all_to_all(tri_cols, 'row', split_axis=2, concat_axis=0, tiled=True)  21.2 us
    all_to_all x1, waiting for transfers between devices, body(): lax.all_to_all(side_a, 'row', split_axis=0, concat_axis=1, tiled=True)  18.2 us
    all_gather x1, waiting for transfers between devices, body(): right_piece = lax.all_gather(right_flat, 'row', axis=0, tiled=True)  16.6 us
    dot_general x1, matrix products, triangle_product(): jnp.einsum('uncik,umcjk->ucnimj', whole_a, whole_b, preferred_element_typ...  5.76 us
    dot_general x16, matrix products, one_row(): jnp.dot(outer, product_final_matrix, preferred_element_type=float_thirty_...  5.39 us
  transfers between devices with their start and end apart: 3, of which 3 were waited for; matrix products, arithmetic and copies ran while one was open for 3% of the time, Pallas kernels for 0%

commit v1 on v0

v1 whole, which is shorter than its diff:
```python
import jax
import jax.numpy as jnp
from jax import lax
from jax.experimental import pallas as pl
from jax.experimental.pallas import tpu as pltpu
from jax.sharding import PartitionSpec as P

F32 = jnp.float32
BF16 = jnp.bfloat16
LANES = 128
NT = (((1,), (1,)), ((), ()))
VMEM_LIMIT = 56 * 1024 * 1024


def params(steps=1):
    return pltpu.CompilerParams(
        vmem_limit_bytes=VMEM_LIMIT, dimension_semantics=("arbitrary",) * steps
    )


def sigmoid(value):
    return 0.5 * jnp.tanh(0.5 * value) + 0.5


def standardize(value, axis):
    mean = jnp.mean(value, axis=axis, keepdims=True)
    centred = value - mean
    var = jnp.mean(centred * centred, axis=axis, keepdims=True)
    return centred * lax.rsqrt(var + 1e-05)


def pair_kernel(
    left_ref, right_ref, mask_ref, couple_ref, w_out_ref, w_in_ref, obs_ref,
    pair_ref, norm_ref, a_ref, b_ref, outer, scratch_a, scratch_b,
):
    rows, block, width = couple_ref.shape
    hidden = a_ref.shape[0]
    tiles = block // LANES
    pairs = right_ref.shape[1] - 1
    proj = w_out_ref.shape[1] // (2 * pairs)

    def right_slice(index):
        return right_ref[:, pl.ds(index, 1)].reshape(block, LANES)

    @pl.loop(0, pairs)
    def _(t):
        both = lax.dot_general(
            left_ref[...], right_slice(t), NT, preferred_element_type=F32
        ).astype(BF16)
        half = rows * proj
        for e in range(2):
            outer[:, pl.ds(pl.multiple_of((2 * t + e) * proj, proj), proj), :] = both[
                e * half : (e + 1) * half
            ].reshape(rows, proj, block)

    count = lax.dot_general(mask_ref[...], right_slice(pairs), NT, preferred_element_type=F32)
    scale = 1.0 / jnp.maximum(count, 1.0)

    for i in range(rows):
        update = jnp.dot(w_out_ref[...], outer[i], preferred_element_type=F32)
        pair = couple_ref[i].astype(F32).T + update * scale[i : i + 1]
        pair_ref[i] = pair
        norm = standardize(pair, 0).astype(BF16)
        norm_ref[i] = norm
        sides = jnp.dot(w_in_ref[...], norm, preferred_element_type=F32)
        seen = obs_ref[i : i + 1]
        side_a = sigmoid(sides[:hidden]) * sides[hidden : 2 * hidden] * seen
        side_b = sigmoid(sides[2 * hidden : 3 * hidden]) * sides[3 * hidden :] * seen
        for tile in range(tiles):
            cols = slice(tile * LANES, (tile + 1) * LANES)
            scratch_a[tile, i * hidden : (i + 1) * hidden] = side_a[:, cols]
            scratch_b[tile, i * hidden : (i + 1) * hidden] = side_b[:, cols]

    @pl.loop(0, hidden, unroll=8)
    def _(d):
        for tile in range(tiles):
            cols = slice(tile * LANES, (tile + 1) * LANES)
            a_ref[d, :, cols] = scratch_a[tile, pl.ds(d, rows, stride=hidden), :].astype(BF16)
            b_ref[d, :, cols] = scratch_b[tile, pl.ds(d, rows, stride=hidden), :].astype(BF16)


def pair_stage(left, right, mask, couple, w_out, w_in, obs):
    rows, total, width = couple.shape
    block = 2 * LANES
    devs = block // rows
    hidden = w_in.shape[0] // 4
    return pl.pallas_call(
        pair_kernel,
        grid=(total // block,),
        in_specs=[
            pl.BlockSpec(left.shape, lambda j: (0, 0)),
            pl.BlockSpec((devs,) + right.shape[1:], lambda j: (j, 0, 0, 0)),
            pl.BlockSpec(mask.shape, lambda j: (0, 0)),
            pl.BlockSpec((rows, block, width), lambda j: (0, j, 0)),
            pl.BlockSpec(w_out.shape, lambda j: (0, 0)),
            pl.BlockSpec(w_in.shape, lambda j: (0, 0)),
            pl.BlockSpec((rows, block), lambda j: (0, j)),
        ],
        out_specs=[
            pl.BlockSpec((rows, width, block), lambda j: (0, 0, j)),
            pl.BlockSpec((rows, width, block), lambda j: (0, 0, j)),
            pl.BlockSpec((hidden, rows, block), lambda j: (0, 0, j)),
            pl.BlockSpec((hidden, rows, block), lambda j: (0, 0, j)),
        ],
        out_shape=[
            jax.ShapeDtypeStruct((rows, width, total), F32),
            jax.ShapeDtypeStruct((rows, width, total), BF16),
            jax.ShapeDtypeStruct((hidden, rows, total), BF16),
            jax.ShapeDtypeStruct((hidden, rows, total), BF16),
        ],
        scratch_shapes=[
            pltpu.VMEM((rows, w_out.shape[1], block), BF16),
            pltpu.VMEM((block // LANES, rows * hidden, LANES), F32),
            pltpu.VMEM((block // LANES, rows * hidden, LANES), F32),
        ],
        compiler_params=params(),
        cost_estimate=pl.CostEstimate(
            flops=4 * rows * total * w_out.shape[1] * width,
            bytes_accessed=16 * rows * total * width,
            transcendentals=2 * rows * total * hidden,
        ),
        name="pair_stage",
    )(left, right, mask, couple, w_out, w_in, obs)


def gate_kernel(norm_ref, w_ref, gate_ref):
    for i in range(norm_ref.shape[0]):
        gate_ref[i] = sigmoid(jnp.dot(w_ref[...], norm_ref[i], preferred_element_type=F32))


def gate_stage(norm, weight):
    rows, width, total = norm.shape
    block = 2 * LANES
    spec = pl.BlockSpec((rows, width, block), lambda j: (0, 0, j))
    return pl.pallas_call(
        gate_kernel,
        grid=(total // block,),
        in_specs=[spec, pl.BlockSpec(weight.shape, lambda j: (0, 0))],
        out_specs=spec,
        out_shape=jax.ShapeDtypeStruct((rows, width, total), F32),
        compiler_params=params(),
        cost_estimate=pl.CostEstimate(
            flops=2 * rows * total * width * width,
            bytes_accessed=6 * rows * total * width,
            transcendentals=rows * total * width,
        ),
        name="gate_stage",
    )(norm, weight)


def tri_kernel(a_ref, b_ref, out_ref):
    parts, chans, rows, total = a_ref.shape
    for c in range(chans):
        product = lax.dot_general(
            a_ref[:, c].reshape(parts * rows, total),
            b_ref[:, c].reshape(parts * rows, total),
            NT,
            preferred_element_type=F32,
        )
        out_ref[:, c] = product.astype(BF16).reshape(out_ref.shape[0], rows, -1)


def tri_stage(side_a, side_b):
    parts, chans, rows, total = side_a.shape
    step = max(1, min(chans, chans * 256 // total))
    spec = pl.BlockSpec((parts, step, rows, total), lambda c: (0, c, 0, 0))
    return pl.pallas_call(
        tri_kernel,
        grid=(chans // step,),
        in_specs=[spec, spec],
        out_specs=spec,
        out_shape=jax.ShapeDtypeStruct(side_a.shape, BF16),
        compiler_params=params(),
        cost_estimate=pl.CostEstimate(
            flops=2 * chans * total**3, bytes_accessed=6 * chans * total**2, transcendentals=0
        ),
        name="tri_stage",
    )(side_a, side_b)


def final_kernel(tri_ref, pair_ref, gate_ref, w_ref, out_ref, normed):
    hidden, rows, block = tri_ref.shape
    tiles = block // LANES
    tri = tri_ref[...].astype(F32)
    values = standardize(tri, 0)
    for tile in range(tiles):
        normed[tile] = values[:, :, tile * LANES : (tile + 1) * LANES].reshape(hidden * rows, LANES)
    for i in range(rows):
        columns = jnp.concatenate(
            [normed[tile, pl.ds(i, hidden, stride=rows), :] for tile in range(tiles)], axis=1
        ).astype(BF16)
        update = jnp.dot(w_ref[...], columns, preferred_element_type=F32)
        result = pair_ref[i] + gate_ref[i] * update
        out_ref[i] = result.T.astype(BF16)


def final_stage(tri, pair, gate, weight):
    hidden, rows, total = tri.shape
    width = weight.shape[0]
    block = 2 * LANES
    spec = pl.BlockSpec((rows, width, block), lambda j: (0, 0, j))
    return pl.pallas_call(
        final_kernel,
        grid=(total // block,),
        in_specs=[
            pl.BlockSpec((hidden, rows, block), lambda j: (0, 0, j)),
            spec,
            spec,
            pl.BlockSpec(weight.shape, lambda j: (0, 0)),
        ],
        out_specs=pl.BlockSpec((rows, block, width), lambda j: (0, j, 0)),
        out_shape=jax.ShapeDtypeStruct((rows, total, width), BF16),
        scratch_shapes=[pltpu.VMEM((block // LANES, hidden * rows, LANES), F32)],
        compiler_params=params(),
        cost_estimate=pl.CostEstimate(
            flops=2 * rows * total * hidden * width,
            bytes_accessed=12 * rows * total * width,
            transcendentals=0,
        ),
        name="final_stage",
    )(tri, pair, gate, weight)


def gather_blocks(block):
    devs = lax.axis_size("row")
    if devs != 16:
        return lax.all_gather(block, "row", axis=0)

    def hop(value, step):
        return lax.ppermute(value, "row", [(i, (i + step) % devs) for i in range(devs)])

    def flip(value, bit):
        return lax.ppermute(value, "row", [(i, i ^ bit) for i in range(devs)])

    held = jnp.stack([block, hop(block, 4), hop(block, 8), hop(block, 12)])
    held = jnp.stack([held, flip(held, 2)], axis=1)
    held = jnp.stack([held, flip(held, 1)], axis=2)
    me = lax.axis_index("row")
    z, y, core = me // 4, (me // 2) % 2, me % 2
    place = jnp.arange(devs)
    source = ((z - place // 4) % 4) * 4 + ((y ^ (place // 2 % 2)) * 2) + (core ^ (place % 2))
    slot = jnp.argsort(source)
    return jnp.take(held.reshape((devs,) + block.shape), slot, axis=0)


def body(
    homolog_features,
    coverage_indicator,
    couple_features,
    observed_indicator,
    first_factor_matrix,
    second_factor_matrix,
    product_final_matrix,
    edge_projection_matrix,
    sigmoid_filter_matrix,
    multiplicative_final_matrix,
):
    seqs, rows, breadth = homolog_features.shape
    proj = first_factor_matrix.shape[1]
    width = couple_features.shape[2]
    hidden = multiplicative_final_matrix.shape[0]
    total = observed_indicator.shape[0]
    devs = lax.axis_size("row")
    chans = hidden // devs

    covered = coverage_indicator.astype(F32)
    msa_norm = standardize(homolog_features.astype(F32), -1).astype(BF16)

    def project(weight):
        value = jnp.einsum("sif,fp->sip", msa_norm, weight, preferred_element_type=F32)
        return (value * covered[..., None]).astype(BF16)

    right = project(second_factor_matrix).reshape(seqs, rows, proj // 2, 2)
    right = right.transpose(2, 1, 3, 0).reshape(proj // 2, rows, 2 * seqs)
    mask = jnp.pad(covered.T.astype(BF16), ((0, 0), (0, seqs)))
    gathered = gather_blocks(jnp.concatenate([right, mask[None]]))

    left = project(first_factor_matrix).transpose(1, 2, 0).reshape(rows * proj, seqs)
    left = jnp.concatenate(
        [jnp.pad(left, ((0, 0), (0, seqs))), jnp.pad(left, ((0, 0), (seqs, 0)))]
    )
    w_out = product_final_matrix.reshape(proj, proj, width).transpose(2, 1, 0)
    w_out = w_out.reshape(width, proj * proj)

    seen = observed_indicator.astype(F32)
    start = lax.axis_index("row") * rows
    obs = lax.dynamic_slice_in_dim(seen, start, rows)[:, None] * seen[None, :]

    pair, norm, side_a, side_b = pair_stage(
        left, gathered, mask, couple_features, w_out, edge_projection_matrix.T, obs
    )

    def spread(side):
        side = side.reshape(devs, chans, rows, total)
        return lax.all_to_all(side, "row", split_axis=0, concat_axis=0, tiled=True)

    tri = tri_stage(spread(side_a), spread(side_b))
    gate = gate_stage(norm, sigmoid_filter_matrix.T)
    tri = lax.all_to_all(tri, "row", split_axis=0, concat_axis=0, tiled=True)
    return final_stage(
        tri.reshape(hidden, rows, total), pair, gate, multiplicative_final_matrix.T
    )


def solution(mesh):
    placed = (
        P(None, ("groups", "row"), None),
        P(None, ("groups", "row")),
        P(("groups", "row"), None, None),
        P("groups"),
        P(),
        P(),
        P(),
        P(),
        P(),
        P(),
    )
    return jax.shard_map(
        body,
        mesh=mesh,
        in_specs=placed,
        out_specs=P(("groups", "row"), None, None),
        check_vma=False,
    )
```

time: 219 us -> 142 us (0.65)
  local copies, waits for them, and re-layouts: 40.8 us -> 6.78 us
  waiting for transfers between devices: 56 us -> 27.7 us
  matrix products: 27.8 us -> 0.96 us
  Pallas kernels: 0 us -> 25.7 us
  between operations: 13.6 us -> 0.24 us
  other arithmetic: 12.8 us -> 6.93 us
  blocking collectives: 54.9 us -> 58.9 us
  starting transfers between devices: 9.4 us -> 12.9 us
    all_to_all x1 -> x2, blocking collectives: 31.7 us -> 58.9 us  [spread(): return lax.all_to_all(side, 'row', split_axis=0, concat_axis=0, tiled=True)]
    dot_general x57 -> x2, matrix products: 27.8 us -> 0.96 us  [project(): jnp.einsum('sif,fp->sip', msa_norm, weight, preferred_element_type=F32)]
    pallas_call x0 -> x4, Pallas kernels: none -> 25.7 us  [the longest x1 14.6 us: pair_stage(): pl.pallas_call(pair_kernel, grid=(total // block,), in_specs=[pl.BlockSpe...]
    all_gather x1 -> x0, blocking collectives: 23.3 us -> none  [body(): mask_piece = lax.all_gather(mask_send, 'row', axis=0, tiled=True)]
    reshape x3 -> x2, local copies, waits for them, and re-layouts: 22.8 us -> 0.97 us  [the longest x1 0.86 us: body(): w_out = w_out.reshape(width, proj * proj)]
    all_to_all x2 -> x1, waiting for transfers between devices: 39.4 us -> 18.5 us  [body(): tri = lax.all_to_all(tri, 'row', split_axis=0, concat_axis=0, tiled=True)]
    all_gather x1 -> x0, waiting for transfers between devices: 16.6 us -> none  [body(): right_piece = lax.all_gather(right_flat, 'row', axis=0, tiled=True)]
    convert_element_type x20 -> x3, local copies, waits for them, and re-layouts: 10.2 us -> 0.68 us  [the longest x2 0.59 us: project(): return (value * covered[..., None]).astype(BF16)]
  transfers between devices with their start and end apart: 3 -> 6, of which waited for: 3 -> 4; matrix products, arithmetic and copies ran while one was open for 3% -> 5% of each run, Pallas kernels for 0% -> 2%
where the time goes in v1:
time: 142 us; the launch traced here: 140 us
  blocking collectives  58.9 us (41%)
  waiting for transfers between devices  27.7 us (20%)
  Pallas kernels  25.7 us (18%)
  starting transfers between devices  12.9 us (9%)
  other arithmetic  6.93 us (5%)
  local copies, waits for them, and re-layouts  6.78 us (5%)
    all_to_all x2, blocking collectives, spread(): return lax.all_to_all(side, 'row', split_axis=0, concat_axis=0, tiled=True)  58.9 us
    all_to_all x1, waiting for transfers between devices, body(): tri = lax.all_to_all(tri, 'row', split_axis=0, concat_axis=0, tiled=True)  18.5 us
    pallas_call x1, Pallas kernels, pair_stage(): pl.pallas_call(pair_kernel, grid=(total // block,), in_specs=[pl.BlockSpe...  14.6 us
    ppermute x3, starting transfers between devices, hop(): lax.ppermute(value, 'row', [(i, (i + step) % devs) for i in range(devs)])  6.11 us
    pallas_call x1, Pallas kernels, final_stage(): pl.pallas_call(final_kernel, grid=(total // block,), in_specs=[pl.BlockSp...  5.17 us
    ppermute x2, waiting for transfers between devices, flip(): return lax.ppermute(value, 'row', [(i, i ^ bit) for i in range(devs)])  5.14 us
    all_to_all x1, starting transfers between devices, body(): tri = lax.all_to_all(tri, 'row', split_axis=0, concat_axis=0, tiled=True)  5.12 us
    ppermute x3, waiting for transfers between devices, hop(): lax.ppermute(value, 'row', [(i, (i + step) % devs) for i in range(devs)])  4.03 us
  transfers between devices with their start and end apart: 6, of which 4 were waited for; matrix products, arithmetic and copies ran while one was open for 5% of the time, Pallas kernels for 2%

profile of v1, /device:TPU:0, one launch (start us, length us, event | category | flops | bytes accessed | tf_op | source)
XLA Modules:
  0.0 140.2 jit_solution(18221026622192857457)
XLA Ops:
  0.0 1.3 convert_reduce_fusion
  1.3 1.4 %fusion.5 = f32[64,16]{1,0:T(8,128)S(1)} fusion(bf16[64,16,256]{2,1,0:T(8,128)(2,1)} %param.10, f32[64,16]{1,0:T(8,128)S(1)} %broadcast_multiply_fusion), kind=kLoop, calls=%fused_computation.12 | loop fusion | flops 1047552 | bytes 532480 | tf_op jit(solution)/shard_map/reduce_sum | solution.py:28
  4.6 5.1 %collective-permute-start.2 = (bf16[17,16,128]{2,1,0:T(8,128)(2,1)S(1)}, bf16[17,16,128]{2,1,0:T(8,128)(2,1)S(1)}, u32[]{:S(2)}, u32[]{:S(2)}) collective-permute-start(bf16[17,16,128]{2,1,0:T(8,128)(2,1)S(1)} %get-tuple-element.20), channel_id=1, source_target_pairs={{0,12},{1,13},{2,14},{3,15},{4,0},{5,1},{6,2},{7,3},{8,4},{9,5},{1... | collective-permute-start | bytes 208904 | tf_op jit(solution)/shard_map/ppermute | solution.py:230
  9.7 1.0 collective-permute-start
  11.6 0.8 fusion.11.left_ref
  12.4 4.0 %collective-permute-done.1 = bf16[17,16,128]{2,1,0:T(8,128)(2,1)S(1)} collective-permute-done((bf16[17,16,128]{2,1,0:T(8,128)(2,1)S(1)}, bf16[17,16,128]{2,1,0:T(8,128)(2,1)S(1)}, u32[]{:S(2)}, u32[]{:S(2)}) %collective-permute-start.1) | collective-permute-done | bytes 69664 | tf_op jit(solution)/shard_map/ppermute | solution.py:230
  16.5 1.6 %collective-permute-start.3 = (bf16[4,17,16,128]{3,2,1,0:T(8,128)(2,1)S(1)}, bf16[4,17,16,128]{3,2,1,0:T(8,128)(2,1)S(1)}, u32[]{:S(2)}, u32[]{:S(2)}) collective-permute-start(bf16[4,17,16,128]{3,2,1,0:T(8,128)(2,1)S(1)} %get-tuple-element.18), channel_id=1, source_target_pairs={{0,2},{1,3},{2,0},{3,1},{4,6},{5,7},{6,4},{7,5},{8,10},{9,11},{10,... | collective-permute-start | bytes 835592 | tf_op jit(solution)/shard_map/ppermute | solution.py:233
  18.2 0.9 copy.36.w_out_ref
  19.1 0.8 copy.35
  19.9 1.2 sort.17
  21.2 3.9 %collective-permute-done.3 = bf16[4,17,16,128]{3,2,1,0:T(8,128)(2,1)S(1)} collective-permute-done((bf16[4,17,16,128]{3,2,1,0:T(8,128)(2,1)S(1)}, bf16[4,17,16,128]{3,2,1,0:T(8,128)(2,1)S(1)}, u32[]{:S(2)}, u32[]{:S(2)}) %collective-permute-start.3) | collective-permute-done | bytes 278560 | tf_op jit(solution)/shard_map/ppermute | solution.py:233
  25.9 1.2 collective-permute-done.4
  27.5 0.8 gather_fusion
  28.3 1.2 broadcast_select_fusion.right_ref
  29.4 14.6 %pair_stage.1 = (f32[16,128,256]{2,1,0:T(8,128)}, bf16[16,128,256]{2,1,0:T(8,128)(2,1)}, bf16[128,16,256]{2,1,0:T(8,128)(2,1)}, bf16[128,16,256]{2,1,0:T(8,128)(2,1)}) custom-call(bf16[1024,128]{1,0:T(8,128)(2,1)} %fusion.11.left_ref, bf16[16,17,16,128]{3,2,1,0:T(8,128)(2,1)} %broadcast_select_fusion.right_ref, bf16[16,128]{1,0:T(8,128)(2,1)} %get-tuple-element.24.mask_ref, ...), custom_call_target="tpu_custom_call" | custom-call | flops 2147483648 | bytes 8388608 | tf_op jit(solution)/shard_map/pair_stage/pallas_call | solution.py:87
  44.0 29.3 %all_to_all.15.a_ref = bf16[16,8,16,256]{3,2,1,0:T(8,128)(2,1)} all-to-all(bf16[16,8,16,256]{3,2,1,0:T(8,128)(2,1)} %bitcast.46), channel_id=1, replica_groups=mesh['groups'=2,'row'=16] {'row'}, dimensions={0} | all-to-all | bytes 2097152 | tf_op jit(solution)/shard_map/all_to_all | solution.py:295
  73.3 29.7 %all_to_all.16.b_ref = bf16[16,8,16,256]{3,2,1,0:T(8,128)(2,1)} all-to-all(bf16[16,8,16,256]{3,2,1,0:T(8,128)(2,1)S(1)} %bitcast.45), channel_id=1, replica_groups=mesh['groups'=2,'row'=16] {'row'}, dimensions={0} | all-to-all | bytes 2097152 | tf_op jit(solution)/shard_map/all_to_all | solution.py:295
  103.0 3.0 %tri_stage.1 = bf16[16,8,16,256]{3,2,1,0:T(8,128)(2,1)} custom-call(bf16[16,8,16,256]{3,2,1,0:T(8,128)(2,1)} %all_to_all.15.a_ref, bf16[16,8,16,256]{3,2,1,0:T(8,128)(2,1)} %all_to_all.16.b_ref), custom_call_target="tpu_custom_call" | custom-call | flops 268435456 | bytes 3145728 | tf_op jit(solution)/shard_map/tri_stage/pallas_call | solution.py:167
  106.0 5.1 %all-to-all-start.2 = ((bf16[16,8,16,256]{3,2,1,0:T(8,128)(2,1)}), bf16[16,8,16,256]{3,2,1,0:T(8,128)(2,1)S(1)}, u32[]{:S(2)}, u32[]{:S(2)}) async-start(bf16[16,8,16,256]{3,2,1,0:T(8,128)(2,1)} %tri_stage.1), calls=%async_computation.2 | async-start | bytes 2097152 | tf_op jit(solution)/shard_map/all_to_all | solution.py:299
  111.1 0.7 copy.37
  112.6 3.0 %gate_stage.1.gate_ref = f32[16,128,256]{2,1,0:T(8,128)} custom-call(bf16[16,128,256]{2,1,0:T(8,128)(2,1)} %get-tuple-element.14.norm_ref, bf16[128,128]{1,0:T(8,128)(2,1)} %bitcast.54), custom_call_target="tpu_custom_call" | custom-call | flops 134217728 | bytes 3145728 | tf_op jit(solution)/shard_map/gate_stage/pallas_call | solution.py:135
  115.5 18.5 %all-to-all-done.2 = bf16[16,8,16,256]{3,2,1,0:T(8,128)(2,1)S(1)} async-done(((bf16[16,8,16,256]{3,2,1,0:T(8,128)(2,1)}), bf16[16,8,16,256]{3,2,1,0:T(8,128)(2,1)S(1)}, u32[]{:S(2)}, u32[]{:S(2)}) %all-to-all-start.2) | async-done | bytes 1048608 | tf_op jit(solution)/shard_map/all_to_all | solution.py:299
  134.0 1.0 copy-done.1
  135.0 5.2 %final_stage.1 = bf16[16,256,128]{2,1,0:T(8,128)(2,1)} custom-call(bf16[128,16,256]{2,1,0:T(8,128)(2,1)} %bitcast.44, f32[16,128,256]{2,1,0:T(8,128)} %get-tuple-element.13.pair_ref, f32[16,128,256]{2,1,0:T(8,128)} %gate_stage.1.gate_ref, bf16[128,128]{1,0:T(8,128)(2,1)} %bitcast.53), custom_call_target="tpu_custom_call" | custom-call | flops 134217728 | bytes 6291456 | tf_op jit(solution)/shard_map/final_stage/pallas_call | solution.py:202
  (52 shorter events, 4.7 us)
Async XLA Ops:
  0.0 3.5 %copy-start = (bf16[256,32]{0,1:T(8,128)(2,1)S(1)}, bf16[256,32]{0,1:T(8,128)(2,1)}, u32[]{:S(2)}) copy-start(bf16[256,32]{0,1:T(8,128)(2,1)} %param.15) | copy-start | bytes 49156
  0.0 3.5 %copy-start.2 = (bf16[64,16,256]{2,1,0:T(8,128)(2,1)S(1)}, bf16[64,16,256]{2,1,0:T(8,128)(2,1)}, u32[]{:S(2)}) copy-start(bf16[64,16,256]{2,1,0:T(8,128)(2,1)} %param.10) | copy-start | bytes 1572868
  0.0 2.8 %copy-start.8 = (s32[64,16]{0,1:T(8,128)S(1)}, s32[64,16]{0,1:T(8,128)}, u32[]{:S(2)}) copy-start(s32[64,16]{0,1:T(8,128)} %param.11) | copy-start | bytes 12292
  3.5 7.3 %copy-start.10 = (bf16[256,32]{0,1:T(8,128)(2,1)S(1)}, bf16[256,32]{0,1:T(8,128)(2,1)}, u32[]{:S(2)}) copy-start(bf16[256,32]{0,1:T(8,128)(2,1)} %param.14) | copy-start | bytes 49156
  4.6 7.9 %collective-permute-start.2 = (bf16[17,16,128]{2,1,0:T(8,128)(2,1)S(1)}, bf16[17,16,128]{2,1,0:T(8,128)(2,1)S(1)}, u32[]{:S(2)}, u32[]{:S(2)}) collective-permute-start(bf16[17,16,128]{2,1,0:T(8,128)(2,1)S(1)} %get-tuple-element.20), channel_id=1, source_target_pairs={{0,12},{1,13},{2,14},{3,15},{4,0},{5,1},{6,2},{7,3},{8,4},{9,5},{1... | collective-permute-start | bytes 208904 | tf_op jit(solution)/shard_map/ppermute | solution.py:230
  9.7 6.8 %collective-permute-start.1 = (bf16[17,16,128]{2,1,0:T(8,128)(2,1)S(1)}, bf16[17,16,128]{2,1,0:T(8,128)(2,1)S(1)}, u32[]{:S(2)}, u32[]{:S(2)}) collective-permute-start(bf16[17,16,128]{2,1,0:T(8,128)(2,1)S(1)} %get-tuple-element.20), channel_id=1, source_target_pairs={{0,8},{1,9},{2,10},{3,11},{4,12},{5,13},{6,14},{7,15},{8,0},{9,1},... | collective-permute-start | bytes 208904 | tf_op jit(solution)/shard_map/ppermute | solution.py:230
  9.7 6.8 %collective-permute-start = (bf16[17,16,128]{2,1,0:T(8,128)(2,1)S(1)}, bf16[17,16,128]{2,1,0:T(8,128)(2,1)S(1)}, u32[]{:S(2)}, u32[]{:S(2)}) collective-permute-start(bf16[17,16,128]{2,1,0:T(8,128)(2,1)S(1)} %get-tuple-element.20), channel_id=1, source_target_pairs={{0,4},{1,5},{2,6},{3,7},{4,8},{5,9},{6,10},{7,11},{8,12},{9,13},{1... | collective-permute-start | bytes 208904 | tf_op jit(solution)/shard_map/ppermute | solution.py:230
  11.3 6.8 %copy-start.4 = (bf16[1024,128]{1,0:T(8,128)(2,1)S(1)}, bf16[1024,128]{1,0:T(8,128)(2,1)}, u32[]{:S(2)}) copy-start(bf16[1024,128]{1,0:T(8,128)(2,1)} %param.16) | copy-start | bytes 786436
  11.6 7.5 %copy-start.5 = (bf16[128,512]{1,0:T(8,128)(2,1)S(1)}, bf16[128,512]{1,0:T(8,128)(2,1)}, u32[]{:S(2)}) copy-start(bf16[128,512]{1,0:T(8,128)(2,1)} %param.17) | copy-start | bytes 393220
  12.4 7.4 %copy-start.9 = (s32[256]{0:T(256)S(1)}, s32[256]{0:T(256)}, u32[]{:S(2)}) copy-start(s32[256]{0:T(256)} %param.13) | copy-start | bytes 3076
  16.5 8.6 %collective-permute-start.3 = (bf16[4,17,16,128]{3,2,1,0:T(8,128)(2,1)S(1)}, bf16[4,17,16,128]{3,2,1,0:T(8,128)(2,1)S(1)}, u32[]{:S(2)}, u32[]{:S(2)}) collective-permute-start(bf16[4,17,16,128]{3,2,1,0:T(8,128)(2,1)S(1)} %get-tuple-element.18), channel_id=1, source_target_pairs={{0,2},{1,3},{2,0},{3,1},{4,6},{5,7},{6,4},{7,5},{8,10},{9,11},{10,... | collective-permute-start | bytes 835592 | tf_op jit(solution)/shard_map/ppermute | solution.py:233
  25.2 2.0 %collective-permute-start.4 = (bf16[4,2,17,16,128]{4,3,2,0,1:T(8,128)(2,1)S(1)}, bf16[4,2,17,16,128]{4,3,2,0,1:T(8,128)(2,1)S(1)}, u32[]{:S(2)}, u32[]{:S(2)}) collective-permute-start(bf16[4,2,17,16,128]{4,3,2,0,1:T(8,128)(2,1)S(1)} %get-tuple-element.16), channel_id=1, source_target_pairs={{0,1},{1,0},{2,3},{3,2},{4,5},{5,4},{6,7},{7,6},{8,9},{9,8},{10,11... | collective-permute-start | bytes 1671176 | tf_op jit(solution)/shard_map/ppermute | solution.py:233
  44.0 29.3 %copy-start.3 = (bf16[128,16,256]{2,1,0:T(8,128)(2,1)S(1)}, bf16[128,16,256]{2,1,0:T(8,128)(2,1)}, u32[]{:S(2)}) copy-start(bf16[128,16,256]{2,1,0:T(8,128)(2,1)} %get-tuple-element.12) | copy-start | bytes 3145732
  106.0 5.1 %copy-start.6 = (bf16[128,128]{1,0:T(8,128)(2,1)S(1)}, bf16[128,128]{1,0:T(8,128)(2,1)}, u32[]{:S(2)}) copy-start(bf16[128,128]{1,0:T(8,128)(2,1)} %param.18) | copy-start | bytes 98308
  106.0 5.9 %copy-start.7 = (bf16[128,128]{1,0:T(8,128)(2,1)S(1)}, bf16[128,128]{1,0:T(8,128)(2,1)}, u32[]{:S(2)}) copy-start(bf16[128,128]{1,0:T(8,128)(2,1)} %param.19) | copy-start | bytes 98308
  106.0 28.1 %all-to-all-start.2 = ((bf16[16,8,16,256]{3,2,1,0:T(8,128)(2,1)}), bf16[16,8,16,256]{3,2,1,0:T(8,128)(2,1)S(1)}, u32[]{:S(2)}, u32[]{:S(2)}) async-start(bf16[16,8,16,256]{3,2,1,0:T(8,128)(2,1)} %tri_stage.1), calls=%async_computation.2 | async-start | bytes 2097152 | tf_op jit(solution)/shard_map/all_to_all | solution.py:299
  134.0 1.0 copy-start.1

commit v2 on v0

v2 whole, which is shorter than its diff:
```python
import jax
import jax.numpy as jnp
from jax import lax
from jax.experimental import pallas as pl
from jax.experimental.pallas import tpu as pltpu
from jax.sharding import PartitionSpec as P

F32 = jnp.float32
BF16 = jnp.bfloat16
LANES = 128
BLOCK = 2 * LANES
PAD = 8
NT = (((1,), (1,)), ((), ()))
MIB = 1024 * 1024


def sigmoid(value):
    return 0.5 * jnp.tanh(0.5 * value) + 0.5


def standardize(value, axis):
    mean = jnp.mean(value, axis=axis, keepdims=True)
    centred = value - mean
    var = jnp.mean(centred * centred, axis=axis, keepdims=True)
    return centred * lax.rsqrt(var + 1e-05)


def local_call(name, kernel, steps, ins, outs, scratch, limit, flops=0, data=0, special=0):
    whole = steps == 1
    in_specs, out_specs, out_shape = [], [], []
    for value, block, index in ins:
        if block is None:
            in_specs.append(pl.BlockSpec(memory_space=pltpu.SMEM))
        elif whole:
            in_specs.append(pl.BlockSpec(memory_space=pltpu.VMEM))
        else:
            in_specs.append(pl.BlockSpec(block, index))
    for shape, dtype, block, index in outs:
        if whole:
            out_specs.append(pl.BlockSpec(memory_space=pltpu.VMEM))
        else:
            out_specs.append(pl.BlockSpec(block, index))
        keep = whole and name != "final_stage"
        out_shape.append(
            pltpu.VMEM(shape, dtype) if keep else jax.ShapeDtypeStruct(shape, dtype)
        )
    return pl.pallas_call(
        kernel,
        grid=() if whole else (steps,),
        in_specs=in_specs,
        out_specs=out_specs,
        out_shape=out_shape,
        scratch_shapes=scratch,
        compiler_params=pltpu.CompilerParams(
            vmem_limit_bytes=(limit if whole else 56) * MIB
        ),
        cost_estimate=pl.CostEstimate(
            flops=flops // 1000, bytes_accessed=data // 1000, transcendentals=special // 1000
        ),
        name=name,
    )(*[value for value, _, _ in ins])


def fixed(value):
    return value, value.shape, lambda j: (0,) * value.ndim


def last(value, block):
    return value, value.shape[:-1] + (block,), lambda j: (0,) * (value.ndim - 1) + (j,)


def last_out(shape, dtype, block):
    return shape, dtype, shape[:-1] + (block,), lambda j: (0,) * (len(shape) - 1) + (j,)


def identity(size, order=lambda row: row):
    row = lax.broadcasted_iota(jnp.int32, (size, size), 0)
    column = lax.broadcasted_iota(jnp.int32, (size, size), 1)
    return (order(row) == column).astype(BF16)


def msa_kernel(msa_ref, cover_ref, left_w_ref, right_w_ref, right_ref, left_ref, values, rights, lefts):
    seqs, rows, breadth = msa_ref.shape
    proj = left_w_ref.shape[0]
    pairs = proj // 2
    tiles = breadth // LANES
    msa = msa_ref[...].astype(F32).reshape(seqs * rows, breadth)
    for tile in range(tiles):
        values[tile] = msa[:, tile * LANES : (tile + 1) * LANES]
    cover = cover_ref[...].astype(F32)
    swap = identity(proj, lambda row: 2 * (row % pairs) + row // pairs)
    right_w = jnp.dot(swap, right_w_ref[...], preferred_element_type=F32).astype(BF16)
    weights = jnp.concatenate([left_w_ref[...], right_w])
    for i in range(rows):
        row = jnp.concatenate(
            [values[tile, pl.ds(i, seqs, stride=rows), :] for tile in range(tiles)], axis=1
        )
        norm = standardize(row, -1).astype(BF16)
        factor = lax.dot_general(weights, norm, NT, preferred_element_type=F32)
        factor = factor * cover[i : i + 1]
        lefts[i] = factor[:proj]
        rights[i * pairs : (i + 1) * pairs] = jnp.concatenate(
            [factor[proj : proj + pairs], factor[proj + pairs :]], axis=1
        )
    half = rows // 2
    for i in range(half):
        left_ref[i * proj : (i + 1) * proj] = jnp.concatenate(
            [lefts[i], lefts[i + half]], axis=1
        ).astype(BF16)
    for t in range(pairs):
        right_ref[t] = rights[pl.ds(t, rows, stride=pairs), :].astype(BF16)
    right_ref[pairs] = jnp.concatenate([cover, jnp.zeros_like(cover)], axis=1).astype(BF16)


def msa_stage(msa, cover, left_w, right_w):
    seqs, rows, breadth = msa.shape
    proj = left_w.shape[0]
    right = (proj // 2 + 1, rows, 2 * seqs)
    left = (rows * proj // 2, 2 * seqs)
    return local_call(
        "msa_stage",
        msa_kernel,
        1,
        [fixed(msa), fixed(cover), fixed(left_w), fixed(right_w)],
        [(right, BF16, None, None), (left, BF16, None, None)],
        [
            pltpu.VMEM((breadth // LANES, seqs * rows, LANES), F32),
            pltpu.VMEM((rows * proj // 2, 2 * seqs), F32),
            pltpu.VMEM((rows, proj, seqs), F32),
        ],
        12,
        flops=4 * seqs * rows * breadth * proj,
        data=2 * seqs * rows * breadth,
    )


def weights_kernel(out_ref, in_ref, gate_ref, final_ref, out_t, in_t, gate_t, final_t, rows):
    one = identity(LANES)

    def turned(value):
        return lax.dot_general(one, value, NT, preferred_element_type=F32).astype(BF16)

    depth, width = out_ref.shape
    proj = int(depth**0.5)
    rows[...] = out_ref[...].astype(F32)
    ordered = jnp.concatenate([rows[pl.ds(q, proj, stride=proj), :] for q in range(proj)])
    out_t[...] = turned(ordered.astype(BF16))
    for k in range(in_ref.shape[1] // LANES):
        cols = slice(k * LANES, (k + 1) * LANES)
        in_t[cols] = turned(in_ref[:, cols])
    gate_t[...] = turned(gate_ref[...])
    final_t[...] = turned(final_ref[...])


def weights_stage(w_out, w_in, w_gate, w_final):
    depth, width = w_out.shape
    shapes = [w_out.shape[::-1], w_in.shape[::-1], w_gate.shape[::-1], w_final.shape[::-1]]
    return local_call(
        "weights_stage",
        weights_kernel,
        1,
        [fixed(w_out), fixed(w_in), fixed(w_gate), fixed(w_final)],
        [(shape, BF16, None, None) for shape in shapes],
        [pltpu.VMEM((depth, width), F32)],
        8,
        flops=2 * LANES * LANES * LANES * 6,
        data=4 * depth * width,
    )


def order_right(right_refs, right):
    me = lax.axis_index("row")
    for index, ref in enumerate(right_refs):
        core, y = index // 2, index % 2
        for z in range(4):
            right[((me // 4 - z) & 3) * 4 + ((me & 3) ^ (2 * y + core))] = ref[z]


def make_updates(left_ref, mask, right, outer, count):
    slices = right.shape[1]
    rows, depth, block = outer.shape
    proj = depth // (2 * (slices - 1))
    count[...] = lax.dot_general(
        mask, right[:, slices - 1].reshape(block, LANES), NT, preferred_element_type=F32
    )
    left = left_ref[...].astype(F32)
    turned = pltpu.roll(left, LANES // 2, 1)
    low = lax.broadcasted_iota(jnp.int32, left.shape, 1) < LANES // 2
    both_left = jnp.concatenate(
        [
            jnp.where(low, left, 0.0),
            jnp.where(low, turned, 0.0),
            jnp.where(low, 0.0, turned),
            jnp.where(low, 0.0, left),
        ]
    ).astype(BF16)
    half = rows * proj

    @pl.loop(0, slices - 1, unroll=4)
    def _(t):
        both = lax.dot_general(
            both_left,
            right[:, pl.ds(t, 1)].reshape(block, LANES),
            NT,
            preferred_element_type=F32,
        ).astype(BF16)
        for e in range(2):
            outer[:, pl.ds(pl.multiple_of((2 * t + e) * proj, proj), proj), :] = both[
                e * half : (e + 1) * half
            ].reshape(rows, proj, block)


def row_update(i, w_out_ref, outer, count):
    update = jnp.dot(w_out_ref[...], outer[i], preferred_element_type=F32)
    return update / jnp.maximum(count[i : i + 1], 1.0)


def chip_here(split):
    return jnp.int32(0) if split == 1 else (lax.axis_index("row") // 2) & (split - 1)


def observed(device, obs_ref, seen_ref, rows, i):
    return seen_ref[...].astype(F32) * obs_ref[device * rows + i].astype(F32)


def keep_sides(i, norm, w_in_ref, seen, sides_of, hidden):
    sides = jnp.dot(w_in_ref[...], norm, preferred_element_type=F32)
    stride = hidden + PAD
    for side, kept in enumerate(sides_of):
        gates = sides[2 * side * hidden : (2 * side + 1) * hidden]
        values = sides[(2 * side + 1) * hidden : (2 * side + 2) * hidden]
        value = sigmoid(gates) * values * seen
        for tile in range(kept.shape[0]):
            kept[tile, i * stride : i * stride + hidden] = value[
                :, tile * LANES : (tile + 1) * LANES
            ]


def write_sides(kept, outs, rows, hidden):
    per, chans = outs[0].shape[:2]
    chip = chip_here(len(outs))
    for part in range(per * len(outs)):
        target = outs[part // per].at[part % per]
        start = (chip ^ part) * chans

        @pl.loop(0, chans, unroll=8 if chans % 8 == 0 else chans)
        def _(c):
            for tile in range(kept.shape[0]):
                target[c, :, tile * LANES : (tile + 1) * LANES] = kept[
                    tile, pl.ds(start + c, rows, stride=hidden + PAD), :
                ].astype(BF16)


def pair_kernel(pieces, split, *refs):
    left_ref, mask_ref, couple_ref, w_out_ref, w_in_ref, w_gate_ref, obs_ref, seen_ref = refs[:8]
    right_refs, refs = refs[8 : 8 + pieces], refs[8 + pieces :]
    pair_ref, gate_ref = refs[:2]
    a_refs, b_refs, refs = refs[2 : 2 + split], refs[2 + split : 2 + 2 * split], refs[2 + 2 * split :]
    if pieces > 1:
        right, refs = refs[0], refs[1:]
        order_right(right_refs, right)
    else:
        right = right_refs[0]
    outer, kept_a, kept_b, count = refs
    rows = couple_ref.shape[0]
    hidden = w_in_ref.shape[0] // 4
    make_updates(left_ref, mask_ref[...], right, outer, count)
    for i in range(rows):
        pair = couple_ref[i].astype(F32).T + row_update(i, w_out_ref, outer, count)
        norm = standardize(pair, 0).astype(BF16)
        pair_ref[i] = pair
        gate_ref[i] = sigmoid(jnp.dot(w_gate_ref[...], norm, preferred_element_type=F32))
        seen = observed(lax.axis_index("row"), obs_ref, seen_ref, rows, i)
        keep_sides(i, norm, w_in_ref, seen, (kept_a, kept_b), hidden)
    write_sides(kept_b, b_refs, rows, hidden)
    write_sides(kept_a, a_refs, rows, hidden)


def update_kernel(left_ref, w_out_ref, right, *refs):
    mask_refs, (update_ref, outer, count) = refs[:-3], refs[-3:]
    if mask_refs:
        mask = mask_refs[0][...]
    else:
        mask = right[lax.axis_index("row") ^ 12, right.shape[1] - 1]
    make_updates(left_ref, mask, right, outer, count)
    for i in range(update_ref.shape[0]):
        update_ref[i] = row_update(i, w_out_ref, outer, count)


def mirror_kernel(low, mirror, update_ref, couple_ref, w_in_ref, obs_ref, seen_ref, *refs):
    outs, kept = refs[:-1], refs[-1]
    rows, block = update_ref.shape[0], couple_ref.shape[1]
    hidden = w_in_ref.shape[0] // 4
    cols = slice(low, low + block)
    for i in range(rows):
        pair = couple_ref[i].astype(F32).T + update_ref[i, :, cols]
        device = mirror(lax.axis_index("row"))
        seen = observed(device, obs_ref, seen_ref, rows, i)[:, cols]
        norm = standardize(pair, 0).astype(BF16)
        keep_sides(i, norm, w_in_ref.at[2 * hidden :], seen, (kept,), hidden)
    write_sides(kept, outs, rows, hidden)


def right_input(value, total):
    return value, (value.shape[0] * BLOCK // total,) + value.shape[1:], lambda j: (j, 0, 0, 0)


def couple_input(couple):
    return couple, (couple.shape[0], BLOCK, couple.shape[2]), lambda j: (0, j, 0)


def kept_scratch(rows, hidden, block):
    return pltpu.VMEM((block // LANES, rows * (hidden + PAD), LANES), F32)


def scalars(value):
    return value, None, None


def pair_stage(left, right, mask, couple, w_out, w_in, w_gate, obs, parts, split):
    rows, total, width = couple.shape
    hidden = w_in.shape[0] // 4
    piece = (parts // split, hidden // parts, rows, total)
    outs = [last_out((rows, width, total), F32, BLOCK)] * 2
    outs += [last_out(piece, BF16, BLOCK)] * (2 * split)
    if len(right) > 1:
        outs += [((total // rows,) + right[0].shape[1:], BF16, None, None)]
    return local_call(
        "pair_stage",
        lambda *refs: pair_kernel(len(right), split, *refs),
        total // BLOCK,
        [fixed(left), fixed(mask), couple_input(couple), fixed(w_out), fixed(w_in)]
        + [fixed(w_gate), scalars(obs), last(obs[None], BLOCK)]
        + [right_input(value, total) for value in right],
        outs,
        [pltpu.VMEM((rows, w_out.shape[1], BLOCK), BF16)]
        + [kept_scratch(rows, hidden, BLOCK)] * 2
        + [pltpu.VMEM((rows, BLOCK), F32)],
        24,
        flops=4 * rows * total * w_out.shape[1] * width,
        data=16 * rows * total * width,
        special=3 * rows * total * hidden,
    )


def update_stage(left, right, mask, w_out, rows, total):
    width = w_out.shape[0]
    return local_call(
        "update_stage",
        update_kernel,
        total // BLOCK,
        [fixed(left), fixed(w_out), right_input(right, total)]
        + ([] if mask is None else [fixed(mask)]),
        [last_out((rows, width, total), F32, BLOCK)],
        [pltpu.VMEM((rows, w_out.shape[1], BLOCK), BF16), pltpu.VMEM((rows, BLOCK), F32)],
        20,
        flops=4 * rows * total * w_out.shape[1] * width,
        data=8 * rows * total * width,
    )[0]


def mirror_stage(low, mirror, update, couple, w_in, obs, parts, split):
    rows, width = update.shape[:2]
    total = couple.shape[1]
    hidden = w_in.shape[0] // 4
    block = min(BLOCK, total)
    return local_call(
        "mirror_stage",
        lambda *refs: mirror_kernel(low, mirror, *refs),
        total // block,
        [last(update, block), couple_input(couple), fixed(w_in), scalars(obs)]
        + [last(obs[None], block)],
        [last_out((parts // split, hidden // parts, rows, total), BF16, block)] * split,
        [kept_scratch(rows, hidden, block)],
        16,
        flops=4 * rows * total * hidden * width,
        data=8 * rows * total * width,
        special=rows * total * hidden,
    )


def tri_kernel(cores, split, cuts, flip, *refs):
    a_refs, refs = refs[:split], refs[split:]
    b_refs = [refs[cut * cores * split : (cut + 1) * cores * split] for cut in range(cuts)]
    outs, whole = refs[cuts * cores * split : -1], refs[-1]
    per, chans, rows, total = a_refs[0].shape
    depth = total // cuts
    chip = chip_here(split)
    core = lax.axis_index("row") & 1
    for c in range(chans):
        for cut in range(cuts):
            for index, ref in enumerate(b_refs[cut]):
                for slot in range(per):
                    part = (index % split) * per + slot
                    place = (chip ^ part ^ flip) * cores
                    if cores == 2:
                        place = place + (core ^ (index // split))
                    place = pl.multiple_of(place * rows, rows)
                    whole[c, pl.ds(place, rows), cut * depth : (cut + 1) * depth] = ref[slot, c]
        side_a = jnp.concatenate([ref[slot, c] for ref in a_refs for slot in range(per)])
        product = lax.dot_general(side_a, whole[c], NT, preferred_element_type=F32).astype(BF16)
        for part in range(per * split):
            outs[part // per][part % per, c] = product[part * rows : (part + 1) * rows]


def channels(value, step):
    return value, value.shape[:1] + (step,) + value.shape[2:], lambda c: (0, c, 0, 0)


def tri_stage(a, b, cores, flip):
    split = len(a)
    per, chans, rows, total = a[0].shape
    step = max(1, min(chans, chans * BLOCK // total))
    half = per * split * cores * rows
    shape = (per, chans, rows, half)
    return local_call(
        "tri_stage",
        lambda *refs: tri_kernel(cores, split, len(b), flip, *refs),
        chans // step,
        [channels(value, step) for value in a]
        + [channels(value, step) for cut in b for value in cut],
        [(shape, BF16, (per, step, rows, half), lambda c: (0, c, 0, 0))] * split,
        [pltpu.VMEM((step, half, total), BF16)],
        16,
        flops=2 * chans * per * split * rows * half * total,
        data=6 * chans * half * total,
    )


def final_kernel(spans, split, pair_ref, gate_ref, w_ref, *refs):
    out_ref, normed = refs[-2:]
    rows, _, whole = pair_ref.shape
    per, chans, _, block = refs[0].shape
    parts = per * split
    hidden = chans * parts
    tiles = block // LANES
    chip = chip_here(split)
    for span in range(spans):
        tri = refs[span * split : (span + 1) * split]
        if spans == 1:
            low = 0
        else:
            devs = lax.axis_size("row")
            mine = lax.div(lax.axis_index("row"), devs // 2)
            low = pl.multiple_of((mine ^ span) * block, block)
        values = standardize(
            jnp.concatenate([ref[slot] for ref in tri for slot in range(per)]).astype(F32), 0
        )
        for part in range(parts):
            first = pl.multiple_of((chip ^ part) * (chans * rows), chans * rows)
            for tile in range(tiles):
                normed[tile, pl.ds(first, chans * rows), :] = values[
                    part * chans : (part + 1) * chans, :, tile * LANES : (tile + 1) * LANES
                ].reshape(chans * rows, LANES)
        for i in range(rows):
            columns = jnp.concatenate(
                [normed[tile, pl.ds(i, hidden, stride=rows), :] for tile in range(tiles)], axis=1
            ).astype(BF16)
            update = jnp.dot(w_ref[...], columns, preferred_element_type=F32)
            cols = pl.ds(low, block)
            result = pair_ref[i, :, cols] + gate_ref[i, :, cols] * update
            out_ref[i, cols, :] = result.T.astype(BF16)


def final_stage(spans, pair, gate, weight):
    rows, width, total = pair.shape
    hidden = weight.shape[1]
    split = len(spans[0])
    block = spans[0][0].shape[-1] if len(spans) > 1 else BLOCK
    return local_call(
        "final_stage",
        lambda *refs: final_kernel(len(spans), split, *refs),
        total // BLOCK,
        [last(pair, BLOCK), last(gate, BLOCK), fixed(weight)]
        + [last(value, block) for span in spans for value in span],
        [((rows, total, width), BF16, (rows, BLOCK, width), lambda j: (0, j, 0))],
        [pltpu.VMEM((block // LANES, hidden * rows, LANES), F32)],
        24,
        flops=2 * rows * total * hidden * width,
        data=12 * rows * total * width,
    )[0]


def send(value, move):
    devs = lax.axis_size("row")
    return lax.ppermute(value, "row", [(i, move(i)) for i in range(devs)])


def after(first, value):
    return lax.optimization_barrier((first, value))


def exchange(pieces, earlier=None):
    devs = lax.axis_size("row")
    half = devs // 2
    if len(pieces) == 1:
        groups = [list(range(half)), list(range(half, devs))]
        return [
            lax.all_to_all(
                pieces[0], "row", split_axis=0, concat_axis=0, tiled=True, axis_index_groups=groups
            )
        ]
    out = list(pieces)
    for r in range(1, len(out)):
        if earlier is not None:
            _, out[r] = after(earlier[r], out[r])
        out[r] = send(out[r], lambda i, r=r: i ^ (2 * r))
    return out


def with_other_core(pieces):
    if len(pieces) == 1:
        return pieces
    return list(pieces) + [send(value, lambda i: i ^ 1) for value in pieces]


def body(
    homolog_features,
    coverage_indicator,
    couple_features,
    observed_indicator,
    first_factor_matrix,
    second_factor_matrix,
    product_final_matrix,
    edge_projection_matrix,
    sigmoid_filter_matrix,
    multiplicative_final_matrix,
):
    rows, total, width = couple_features.shape
    devs = lax.axis_size("row")
    half = devs // 2
    me = lax.axis_index("row")
    hops = devs == 16
    cores, cuts = (2, 2) if hops else (1, 1)
    parts = half // cores
    split = parts if hops else 1
    obs = observed_indicator

    def mirror(device):
        return device ^ 12 if hops else (device + half) % devs

    def mirrored(value):
        return send(value, mirror)

    block, left = msa_stage(
        homolog_features,
        coverage_indicator.T,
        first_factor_matrix.T,
        second_factor_matrix.T,
    )
    couples = [
        couple_features[:, cut * total // cuts : (cut + 1) * total // cuts] for cut in range(cuts)
    ]
    if hops:
        couples[0] = jnp.concatenate([couples[0], left.reshape(-1, total // cuts, width)])
    weights = weights_stage(
        product_final_matrix,
        edge_projection_matrix,
        sigmoid_filter_matrix,
        multiplicative_final_matrix,
    )
    if hops:
        held = [block] + [send(block, lambda i, d=d: (i + 4 * d) % devs) for d in (1, 2, 3)]
        held, (*couples, weights) = after(jnp.stack(held), (*couples, weights))
        other = send(held, lambda i: i ^ 2)
        right = [held, other, send(held, lambda i: i ^ 1), send(other, lambda i: i ^ 1)]
        far_mask = None
    else:
        right = [lax.all_gather(block, "row", axis=0)]
        far_left = mirrored(left)
        far_mask = right[0][mirror(me), -1]
    far_couples = [mirrored(value) for value in couples]
    if hops:
        far_left = far_couples[0][rows:].reshape(left.shape)
    w_out, w_in, w_gate, w_final = weights

    pair, gate, *sides = pair_stage(
        left, right, block[-1], couple_features, w_out, w_in, w_gate, obs, parts, split
    )
    a, b = sides[:split], sides[split : 2 * split]
    ordered = sides[2 * split] if hops else right[0]
    b = exchange(b)
    update = update_stage(far_left, ordered, far_mask, w_out, rows, total)
    if hops:
        update, b = after(update, b)
    a = exchange(a, b)
    b = with_other_core(b)
    near = exchange(tri_stage(a, [b], cores, 0))
    far_b = []
    for cut, value in enumerate(far_couples):
        low = cut * total // cuts
        sides = mirror_stage(low, mirror, update, value, w_in, obs, parts, split)
        far_b.append(with_other_core(exchange(sides, a)))
    far = exchange(tri_stage(a, far_b, cores, 2 if hops else 0))
    if hops:
        spans = [near, far]
    else:
        lower = me < half
        spans = [
            [
                jnp.concatenate(
                    [jnp.where(lower, x, y), jnp.where(lower, y, x)], axis=-1
                )
                for x, y in zip(near, far)
            ]
        ]
    return final_stage(spans, pair, gate, w_final)


def solution(mesh):
    placed = (
        P(None, ("groups", "row"), None),
        P(None, ("groups", "row")),
        P(("groups", "row"), None, None),
        P("groups"),
        P(),
        P(),
        P(),
        P(),
        P(),
        P(),
    )
    return jax.shard_map(
        body,
        mesh=mesh,
        in_specs=placed,
        out_specs=P(("groups", "row"), None, None),
        check_vma=False,
    )
```

time: 219 us -> 111 us (0.51); the launches traced: 216 us -> 110 us
  blocking collectives: 54.9 us -> 0 us
  local copies, waits for them, and re-layouts: 40.8 us -> 4.48 us
  starting transfers between devices: 9.4 us -> 38.1 us
  matrix products: 27.8 us -> 0 us
  Pallas kernels: 0 us -> 24.4 us
  between operations: 13.6 us -> 0.22 us
  waiting for transfers between devices: 56 us -> 43.2 us
  other arithmetic: 12.8 us -> 0.09 us
    ppermute x0 -> x38, waiting for transfers between devices: none -> 43.2 us  [send(): return lax.ppermute(value, 'row', [(i, move(i)) for i in range(devs)])]
    all_to_all x2 -> x0, waiting for transfers between devices: 39.4 us -> none  [the longest x1 21.2 us: body(): lax.all_to_all(tri_cols, 'row', split_axis=2, concat_axis=0, tiled=True)]
    ppermute x0 -> x38, starting transfers between devices: none -> 38.1 us  [send(): return lax.ppermute(value, 'row', [(i, move(i)) for i in range(devs)])]
    all_to_all x1 -> x0, blocking collectives: 31.7 us -> none  [body(): lax.all_to_all(side_b, 'row', split_axis=0, concat_axis=1, tiled=True)]
    dot_general x57 -> x0, matrix products: 27.8 us -> none  [the longest x1 5.76 us: triangle_product(): jnp.einsum('uncik,umcjk->ucnimj', whole_a, whole_b, preferred_element_typ...]
    pallas_call x0 -> x9, Pallas kernels: none -> 24.4 us  [local_call(): pl.pallas_call(kernel, grid=() if whole else (steps,), in_specs=in_specs,...]
    all_gather x1 -> x0, blocking collectives: 23.3 us -> none  [body(): mask_piece = lax.all_gather(mask_send, 'row', axis=0, tiled=True)]
    reshape x3 -> x0, local copies, waits for them, and re-layouts: 22.8 us -> none  [the longest x2 21.8 us: body(): tri_cols.reshape(1, chan_local, n_dev, local_amino_acids, total_res)]
  transfers between devices with their start and end apart: 3 -> 38, of which waited for: 3 -> 17; matrix products, arithmetic and copies ran while one was open for 3% -> 1% of each run, Pallas kernels for 0% -> 18%
where the time goes in v2:
time: 111 us; the launch traced here: 110 us
  waiting for transfers between devices  43.2 us (39%)
  starting transfers between devices  38.1 us (34%)
  Pallas kernels  24.4 us (22%)
  local copies, waits for them, and re-layouts  4.48 us (4%)
    ppermute x38, waiting for transfers between devices, send(): return lax.ppermute(value, 'row', [(i, move(i)) for i in range(devs)])  43.2 us
    ppermute x38, starting transfers between devices, send(): return lax.ppermute(value, 'row', [(i, move(i)) for i in range(devs)])  38.1 us
    pallas_call x9, Pallas kernels, local_call(): pl.pallas_call(kernel, grid=() if whole else (steps,), in_specs=in_specs,...  24.4 us
    unnamed x20, local copies, waits for them, and re-layouts  3.2 us
  transfers between devices with their start and end apart: 38, of which 17 were waited for; matrix products, arithmetic and copies ran while one was open for 1% of the time, Pallas kernels for 18%

profile of v2, /device:TPU:0, one launch (start us, length us, event | category | flops | bytes accessed | tf_op | source)
XLA Modules:
  0.0 110.5 jit_solution(13081907665213144962)
XLA Ops:
  4.4 5.1 %collective-permute-start.2 = (bf16[17,16,128]{2,1,0:T(8,128)(2,1)S(1)}, bf16[17,16,128]{2,1,0:T(8,128)(2,1)S(1)}, u32[]{:S(2)}, u32[]{:S(2)}) collective-permute-start(bf16[17,16,128]{2,1,0:T(8,128)(2,1)S(1)} %get-tuple-element.60), channel_id=1, source_target_pairs={{0,12},{1,13},{2,14},{3,15},{4,0},{5,1},{6,2},{7,3},{8,4},{9,5},{1... | collective-permute-start | bytes 208904 | tf_op jit(solution)/shard_map/ppermute | solution.py:486
  12.5 3.8 %collective-permute-done.1 = bf16[17,16,128]{2,1,0:T(8,128)(2,1)S(1)} collective-permute-done((bf16[17,16,128]{2,1,0:T(8,128)(2,1)S(1)}, bf16[17,16,128]{2,1,0:T(8,128)(2,1)S(1)}, u32[]{:S(2)}, u32[]{:S(2)}) %collective-permute-start.1) | collective-permute-done | bytes 69664 | tf_op jit(solution)/shard_map/ppermute | solution.py:486
  17.9 1.9 %collective-permute-start.6 = (bf16[18,128,128]{2,1,0:T(8,128)(2,1)S(1)}, bf16[18,128,128]{2,1,0:T(8,128)(2,1)S(1)}, u32[]{:S(2)}, u32[]{:S(2)}) collective-permute-start(bf16[18,128,128]{2,1,0:T(8,128)(2,1)S(1)} %pad_maximum_fusion), channel_id=1, source_target_pairs={{0,12},{1,13},{2,14},{3,15},{4,8},{5,9},{6,10},{7,11},{8,4},{9,5},... | collective-permute-start | bytes 1769480 | tf_op jit(solution)/shard_map/ppermute | solution.py:486
  19.8 5.1 %collective-permute-done.3.refs_9_ = bf16[4,17,16,128]{3,2,1,0:T(8,128)(2,1)S(1)} collective-permute-done((bf16[4,17,16,128]{3,2,1,0:T(8,128)(2,1)S(1)}, bf16[4,17,16,128]{3,2,1,0:T(8,128)(2,1)S(1)}, u32[]{:S(2)}, u32[]{:S(2)}) %collective-permute-start.3) | collective-permute-done | bytes 278560 | tf_op jit(solution)/shard_map/ppermute | solution.py:486
  26.5 10.3 %pair_stage.1 = (f32[16,128,256]{2,1,0:T(8,128)S(1)}, f32[16,128,256]{2,1,0:T(8,128)S(1)}, bf16[1,32,16,256]{3,2,1,0:T(8,128)(2,1)S(1)}, bf16[1,32,16,256]{3,2,1...) custom-call(bf16[256,128]{1,0:T(8,128)(2,1)S(1)} %get-tuple-element., ...), custom_call_target="tpu_custom_call" | custom-call | flops 2147483 | bytes 8388 | tf_op jit(solution)/shard_map/pair_stage/pallas_call | solution.py:47
  38.7 1.6 %collective-permute-start.9 = (bf16[1,32,16,256]{3,2,1,0:T(8,128)(2,1)S(1)}, bf16[1,32,16,256]{3,2,1,0:T(8,128)(2,1)S(1)}, u32[]{:S(2)}, u32[]{:S(2)}) collective-permute-start(bf16[1,32,16,256]{3,2,1,0:T(8,128)(2,1)S(1)} %get-tuple-element.78), channel_id=1, source_target_pairs={{0,6},{1,7},{2,4},{3,5},{4,2},{5,3},{6,0},{7,1},{8,14},{9,15},{10,... | collective-permute-start | bytes 786440 | tf_op jit(solution)/shard_map/ppermute | solution.py:486
  40.4 4.6 %update_stage.1.refs_0_ = f32[16,128,256]{2,1,0:T(8,128)S(1)} custom-call(bf16[256,128]{1,0:T(8,128)(2,1)S(1)} %bitcast.12, bf16[128,1024]{1,0:T(8,128)(2,1)S(1)} %get-tuple-element.65.refs_3_.w_out_ref, bf16[16,17,16,128]{3,2,1,0:T(8,128)(2,1)S(1)} %get-tuple-element.74.right), custom_call_target="tpu_custom_call" | custom-call | flops 2147483 | bytes 4194 | tf_op jit(solution)/shard_map/update_stage/pallas_call | solution.py:47
  45.3 6.4 %collective-permute-done.8.refs_6_ = bf16[1,32,16,256]{3,2,1,0:T(8,128)(2,1)S(1)} collective-permute-done((bf16[1,32,16,256]{3,2,1,0:T(8,128)(2,1)S(1)}, bf16[1,32,16,256]{3,2,1,0:T(8,128)(2,1)S(1)}, u32[]{:S(2)}, u32[]{:S(2)}) %collective-permute-start.8) | collective-permute-done | bytes 262176 | tf_op jit(solution)/shard_map/ppermute | solution.py:486
  51.7 5.5 %collective-permute-done.9.refs_7_ = bf16[1,32,16,256]{3,2,1,0:T(8,128)(2,1)S(1)} collective-permute-done((bf16[1,32,16,256]{3,2,1,0:T(8,128)(2,1)S(1)}, bf16[1,32,16,256]{3,2,1,0:T(8,128)(2,1)S(1)}, u32[]{:S(2)}, u32[]{:S(2)}) %collective-permute-start.9) | collective-permute-done | bytes 262176 | tf_op jit(solution)/shard_map/ppermute | solution.py:486
  57.1 5.9 %collective-permute-start.12 = (bf16[1,32,16,256]{3,2,1,0:T(8,128)(2,1)S(1)}, bf16[1,32,16,256]{3,2,1,0:T(8,128)(2,1)S(1)}, u32[]{:S(2)}, u32[]{:S(2)}) collective-permute-start(bf16[1,32,16,256]{3,2,1,0:T(8,128)(2,1)S(1)} %get-tuple-element.87), channel_id=1, source_target_pairs={{0,6},{1,7},{2,4},{3,5},{4,2},{5,3},{6,0},{7,1},{8,14},{9,15},{10,... | collective-permute-start | bytes 786440 | tf_op jit(solution)/shard_map/ppermute | solution.py:486
  64.8 1.7 %mirror_stage.3 = (bf16[1,32,16,128]{3,2,1,0:T(8,128)(2,1)S(1)}, bf16[1,32,16,128]{3,2,1,0:T(8,128)(2,1)S(1)}, bf16[1,32,16,128]{3,2,1,0:T(8,128)(2,1)S(1)}, bf16[1,32,16,128]{3,2,1,0:T(8,128)(2,1)S(1)}) custom-call(f32[16,128,256]{2,1,0:T(8,128)S(1)} %update_stage.1.refs_0_, bf16[16,128,128]{2,1,0:T(8,128)(2,1)S(1)} %collective-permute-done.27.refs_1_, ...), custom_call_target="tpu_custom_call" | custom-call | flops 134217 | bytes 2097 | tf_op jit(solution)/shard_map/mirror_stage/pallas_call | solution.py:47
  70.0 2.8 %collective-permute-done.11.refs_2_ = bf16[1,32,16,256]{3,2,1,0:T(8,128)(2,1)S(1)} collective-permute-done((bf16[1,32,16,256]{3,2,1,0:T(8,128)(2,1)S(1)}, bf16[1,32,16,256]{3,2,1,0:T(8,128)(2,1)S(1)}, u32[]{:S(2)}, u32[]{:S(2)}) %collective-permute-start.11) | collective-permute-done | bytes 262176 | tf_op jit(solution)/shard_map/ppermute | solution.py:486
  72.8 2.7 %collective-permute-done.10.refs_1_ = bf16[1,32,16,256]{3,2,1,0:T(8,128)(2,1)S(1)} collective-permute-done((bf16[1,32,16,256]{3,2,1,0:T(8,128)(2,1)S(1)}, bf16[1,32,16,256]{3,2,1,0:T(8,128)(2,1)S(1)}, u32[]{:S(2)}, u32[]{:S(2)}) %collective-permute-start.10) | collective-permute-done | bytes 262176 | tf_op jit(solution)/shard_map/ppermute | solution.py:486
  75.6 2.8 %collective-permute-start.22 = (bf16[1,32,16,128]{3,2,1,0:T(8,128)(2,1)S(1)}, bf16[1,32,16,128]{3,2,1,0:T(8,128)(2,1)S(1)}, u32[]{:S(2)}, u32[]{:S(2)}) collective-permute-start(bf16[1,32,16,128]{3,2,1,0:T(8,128)(2,1)S(1)} %get-tuple-element.100), channel_id=1, source_target_pairs={{0,6},{1,7},{2,4},{3,5},{4,2},{5,3},{6,0},{7,1},{8,14},{9,15},{10,... | collective-permute-start | bytes 393224 | tf_op jit(solution)/shard_map/ppermute | solution.py:486
  78.5 2.9 %collective-permute-start.21 = (bf16[1,32,16,128]{3,2,1,0:T(8,128)(2,1)S(1)}, bf16[1,32,16,128]{3,2,1,0:T(8,128)(2,1)S(1)}, u32[]{:S(2)}, u32[]{:S(2)}) collective-permute-start(bf16[1,32,16,128]{3,2,1,0:T(8,128)(2,1)S(1)} %get-tuple-element.98), channel_id=1, source_target_pairs={{0,4},{1,5},{2,6},{3,7},{4,0},{5,1},{6,2},{7,3},{8,12},{9,13},{10,... | collective-permute-start | bytes 393224 | tf_op jit(solution)/shard_map/ppermute | solution.py:486
  83.9 1.9 %collective-permute-done.30.refs_15_ = bf16[1,32,16,128]{3,2,1,0:T(8,128)(2,1)S(1)} collective-permute-done((bf16[1,32,16,128]{3,2,1,0:T(8,128)(2,1)S(1)}, bf16[1,32,16,128]{3,2,1,0:T(8,128)(2,1)S(1)}, u32[]{:S(2)}, u32[]{:S(2)}) %collective-permute-start.30) | collective-permute-done | bytes 131104 | tf_op jit(solution)/shard_map/ppermute | solution.py:486
  85.8 2.9 %collective-permute-done.21.refs_6_ = bf16[1,32,16,128]{3,2,1,0:T(8,128)(2,1)S(1)} collective-permute-done((bf16[1,32,16,128]{3,2,1,0:T(8,128)(2,1)S(1)}, bf16[1,32,16,128]{3,2,1,0:T(8,128)(2,1)S(1)}, u32[]{:S(2)}, u32[]{:S(2)}) %collective-permute-start.21) | collective-permute-done | bytes 131104 | tf_op jit(solution)/shard_map/ppermute | solution.py:486
  88.7 1.6 %collective-permute-done.29.refs_14_ = bf16[1,32,16,128]{3,2,1,0:T(8,128)(2,1)S(1)} collective-permute-done((bf16[1,32,16,128]{3,2,1,0:T(8,128)(2,1)S(1)}, bf16[1,32,16,128]{3,2,1,0:T(8,128)(2,1)S(1)}, u32[]{:S(2)}, u32[]{:S(2)}) %collective-permute-start.29) | collective-permute-done | bytes 131104 | tf_op jit(solution)/shard_map/ppermute | solution.py:486
  93.2 2.3 %collective-permute-start.18 = (bf16[1,32,16,128]{3,2,1,0:T(8,128)(2,1)S(1)}, bf16[1,32,16,128]{3,2,1,0:T(8,128)(2,1)S(1)}, u32[]{:S(2)}, u32[]{:S(2)}) collective-permute-start(bf16[1,32,16,128]{3,2,1,0:T(8,128)(2,1)S(1)} %get-tuple-element.91), channel_id=1, source_target_pairs={{0,4},{1,5},{2,6},{3,7},{4,0},{5,1},{6,2},{7,3},{8,12},{9,13},{10,... | collective-permute-start | bytes 393224 | tf_op jit(solution)/shard_map/ppermute | solution.py:486
  97.9 1.9 %collective-permute-start.36 = (bf16[1,32,16,128]{3,2,1,0:T(8,128)(2,1)S(1)}, bf16[1,32,16,128]{3,2,1,0:T(8,128)(2,1)S(1)}, u32[]{:S(2)}, u32[]{:S(2)}) collective-permute-start(bf16[1,32,16,128]{3,2,1,0:T(8,128)(2,1)S(1)} %get-tuple-element.111), channel_id=1, source_target_pairs={{0,4},{1,5},{2,6},{3,7},{4,0},{5,1},{6,2},{7,3},{8,12},{9,13},{10,... | collective-permute-start | bytes 393224 | tf_op jit(solution)/shard_map/ppermute | solution.py:486
  100.3 2.4 %collective-permute-done.19.refs_6_ = bf16[1,32,16,128]{3,2,1,0:T(8,128)(2,1)S(1)} collective-permute-done((bf16[1,32,16,128]{3,2,1,0:T(8,128)(2,1)S(1)}, bf16[1,32,16,128]{3,2,1,0:T(8,128)(2,1)S(1)}, u32[]{:S(2)}, u32[]{:S(2)}) %collective-permute-start.19) | collective-permute-done | bytes 131104 | tf_op jit(solution)/shard_map/ppermute | solution.py:486
  102.8 1.6 %collective-permute-done.35.refs_8_ = bf16[1,32,16,128]{3,2,1,0:T(8,128)(2,1)S(1)} collective-permute-done((bf16[1,32,16,128]{3,2,1,0:T(8,128)(2,1)S(1)}, bf16[1,32,16,128]{3,2,1,0:T(8,128)(2,1)S(1)}, u32[]{:S(2)}, u32[]{:S(2)}) %collective-permute-start.35) | collective-permute-done | bytes 131104 | tf_op jit(solution)/shard_map/ppermute | solution.py:486
  105.4 2.3 %collective-permute-done.37.refs_10_ = bf16[1,32,16,128]{3,2,1,0:T(8,128)(2,1)S(1)} collective-permute-done((bf16[1,32,16,128]{3,2,1,0:T(8,128)(2,1)S(1)}, bf16[1,32,16,128]{3,2,1,0:T(8,128)(2,1)S(1)}, u32[]{:S(2)}, u32[]{:S(2)}) %collective-permute-start.37) | collective-permute-done | bytes 131104 | tf_op jit(solution)/shard_map/ppermute | solution.py:486
  107.7 2.8 %final_stage.1 = bf16[16,256,128]{2,1,0:T(8,128)(2,1)} custom-call(f32[16,128,256]{2,1,0:T(8,128)S(1)} %get-tuple-element.69.refs_0_, f32[16,128,256]{2,1,0:T(8,128)S(1)} %get-tuple-element.70.refs_1_, bf16[128,128]{1,0:T(8,128)(2,1)S(1)} %get-tuple-element.71.refs_2_, bf16[1,32,16,128]{3,2,1,0:T(8,128)(2,1)S(1)} %get-tuple-element.89.refs_3_, ...), custom_call_target="tpu_custom_call" | custom-call | flops 134217 | bytes 6291 | tf_op jit(solution)/shard_map/final_stage/pallas_call | solution.py:47
  (86 shorter events, 27.2 us)
Async XLA Ops:
  4.4 8.1 %collective-permute-start.2 = (bf16[17,16,128]{2,1,0:T(8,128)(2,1)S(1)}, bf16[17,16,128]{2,1,0:T(8,128)(2,1)S(1)}, u32[]{:S(2)}, u32[]{:S(2)}) collective-permute-start(bf16[17,16,128]{2,1,0:T(8,128)(2,1)S(1)} %get-tuple-element.60), channel_id=1, source_target_pairs={{0,12},{1,13},{2,14},{3,15},{4,0},{5,1},{6,2},{7,3},{8,4},{9,5},{1... | collective-permute-start | bytes 208904 | tf_op jit(solution)/shard_map/ppermute | solution.py:486
  16.3 8.6 %collective-permute-start.3 = (bf16[4,17,16,128]{3,2,1,0:T(8,128)(2,1)S(1)}, bf16[4,17,16,128]{3,2,1,0:T(8,128)(2,1)S(1)}, u32[]{:S(2)}, u32[]{:S(2)}) collective-permute-start(bf16[4,17,16,128]{3,2,1,0:T(8,128)(2,1)S(1)} %pad_maximum_fusion.1.refs_8_), channel_id=1, source_target_pairs={{0,2},{1,3},{2,0},{3,1},{4,6},{5,7},{6,4},{7,5},{8,10},{9,11},{10,... | collective-permute-start | bytes 835592 | tf_op jit(solution)/shard_map/ppermute | solution.py:486
  17.9 22.5 %collective-permute-start.6 = (bf16[18,128,128]{2,1,0:T(8,128)(2,1)S(1)}, bf16[18,128,128]{2,1,0:T(8,128)(2,1)S(1)}, u32[]{:S(2)}, u32[]{:S(2)}) collective-permute-start(bf16[18,128,128]{2,1,0:T(8,128)(2,1)S(1)} %pad_maximum_fusion), channel_id=1, source_target_pairs={{0,12},{1,13},{2,14},{3,15},{4,8},{5,9},{6,10},{7,11},{8,4},{9,5},... | collective-permute-start | bytes 1769480 | tf_op jit(solution)/shard_map/ppermute | solution.py:486
  24.9 39.9 %collective-permute-start.27 = (bf16[16,128,128]{2,1,0:T(8,128)(2,1)S(1)}, bf16[16,128,128]{2,1,0:T(8,128)(2,1)S(1)}, u32[]{:S(2)}, u32[]{:S(2)}) collective-permute-start(bf16[16,128,128]{2,1,0:T(8,128)(2,1)S(1)} %get-tuple-element.101), channel_id=1, source_target_pairs={{0,12},{1,13},{2,14},{3,15},{4,8},{5,9},{6,10},{7,11},{8,4},{9,5},... | collective-permute-start | bytes 1572872 | tf_op jit(solution)/shard_map/ppermute | solution.py:486
  36.8 8.4 %collective-permute-start.7 = (bf16[1,32,16,256]{3,2,1,0:T(8,128)(2,1)S(1)}, bf16[1,32,16,256]{3,2,1,0:T(8,128)(2,1)S(1)}, u32[]{:S(2)}, u32[]{:S(2)}) collective-permute-start(bf16[1,32,16,256]{3,2,1,0:T(8,128)(2,1)S(1)} %get-tuple-element.76), channel_id=1, source_target_pairs={{0,2},{1,3},{2,0},{3,1},{4,6},{5,7},{6,4},{7,5},{8,10},{9,11},{10,... | collective-permute-start | bytes 786440 | tf_op jit(solution)/shard_map/ppermute | solution.py:486
  38.4 13.3 %collective-permute-start.8 = (bf16[1,32,16,256]{3,2,1,0:T(8,128)(2,1)S(1)}, bf16[1,32,16,256]{3,2,1,0:T(8,128)(2,1)S(1)}, u32[]{:S(2)}, u32[]{:S(2)}) collective-permute-start(bf16[1,32,16,256]{3,2,1,0:T(8,128)(2,1)S(1)} %get-tuple-element.77), channel_id=1, source_target_pairs={{0,4},{1,5},{2,6},{3,7},{4,0},{5,1},{6,2},{7,3},{8,12},{9,13},{10,... | collective-permute-start | bytes 786440 | tf_op jit(solution)/shard_map/ppermute | solution.py:486
  38.7 18.4 %collective-permute-start.9 = (bf16[1,32,16,256]{3,2,1,0:T(8,128)(2,1)S(1)}, bf16[1,32,16,256]{3,2,1,0:T(8,128)(2,1)S(1)}, u32[]{:S(2)}, u32[]{:S(2)}) collective-permute-start(bf16[1,32,16,256]{3,2,1,0:T(8,128)(2,1)S(1)} %get-tuple-element.78), channel_id=1, source_target_pairs={{0,6},{1,7},{2,4},{3,5},{4,2},{5,3},{6,0},{7,1},{8,14},{9,15},{10,... | collective-permute-start | bytes 786440 | tf_op jit(solution)/shard_map/ppermute | solution.py:486
  57.1 12.9 %collective-permute-start.12 = (bf16[1,32,16,256]{3,2,1,0:T(8,128)(2,1)S(1)}, bf16[1,32,16,256]{3,2,1,0:T(8,128)(2,1)S(1)}, u32[]{:S(2)}, u32[]{:S(2)}) collective-permute-start(bf16[1,32,16,256]{3,2,1,0:T(8,128)(2,1)S(1)} %get-tuple-element.87), channel_id=1, source_target_pairs={{0,6},{1,7},{2,4},{3,5},{4,2},{5,3},{6,0},{7,1},{8,14},{9,15},{10,... | collective-permute-start | bytes 786440 | tf_op jit(solution)/shard_map/ppermute | solution.py:486
  63.1 9.7 %collective-permute-start.11 = (bf16[1,32,16,256]{3,2,1,0:T(8,128)(2,1)S(1)}, bf16[1,32,16,256]{3,2,1,0:T(8,128)(2,1)S(1)}, u32[]{:S(2)}, u32[]{:S(2)}) collective-permute-start(bf16[1,32,16,256]{3,2,1,0:T(8,128)(2,1)S(1)} %get-tuple-element.84), channel_id=1, source_target_pairs={{0,4},{1,5},{2,6},{3,7},{4,0},{5,1},{6,2},{7,3},{8,12},{9,13},{10,... | collective-permute-start | bytes 786440 | tf_op jit(solution)/shard_map/ppermute | solution.py:486
  67.0 8.6 %collective-permute-start.10 = (bf16[1,32,16,256]{3,2,1,0:T(8,128)(2,1)S(1)}, bf16[1,32,16,256]{3,2,1,0:T(8,128)(2,1)S(1)}, u32[]{:S(2)}, u32[]{:S(2)}) collective-permute-start(bf16[1,32,16,256]{3,2,1,0:T(8,128)(2,1)S(1)} %get-tuple-element.81), channel_id=1, source_target_pairs={{0,2},{1,3},{2,0},{3,1},{4,6},{5,7},{6,4},{7,5},{8,10},{9,11},{10,... | collective-permute-start | bytes 786440 | tf_op jit(solution)/shard_map/ppermute | solution.py:486
  68.4 10.0 %collective-permute-start.13 = (bf16[1,32,16,256]{3,2,1,0:T(8,128)(2,1)S(1)}, bf16[1,32,16,256]{3,2,1,0:T(8,128)(2,1)S(1)}, u32[]{:S(2)}, u32[]{:S(2)}) collective-permute-start(bf16[1,32,16,256]{3,2,1,0:T(8,128)(2,1)S(1)} %get-tuple-element.88.refs_4_), channel_id=1, source_target_pairs={{0,1},{1,0},{2,3},{3,2},{4,5},{5,4},{6,7},{7,6},{8,9},{9,8},{10,11... | collective-permute-start | bytes 786440 | tf_op jit(solution)/shard_map/ppermute | solution.py:486
  68.4 10.1 %collective-permute-start.14 = (bf16[1,32,16,256]{3,2,1,0:T(8,128)(2,1)S(1)}, bf16[1,32,16,256]{3,2,1,0:T(8,128)(2,1)S(1)}, u32[]{:S(2)}, u32[]{:S(2)}) collective-permute-start(bf16[1,32,16,256]{3,2,1,0:T(8,128)(2,1)S(1)} %collective-permute-done.7.refs_5_), channel_id=1, source_target_pairs={{0,1},{1,0},{2,3},{3,2},{4,5},{5,4},{6,7},{7,6},{8,9},{9,8},{10,11... | collective-permute-start | bytes 786440 | tf_op jit(solution)/shard_map/ppermute | solution.py:486
  70.0 11.4 %collective-permute-start.15 = (bf16[1,32,16,256]{3,2,1,0:T(8,128)(2,1)S(1)}, bf16[1,32,16,256]{3,2,1,0:T(8,128)(2,1)S(1)}, u32[]{:S(2)}, u32[]{:S(2)}) collective-permute-start(bf16[1,32,16,256]{3,2,1,0:T(8,128)(2,1)S(1)} %collective-permute-done.8.refs_6_), channel_id=1, source_target_pairs={{0,1},{1,0},{2,3},{3,2},{4,5},{5,4},{6,7},{7,6},{8,9},{9,8},{10,11... | collective-permute-start | bytes 786440 | tf_op jit(solution)/shard_map/ppermute | solution.py:486
  72.8 8.7 %collective-permute-start.16 = (bf16[1,32,16,256]{3,2,1,0:T(8,128)(2,1)S(1)}, bf16[1,32,16,256]{3,2,1,0:T(8,128)(2,1)S(1)}, u32[]{:S(2)}, u32[]{:S(2)}) collective-permute-start(bf16[1,32,16,256]{3,2,1,0:T(8,128)(2,1)S(1)} %collective-permute-done.9.refs_7_), channel_id=1, source_target_pairs={{0,1},{1,0},{2,3},{3,2},{4,5},{5,4},{6,7},{7,6},{8,9},{9,8},{10,11... | collective-permute-start | bytes 786440 | tf_op jit(solution)/shard_map/ppermute | solution.py:486
  78.4 7.3 %collective-permute-start.30 = (bf16[1,32,16,128]{3,2,1,0:T(8,128)(2,1)S(1)}, bf16[1,32,16,128]{3,2,1,0:T(8,128)(2,1)S(1)}, u32[]{:S(2)}, u32[]{:S(2)}) collective-permute-start(bf16[1,32,16,128]{3,2,1,0:T(8,128)(2,1)S(1)} %get-tuple-element.108), channel_id=1, source_target_pairs={{0,6},{1,7},{2,4},{3,5},{4,2},{5,3},{6,0},{7,1},{8,14},{9,15},{10,... | collective-permute-start | bytes 393224 | tf_op jit(solution)/shard_map/ppermute | solution.py:486
  78.5 10.1 %collective-permute-start.21 = (bf16[1,32,16,128]{3,2,1,0:T(8,128)(2,1)S(1)}, bf16[1,32,16,128]{3,2,1,0:T(8,128)(2,1)S(1)}, u32[]{:S(2)}, u32[]{:S(2)}) collective-permute-start(bf16[1,32,16,128]{3,2,1,0:T(8,128)(2,1)S(1)} %get-tuple-element.98), channel_id=1, source_target_pairs={{0,4},{1,5},{2,6},{3,7},{4,0},{5,1},{6,2},{7,3},{8,12},{9,13},{10,... | collective-permute-start | bytes 393224 | tf_op jit(solution)/shard_map/ppermute | solution.py:486
  81.4 8.8 %collective-permute-start.29 = (bf16[1,32,16,128]{3,2,1,0:T(8,128)(2,1)S(1)}, bf16[1,32,16,128]{3,2,1,0:T(8,128)(2,1)S(1)}, u32[]{:S(2)}, u32[]{:S(2)}) collective-permute-start(bf16[1,32,16,128]{3,2,1,0:T(8,128)(2,1)S(1)} %get-tuple-element.106), channel_id=1, source_target_pairs={{0,4},{1,5},{2,6},{3,7},{4,0},{5,1},{6,2},{7,3},{8,12},{9,13},{10,... | collective-permute-start | bytes 393224 | tf_op jit(solution)/shard_map/ppermute | solution.py:486
  81.5 8.7 %collective-permute-start.20 = (bf16[1,32,16,128]{3,2,1,0:T(8,128)(2,1)S(1)}, bf16[1,32,16,128]{3,2,1,0:T(8,128)(2,1)S(1)}, u32[]{:S(2)}, u32[]{:S(2)}) collective-permute-start(bf16[1,32,16,128]{3,2,1,0:T(8,128)(2,1)S(1)} %get-tuple-element.96), channel_id=1, source_target_pairs={{0,2},{1,3},{2,0},{3,1},{4,6},{5,7},{6,4},{7,5},{8,10},{9,11},{10,... | collective-permute-start | bytes 393224 | tf_op jit(solution)/shard_map/ppermute | solution.py:486
  82.4 8.4 %collective-permute-start.28 = (bf16[1,32,16,128]{3,2,1,0:T(8,128)(2,1)S(1)}, bf16[1,32,16,128]{3,2,1,0:T(8,128)(2,1)S(1)}, u32[]{:S(2)}, u32[]{:S(2)}) collective-permute-start(bf16[1,32,16,128]{3,2,1,0:T(8,128)(2,1)S(1)} %get-tuple-element.104), channel_id=1, source_target_pairs={{0,2},{1,3},{2,0},{3,1},{4,6},{5,7},{6,4},{7,5},{8,10},{9,11},{10,... | collective-permute-start | bytes 393224 | tf_op jit(solution)/shard_map/ppermute | solution.py:486
  92.1 7.7 %collective-permute-start.17 = (bf16[1,32,16,128]{3,2,1,0:T(8,128)(2,1)S(1)}, bf16[1,32,16,128]{3,2,1,0:T(8,128)(2,1)S(1)}, u32[]{:S(2)}, u32[]{:S(2)}) collective-permute-start(bf16[1,32,16,128]{3,2,1,0:T(8,128)(2,1)S(1)} %get-tuple-element.90), channel_id=1, source_target_pairs={{0,2},{1,3},{2,0},{3,1},{4,6},{5,7},{6,4},{7,5},{8,10},{9,11},{10,... | collective-permute-start | bytes 393224 | tf_op jit(solution)/shard_map/ppermute | solution.py:486
  95.4 7.4 %collective-permute-start.19 = (bf16[1,32,16,128]{3,2,1,0:T(8,128)(2,1)S(1)}, bf16[1,32,16,128]{3,2,1,0:T(8,128)(2,1)S(1)}, u32[]{:S(2)}, u32[]{:S(2)}) collective-permute-start(bf16[1,32,16,128]{3,2,1,0:T(8,128)(2,1)S(1)} %get-tuple-element.92), channel_id=1, source_target_pairs={{0,6},{1,7},{2,4},{3,5},{4,2},{5,3},{6,0},{7,1},{8,14},{9,15},{10,... | collective-permute-start | bytes 393224 | tf_op jit(solution)/shard_map/ppermute | solution.py:486
  96.7 7.7 %collective-permute-start.35 = (bf16[1,32,16,128]{3,2,1,0:T(8,128)(2,1)S(1)}, bf16[1,32,16,128]{3,2,1,0:T(8,128)(2,1)S(1)}, u32[]{:S(2)}, u32[]{:S(2)}) collective-permute-start(bf16[1,32,16,128]{3,2,1,0:T(8,128)(2,1)S(1)} %get-tuple-element.110), channel_id=1, source_target_pairs={{0,2},{1,3},{2,0},{3,1},{4,6},{5,7},{6,4},{7,5},{8,10},{9,11},{10,... | collective-permute-start | bytes 393224 | tf_op jit(solution)/shard_map/ppermute | solution.py:486
  97.9 7.5 %collective-permute-start.36 = (bf16[1,32,16,128]{3,2,1,0:T(8,128)(2,1)S(1)}, bf16[1,32,16,128]{3,2,1,0:T(8,128)(2,1)S(1)}, u32[]{:S(2)}, u32[]{:S(2)}) collective-permute-start(bf16[1,32,16,128]{3,2,1,0:T(8,128)(2,1)S(1)} %get-tuple-element.111), channel_id=1, source_target_pairs={{0,4},{1,5},{2,6},{3,7},{4,0},{5,1},{6,2},{7,3},{8,12},{9,13},{10,... | collective-permute-start | bytes 393224 | tf_op jit(solution)/shard_map/ppermute | solution.py:486
  99.8 7.8 %collective-permute-start.37 = (bf16[1,32,16,128]{3,2,1,0:T(8,128)(2,1)S(1)}, bf16[1,32,16,128]{3,2,1,0:T(8,128)(2,1)S(1)}, u32[]{:S(2)}, u32[]{:S(2)}) collective-permute-start(bf16[1,32,16,128]{3,2,1,0:T(8,128)(2,1)S(1)} %get-tuple-element.112), channel_id=1, source_target_pairs={{0,6},{1,7},{2,4},{3,5},{4,2},{5,3},{6,0},{7,1},{8,14},{9,15},{10,... | collective-permute-start | bytes 393224 | tf_op jit(solution)/shard_map/ppermute | solution.py:486
  (24 other events, 148.6 us)

commit v3 on v2

--- a/solution.py
+++ b/solution.py
@@ -25,12 +25,14 @@
     return centred * lax.rsqrt(var + 1e-05)
 
 
-def local_call(name, kernel, steps, ins, outs, scratch, limit, flops=0, data=0, special=0):
+def local_call(name, kernel, steps, ins, outs, scratch, limit, flops=0, data=0, special=0, windows=False):
     whole = steps == 1
     in_specs, out_specs, out_shape = [], [], []
     for value, block, index in ins:
         if block is None:
             in_specs.append(pl.BlockSpec(memory_space=pltpu.SMEM))
+        elif whole and windows:
+            in_specs.append(pl.BlockSpec(value.shape, lambda ndim=value.ndim: (0,) * ndim))
         elif whole:
             in_specs.append(pl.BlockSpec(memory_space=pltpu.VMEM))
         else:
@@ -131,6 +133,7 @@
         12,
         flops=4 * seqs * rows * breadth * proj,
         data=2 * seqs * rows * breadth,
+        windows=True,
     )
 
 
@@ -173,16 +176,17 @@
     for index, ref in enumerate(right_refs):
         core, y = index // 2, index % 2
         for z in range(4):
-            right[((me // 4 - z) & 3) * 4 + ((me & 3) ^ (2 * y + core))] = ref[z]
-
-
-def make_updates(left_ref, mask, right, outer, count):
+            right[me ^ (4 * z + 2 * y + core)] = ref[z]
+
+
+def make_updates(left_ref, mask, right, outer, scale):
     slices = right.shape[1]
     rows, depth, block = outer.shape
     proj = depth // (2 * (slices - 1))
-    count[...] = lax.dot_general(
+    count = lax.dot_general(
         mask, right[:, slices - 1].reshape(block, LANES), NT, preferred_element_type=F32
     )
+    scale[...] = 1.0 / jnp.maximum(count, 1.0)
     left = left_ref[...].astype(F32)
     turned = pltpu.roll(left, LANES // 2, 1)
     low = lax.broadcasted_iota(jnp.int32, left.shape, 1) < LANES // 2
@@ -210,9 +214,9 @@
             ].reshape(rows, proj, block)
 
 
-def row_update(i, w_out_ref, outer, count):
+def row_update(i, w_out_ref, outer, scale):
     update = jnp.dot(w_out_ref[...], outer[i], preferred_element_type=F32)
-    return update / jnp.maximum(count[i : i + 1], 1.0)
+    return update * scale[i : i + 1]
 
 
 def chip_here(split):
@@ -261,12 +265,12 @@
         order_right(right_refs, right)
     else:
         right = right_refs[0]
-    outer, kept_a, kept_b, count = refs
+    outer, kept_a, kept_b, scale = refs
     rows = couple_ref.shape[0]
     hidden = w_in_ref.shape[0] // 4
-    make_updates(left_ref, mask_ref[...], right, outer, count)
+    make_updates(left_ref, mask_ref[...], right, outer, scale)
     for i in range(rows):
-        pair = couple_ref[i].astype(F32).T + row_update(i, w_out_ref, outer, count)
+        pair = couple_ref[i].astype(F32).T + row_update(i, w_out_ref, outer, scale)
         norm = standardize(pair, 0).astype(BF16)
         pair_ref[i] = pair
         gate_ref[i] = sigmoid(jnp.dot(w_gate_ref[...], norm, preferred_element_type=F32))
@@ -277,25 +281,24 @@
 
 
 def update_kernel(left_ref, w_out_ref, right, *refs):
-    mask_refs, (update_ref, outer, count) = refs[:-3], refs[-3:]
+    mask_refs, (update_ref, outer, scale) = refs[:-3], refs[-3:]
     if mask_refs:
         mask = mask_refs[0][...]
     else:
         mask = right[lax.axis_index("row") ^ 12, right.shape[1] - 1]
-    make_updates(left_ref, mask, right, outer, count)
+    make_updates(left_ref, mask, right, outer, scale)
     for i in range(update_ref.shape[0]):
-        update_ref[i] = row_update(i, w_out_ref, outer, count)
-
-
-def mirror_kernel(low, mirror, update_ref, couple_ref, w_in_ref, obs_ref, seen_ref, *refs):
+        update_ref[i] = row_update(i, w_out_ref, outer, scale)
+
+
+def mirror_kernel(mirror, update_ref, couple_ref, w_in_ref, obs_ref, seen_ref, *refs):
     outs, kept = refs[:-1], refs[-1]
-    rows, block = update_ref.shape[0], couple_ref.shape[1]
+    rows = couple_ref.shape[0]
     hidden = w_in_ref.shape[0] // 4
-    cols = slice(low, low + block)
     for i in range(rows):
-        pair = couple_ref[i].astype(F32).T + update_ref[i, :, cols]
+        pair = couple_ref[i].astype(F32).T + update_ref[i]
         device = mirror(lax.axis_index("row"))
-        seen = observed(device, obs_ref, seen_ref, rows, i)[:, cols]
+        seen = observed(device, obs_ref, seen_ref, rows, i)
         norm = standardize(pair, 0).astype(BF16)
         keep_sides(i, norm, w_in_ref.at[2 * hidden :], seen, (kept,), hidden)
     write_sides(kept, outs, rows, hidden)
@@ -359,44 +362,39 @@
     )[0]
 
 
-def mirror_stage(low, mirror, update, couple, w_in, obs, parts, split):
-    rows, width = update.shape[:2]
-    total = couple.shape[1]
+def mirror_stage(mirror, update, couple, w_in, obs, parts, split):
+    rows, total, width = couple.shape
     hidden = w_in.shape[0] // 4
-    block = min(BLOCK, total)
     return local_call(
         "mirror_stage",
-        lambda *refs: mirror_kernel(low, mirror, *refs),
-        total // block,
-        [last(update, block), couple_input(couple), fixed(w_in), scalars(obs)]
-        + [last(obs[None], block)],
-        [last_out((parts // split, hidden // parts, rows, total), BF16, block)] * split,
-        [kept_scratch(rows, hidden, block)],
+        lambda *refs: mirror_kernel(mirror, *refs),
+        total // BLOCK,
+        [last(update, BLOCK), couple_input(couple), fixed(w_in), scalars(obs)]
+        + [last(obs[None], BLOCK)],
+        [last_out((parts // split, hidden // parts, rows, total), BF16, BLOCK)] * split,
+        [kept_scratch(rows, hidden, BLOCK)],
         16,
         flops=4 * rows * total * hidden * width,
-        data=8 * rows * total * width,
+        data=40000 * rows * total * width,
         special=rows * total * hidden,
     )
 
 
-def tri_kernel(cores, split, cuts, flip, *refs):
+def tri_kernel(cores, split, flip, *refs):
     a_refs, refs = refs[:split], refs[split:]
-    b_refs = [refs[cut * cores * split : (cut + 1) * cores * split] for cut in range(cuts)]
-    outs, whole = refs[cuts * cores * split : -1], refs[-1]
+    b_refs, refs = refs[: cores * split], refs[cores * split :]
+    outs, whole = refs[:-1], refs[-1]
     per, chans, rows, total = a_refs[0].shape
-    depth = total // cuts
     chip = chip_here(split)
     core = lax.axis_index("row") & 1
     for c in range(chans):
-        for cut in range(cuts):
-            for index, ref in enumerate(b_refs[cut]):
-                for slot in range(per):
-                    part = (index % split) * per + slot
-                    place = (chip ^ part ^ flip) * cores
-                    if cores == 2:
-                        place = place + (core ^ (index // split))
-                    place = pl.multiple_of(place * rows, rows)
-                    whole[c, pl.ds(place, rows), cut * depth : (cut + 1) * depth] = ref[slot, c]
+        for index, ref in enumerate(b_refs):
+            for slot in range(per):
+                part = (index % split) * per + slot
+                place = (chip ^ part ^ flip) * cores
+                if cores == 2:
+                    place = place + (core ^ (index // split))
+                whole[c, pl.ds(pl.multiple_of(place * rows, rows), rows), :] = ref[slot, c]
         side_a = jnp.concatenate([ref[slot, c] for ref in a_refs for slot in range(per)])
         product = lax.dot_general(side_a, whole[c], NT, preferred_element_type=F32).astype(BF16)
         for part in range(per * split):
@@ -415,10 +413,10 @@
     shape = (per, chans, rows, half)
     return local_call(
         "tri_stage",
-        lambda *refs: tri_kernel(cores, split, len(b), flip, *refs),
+        lambda *refs: tri_kernel(cores, split, flip, *refs),
         chans // step,
         [channels(value, step) for value in a]
-        + [channels(value, step) for cut in b for value in cut],
+        + [channels(value, step) for value in b],
         [(shape, BF16, (per, step, rows, half), lambda c: (0, c, 0, 0))] * split,
         [pltpu.VMEM((step, half, total), BF16)],
         16,
@@ -531,7 +529,7 @@
     half = devs // 2
     me = lax.axis_index("row")
     hops = devs == 16
-    cores, cuts = (2, 2) if hops else (1, 1)
+    cores = 2 if hops else 1
     parts = half // cores
     split = parts if hops else 1
     obs = observed_indicator
@@ -548,11 +546,6 @@
         first_factor_matrix.T,
         second_factor_matrix.T,
     )
-    couples = [
-        couple_features[:, cut * total // cuts : (cut + 1) * total // cuts] for cut in range(cuts)
-    ]
-    if hops:
-        couples[0] = jnp.concatenate([couples[0], left.reshape(-1, total // cuts, width)])
     weights = weights_stage(
         product_final_matrix,
         edge_projection_matrix,
@@ -560,37 +553,38 @@
         multiplicative_final_matrix,
     )
     if hops:
-        held = [block] + [send(block, lambda i, d=d: (i + 4 * d) % devs) for d in (1, 2, 3)]
-        held, (*couples, weights) = after(jnp.stack(held), (*couples, weights))
+        slices = block.shape[0]
+        both = send(jnp.concatenate([block, left.reshape((-1,) + block.shape[1:])]), mirror)
+        held = [block, send(block, lambda i: i ^ 4), send(block, lambda i: i ^ 8), both[:slices]]
+        far_left = both[slices:].reshape(left.shape)
+        held, (couple_out, weights) = after(jnp.stack(held), (couple_features, weights))
+        far_couple = mirrored(couple_out)
         other = send(held, lambda i: i ^ 2)
         right = [held, other, send(held, lambda i: i ^ 1), send(other, lambda i: i ^ 1)]
         far_mask = None
     else:
         right = [lax.all_gather(block, "row", axis=0)]
         far_left = mirrored(left)
+        far_couple = mirrored(couple_features)
         far_mask = right[0][mirror(me), -1]
-    far_couples = [mirrored(value) for value in couples]
-    if hops:
-        far_left = far_couples[0][rows:].reshape(left.shape)
     w_out, w_in, w_gate, w_final = weights
 
     pair, gate, *sides = pair_stage(
         left, right, block[-1], couple_features, w_out, w_in, w_gate, obs, parts, split
     )
-    a, b = sides[:split], sides[split : 2 * split]
+    a, b = list(sides[:split]), list(sides[split : 2 * split])
     ordered = sides[2 * split] if hops else right[0]
     b = exchange(b)
+    a = exchange(a, b)
+    if hops:
+        _, far_left = after(b[1], far_left)
     update = update_stage(far_left, ordered, far_mask, w_out, rows, total)
     if hops:
         update, b = after(update, b)
-    a = exchange(a, b)
-    b = with_other_core(b)
-    near = exchange(tri_stage(a, [b], cores, 0))
-    far_b = []
-    for cut, value in enumerate(far_couples):
-        low = cut * total // cuts
-        sides = mirror_stage(low, mirror, update, value, w_in, obs, parts, split)
-        far_b.append(with_other_core(exchange(sides, a)))
+    near = tri_stage(a, with_other_core(b), cores, 0)
+    far_b = mirror_stage(mirror, update, far_couple, w_in, obs, parts, split)
+    far_b = with_other_core(exchange(far_b, a))
+    near = exchange(near)
     far = exchange(tri_stage(a, far_b, cores, 2 if hops else 0))
     if hops:
         spans = [near, far]

time: 111 us -> 101 us (0.910)
  starting transfers between devices: 38.1 us -> 28.4 us
  local copies, waits for them, and re-layouts: 4.48 us -> 7.32 us
  waiting for transfers between devices: 43.2 us -> 41 us
    ppermute x38 -> x30, starting transfers between devices: 38.1 us -> 28.4 us  [send(): return lax.ppermute(value, 'row', [(i, move(i)) for i in range(devs)])]
    unnamed x20, local copies, waits for them, and re-layouts: 3.2 us -> 7.31 us
    ppermute x38 -> x30, waiting for transfers between devices: 43.2 us -> 41 us  [send(): return lax.ppermute(value, 'row', [(i, move(i)) for i in range(devs)])]
    slice x2 -> x1, local copies, waits for them, and re-layouts: 1.28 us -> 0.01 us  [body(): far_left = both[slices:].reshape(left.shape)]
    pallas_call x9 -> x8, Pallas kernels: 24.4 us -> 23.9 us  [local_call(): pl.pallas_call(kernel, grid=() if whole else (steps,), in_specs=in_specs,...]
  transfers between devices with their start and end apart: 38 -> 30, of which waited for: 17 -> 14; matrix products, arithmetic and copies ran while one was open for 1% -> 0% of each run, Pallas kernels for 18% -> 20%
where the time goes in v3:
time: 101 us
  waiting for transfers between devices  41 us (41%)
  starting transfers between devices  28.4 us (28%)
  Pallas kernels  23.9 us (24%)
  local copies, waits for them, and re-layouts  7.32 us (7%)
    ppermute x30, waiting for transfers between devices, send(): return lax.ppermute(value, 'row', [(i, move(i)) for i in range(devs)])  41 us
    ppermute x30, starting transfers between devices, send(): return lax.ppermute(value, 'row', [(i, move(i)) for i in range(devs)])  28.4 us
    pallas_call x8, Pallas kernels, local_call(): pl.pallas_call(kernel, grid=() if whole else (steps,), in_specs=in_specs,...  23.9 us
    unnamed x20, local copies, waits for them, and re-layouts  7.31 us
  transfers between devices with their start and end apart: 30, of which 14 were waited for; matrix products, arithmetic and copies ran while one was open for 0% of the time, Pallas kernels for 20%

profile of v3, /device:TPU:0, one launch (start us, length us, event | category | flops | bytes accessed | tf_op | source)
XLA Modules:
  0.0 100.8 jit_solution(3358819882244356987)
XLA Ops:
  4.5 5.1 %collective-permute-start.2 = (bf16[33,16,128]{2,1,0:T(8,128)(2,1)S(1)}, bf16[33,16,128]{2,1,0:T(8,128)(2,1)S(1)}, u32[]{:S(2)}, u32[]{:S(2)}) collective-permute-start(bf16[33,16,128]{2,1,0:T(8,128)(2,1)S(1)} %pad_maximum_fusion.1), channel_id=1, source_target_pairs={{0,12},{1,13},{2,14},{3,15},{4,8},{5,9},{6,10},{7,11},{8,4},{9,5},... | collective-permute-start | bytes 405512 | tf_op jit(solution)/shard_map/ppermute | solution.py:484
  14.2 4.0 %collective-permute-done.1 = bf16[17,16,128]{2,1,0:T(8,128)(2,1)S(1)} collective-permute-done((bf16[17,16,128]{2,1,0:T(8,128)(2,1)S(1)}, bf16[17,16,128]{2,1,0:T(8,128)(2,1)S(1)}, u32[]{:S(2)}, u32[]{:S(2)}) %collective-permute-start.1) | collective-permute-done | bytes 69664 | tf_op jit(solution)/shard_map/ppermute | solution.py:484
  18.3 2.5 %collective-permute-start.19 = (bf16[16,256,128]{2,1,0:T(8,128)(2,1)}, bf16[16,256,128]{2,1,0:T(8,128)(2,1)S(1)}, u32[]{:S(2)}, u32[]{:S(2)}) collective-permute-start(bf16[16,256,128]{2,1,0:T(8,128)(2,1)} %refs_2_.1), channel_id=1, source_target_pairs={{0,12},{1,13},{2,14},{3,15},{4,8},{5,9},{6,10},{7,11},{8,4},{9,5},... | collective-permute-start | bytes 3145736 | tf_op jit(solution)/shard_map/ppermute | solution.py:484
  22.4 5.4 %collective-permute-done.3.refs_9_ = bf16[4,17,16,128]{3,2,1,0:T(8,128)(2,1)S(1)} collective-permute-done((bf16[4,17,16,128]{3,2,1,0:T(8,128)(2,1)S(1)}, bf16[4,17,16,128]{3,2,1,0:T(8,128)(2,1)S(1)}, u32[]{:S(2)}, u32[]{:S(2)}) %collective-permute-start.3) | collective-permute-done | bytes 278560 | tf_op jit(solution)/shard_map/ppermute | solution.py:484
  30.0 10.3 %pair_stage.1 = (f32[16,128,256]{2,1,0:T(8,128)S(1)}, f32[16,128,256]{2,1,0:T(8,128)S(1)}, bf16[1,32,16,256]{3,2,1,0:T(8,128)(2,1)S(1)}, bf16[1,32,16,256]{3,2,1...) custom-call(bf16[256,128]{1,0:T(8,128)(2,1)S(1)} %get-tuple-element., ...), custom_call_target="tpu_custom_call" | custom-call | flops 2147483 | bytes 8388 | tf_op jit(solution)/shard_map/pair_stage/pallas_call | solution.py:49
  40.4 1.6 %collective-permute-start.6 = (bf16[1,32,16,256]{3,2,1,0:T(8,128)(2,1)S(1)}, bf16[1,32,16,256]{3,2,1,0:T(8,128)(2,1)S(1)}, u32[]{:S(2)}, u32[]{:S(2)}) collective-permute-start(bf16[1,32,16,256]{3,2,1,0:T(8,128)(2,1)S(1)} %get-tuple-element.66), channel_id=1, source_target_pairs={{0,2},{1,3},{2,0},{3,1},{4,6},{5,7},{6,4},{7,5},{8,10},{9,11},{10,... | collective-permute-start | bytes 786440 | tf_op jit(solution)/shard_map/ppermute | solution.py:484
  42.0 2.0 %collective-permute-start.10 = (bf16[1,32,16,256]{3,2,1,0:T(8,128)(2,1)S(1)}, bf16[1,32,16,256]{3,2,1,0:T(8,128)(2,1)S(1)}, u32[]{:S(2)}, u32[]{:S(2)}) collective-permute-start(bf16[1,32,16,256]{3,2,1,0:T(8,128)(2,1)S(1)} %get-tuple-element.72), channel_id=1, source_target_pairs={{0,6},{1,7},{2,4},{3,5},{4,2},{5,3},{6,0},{7,1},{8,14},{9,15},{10,... | collective-permute-start | bytes 786440 | tf_op jit(solution)/shard_map/ppermute | solution.py:484
  43.9 4.8 %collective-permute-done.6.refs_5_ = bf16[1,32,16,256]{3,2,1,0:T(8,128)(2,1)S(1)} collective-permute-done((bf16[1,32,16,256]{3,2,1,0:T(8,128)(2,1)S(1)}, bf16[1,32,16,256]{3,2,1,0:T(8,128)(2,1)S(1)}, u32[]{:S(2)}, u32[]{:S(2)}) %collective-permute-start.6) | collective-permute-done | bytes 262176 | tf_op jit(solution)/shard_map/ppermute | solution.py:484
  51.1 6.0 %collective-permute-done.10.refs_7_ = bf16[1,32,16,256]{3,2,1,0:T(8,128)(2,1)S(1)} collective-permute-done((bf16[1,32,16,256]{3,2,1,0:T(8,128)(2,1)S(1)}, bf16[1,32,16,256]{3,2,1,0:T(8,128)(2,1)S(1)}, u32[]{:S(2)}, u32[]{:S(2)}) %collective-permute-start.10) | collective-permute-done | bytes 262176 | tf_op jit(solution)/shard_map/ppermute | solution.py:484
  57.7 4.7 %update_stage.1.refs_0_ = f32[16,128,256]{2,1,0:T(8,128)S(1)} custom-call(bf16[256,128]{1,0:T(8,128)(2,1)S(1)} %bitcast.14, bf16[128,1024]{1,0:T(8,128)(2,1)S(1)} %get-tuple-element.58.refs_3_.w_out_ref, bf16[16,17,16,128]{3,2,1,0:T(8,128)(2,1)S(1)} %get-tuple-element.76.right), custom_call_target="tpu_custom_call" | custom-call | flops 2147483 | bytes 4194 | tf_op jit(solution)/shard_map/update_stage/pallas_call | solution.py:49
  62.9 2.6 %mirror_stage.1 = (bf16[1,32,16,256]{3,2,1,0:T(8,128)(2,1)S(1)}, bf16[1,32,16,256]{3,2,1,0:T(8,128)(2,1)S(1)}, bf16[1,32,16,256]{3,2,1,0:T(8,128)(2,1)S(1)}, bf16[1,32,16,256]{3,2,1,0:T(8,128)(2,1)S(1)}) custom-call(f32[16,128,256]{2,1,0:T(8,128)S(1)} %update_stage.1.refs_0_, bf16[16,256,128]{2,1,0:T(8,128)(2,1)S(1)} %collective-permute-done.19.refs_1_, ...), custom_call_target="tpu_custom_call" | custom-call | flops 268435 | bytes 20971520 | tf_op jit(solution)/shard_map/mirror_stage/pallas_call | solution.py:49
  65.7 1.9 %collective-permute-start.20 = (bf16[1,32,16,256]{3,2,1,0:T(8,128)(2,1)S(1)}, bf16[1,32,16,256]{3,2,1,0:T(8,128)(2,1)S(1)}, u32[]{:S(2)}, u32[]{:S(2)}) collective-permute-start(bf16[1,32,16,256]{3,2,1,0:T(8,128)(2,1)S(1)} %get-tuple-element.90), channel_id=1, source_target_pairs={{0,2},{1,3},{2,0},{3,1},{4,6},{5,7},{6,4},{7,5},{8,10},{9,11},{10,... | collective-permute-start | bytes 786440 | tf_op jit(solution)/shard_map/ppermute | solution.py:484
  67.9 1.8 %collective-permute-start.21 = (bf16[1,32,16,256]{3,2,1,0:T(8,128)(2,1)S(1)}, bf16[1,32,16,256]{3,2,1,0:T(8,128)(2,1)S(1)}, u32[]{:S(2)}, u32[]{:S(2)}) collective-permute-start(bf16[1,32,16,256]{3,2,1,0:T(8,128)(2,1)S(1)} %get-tuple-element.92), channel_id=1, source_target_pairs={{0,4},{1,5},{2,6},{3,7},{4,0},{5,1},{6,2},{7,3},{8,12},{9,13},{10,... | collective-permute-start | bytes 786440 | tf_op jit(solution)/shard_map/ppermute | solution.py:484
  70.4 4.2 %collective-permute-done.20.refs_5_ = bf16[1,32,16,256]{3,2,1,0:T(8,128)(2,1)S(1)} collective-permute-done((bf16[1,32,16,256]{3,2,1,0:T(8,128)(2,1)S(1)}, bf16[1,32,16,256]{3,2,1,0:T(8,128)(2,1)S(1)}, u32[]{:S(2)}, u32[]{:S(2)}) %collective-permute-start.20) | collective-permute-done | bytes 262176 | tf_op jit(solution)/shard_map/ppermute | solution.py:484
  74.6 2.5 %collective-permute-done.21.refs_6_ = bf16[1,32,16,256]{3,2,1,0:T(8,128)(2,1)S(1)} collective-permute-done((bf16[1,32,16,256]{3,2,1,0:T(8,128)(2,1)S(1)}, bf16[1,32,16,256]{3,2,1,0:T(8,128)(2,1)S(1)}, u32[]{:S(2)}, u32[]{:S(2)}) %collective-permute-start.21) | collective-permute-done | bytes 262176 | tf_op jit(solution)/shard_map/ppermute | solution.py:484
  77.0 4.5 %collective-permute-done.22.refs_7_ = bf16[1,32,16,256]{3,2,1,0:T(8,128)(2,1)S(1)} collective-permute-done((bf16[1,32,16,256]{3,2,1,0:T(8,128)(2,1)S(1)}, bf16[1,32,16,256]{3,2,1,0:T(8,128)(2,1)S(1)}, u32[]{:S(2)}, u32[]{:S(2)}) %collective-permute-start.22) | collective-permute-done | bytes 262176 | tf_op jit(solution)/shard_map/ppermute | solution.py:484
  82.3 1.7 %collective-permute-start.16 = (bf16[1,32,16,128]{3,2,1,0:T(8,128)(2,1)S(1)}, bf16[1,32,16,128]{3,2,1,0:T(8,128)(2,1)S(1)}, u32[]{:S(2)}, u32[]{:S(2)}) collective-permute-start(bf16[1,32,16,128]{3,2,1,0:T(8,128)(2,1)S(1)} %get-tuple-element.83), channel_id=1, source_target_pairs={{0,2},{1,3},{2,0},{3,1},{4,6},{5,7},{6,4},{7,5},{8,10},{9,11},{10,... | collective-permute-start | bytes 393224 | tf_op jit(solution)/shard_map/ppermute | solution.py:484
  84.1 1.6 %collective-permute-start.17 = (bf16[1,32,16,128]{3,2,1,0:T(8,128)(2,1)S(1)}, bf16[1,32,16,128]{3,2,1,0:T(8,128)(2,1)S(1)}, u32[]{:S(2)}, u32[]{:S(2)}) collective-permute-start(bf16[1,32,16,128]{3,2,1,0:T(8,128)(2,1)S(1)} %get-tuple-element.84), channel_id=1, source_target_pairs={{0,4},{1,5},{2,6},{3,7},{4,0},{5,1},{6,2},{7,3},{8,12},{9,13},{10,... | collective-permute-start | bytes 393224 | tf_op jit(solution)/shard_map/ppermute | solution.py:484
  86.7 1.7 %collective-permute-start.27 = (bf16[1,32,16,128]{3,2,1,0:T(8,128)(2,1)S(1)}, bf16[1,32,16,128]{3,2,1,0:T(8,128)(2,1)S(1)}, u32[]{:S(2)}, u32[]{:S(2)}) collective-permute-start(bf16[1,32,16,128]{3,2,1,0:T(8,128)(2,1)S(1)} %get-tuple-element.96), channel_id=1, source_target_pairs={{0,2},{1,3},{2,0},{3,1},{4,6},{5,7},{6,4},{7,5},{8,10},{9,11},{10,... | collective-permute-start | bytes 393224 | tf_op jit(solution)/shard_map/ppermute | solution.py:484
  88.4 1.6 %collective-permute-start.28 = (bf16[1,32,16,128]{3,2,1,0:T(8,128)(2,1)S(1)}, bf16[1,32,16,128]{3,2,1,0:T(8,128)(2,1)S(1)}, u32[]{:S(2)}, u32[]{:S(2)}) collective-permute-start(bf16[1,32,16,128]{3,2,1,0:T(8,128)(2,1)S(1)} %get-tuple-element.97), channel_id=1, source_target_pairs={{0,4},{1,5},{2,6},{3,7},{4,0},{5,1},{6,2},{7,3},{8,12},{9,13},{10,... | collective-permute-start | bytes 393224 | tf_op jit(solution)/shard_map/ppermute | solution.py:484
  91.0 2.0 %collective-permute-done.18.refs_6_ = bf16[1,32,16,128]{3,2,1,0:T(8,128)(2,1)S(1)} collective-permute-done((bf16[1,32,16,128]{3,2,1,0:T(8,128)(2,1)S(1)}, bf16[1,32,16,128]{3,2,1,0:T(8,128)(2,1)S(1)}, u32[]{:S(2)}, u32[]{:S(2)}) %collective-permute-start.18) | collective-permute-done | bytes 131104 | tf_op jit(solution)/shard_map/ppermute | solution.py:484
  93.0 1.9 %collective-permute-done.27.refs_8_ = bf16[1,32,16,128]{3,2,1,0:T(8,128)(2,1)S(1)} collective-permute-done((bf16[1,32,16,128]{3,2,1,0:T(8,128)(2,1)S(1)}, bf16[1,32,16,128]{3,2,1,0:T(8,128)(2,1)S(1)}, u32[]{:S(2)}, u32[]{:S(2)}) %collective-permute-start.27) | collective-permute-done | bytes 131104 | tf_op jit(solution)/shard_map/ppermute | solution.py:484
  96.1 1.9 %collective-permute-done.29.refs_10_ = bf16[1,32,16,128]{3,2,1,0:T(8,128)(2,1)S(1)} collective-permute-done((bf16[1,32,16,128]{3,2,1,0:T(8,128)(2,1)S(1)}, bf16[1,32,16,128]{3,2,1,0:T(8,128)(2,1)S(1)}, u32[]{:S(2)}, u32[]{:S(2)}) %collective-permute-start.29) | collective-permute-done | bytes 131104 | tf_op jit(solution)/shard_map/ppermute | solution.py:484
  98.0 2.8 %final_stage.1 = bf16[16,256,128]{2,1,0:T(8,128)(2,1)} custom-call(f32[16,128,256]{2,1,0:T(8,128)S(1)} %get-tuple-element.62.refs_0_, f32[16,128,256]{2,1,0:T(8,128)S(1)} %get-tuple-element.63.refs_1_, bf16[128,128]{1,0:T(8,128)(2,1)S(1)} %get-tuple-element.64.refs_2_, bf16[1,32,16,128]{3,2,1,0:T(8,128)(2,1)S(1)} %get-tuple-element.82.refs_3_, ...), custom_call_target="tpu_custom_call" | custom-call | flops 134217 | bytes 6291 | tf_op jit(solution)/shard_map/final_stage/pallas_call | solution.py:49
  (69 shorter events, 21.5 us)
Async XLA Ops:
  4.5 9.7 %collective-permute-start.2 = (bf16[33,16,128]{2,1,0:T(8,128)(2,1)S(1)}, bf16[33,16,128]{2,1,0:T(8,128)(2,1)S(1)}, u32[]{:S(2)}, u32[]{:S(2)}) collective-permute-start(bf16[33,16,128]{2,1,0:T(8,128)(2,1)S(1)} %pad_maximum_fusion.1), channel_id=1, source_target_pairs={{0,12},{1,13},{2,14},{3,15},{4,8},{5,9},{6,10},{7,11},{8,4},{9,5},... | collective-permute-start | bytes 405512 | tf_op jit(solution)/shard_map/ppermute | solution.py:484
  9.6 8.6 %collective-permute-start.1 = (bf16[17,16,128]{2,1,0:T(8,128)(2,1)S(1)}, bf16[17,16,128]{2,1,0:T(8,128)(2,1)S(1)}, u32[]{:S(2)}, u32[]{:S(2)}) collective-permute-start(bf16[17,16,128]{2,1,0:T(8,128)(2,1)S(1)} %get-tuple-element.53), channel_id=1, source_target_pairs={{0,8},{1,9},{2,10},{3,11},{4,12},{5,13},{6,14},{7,15},{8,0},{9,1},... | collective-permute-start | bytes 208904 | tf_op jit(solution)/shard_map/ppermute | solution.py:484
  9.6 8.6 %collective-permute-start = (bf16[17,16,128]{2,1,0:T(8,128)(2,1)S(1)}, bf16[17,16,128]{2,1,0:T(8,128)(2,1)S(1)}, u32[]{:S(2)}, u32[]{:S(2)}) collective-permute-start(bf16[17,16,128]{2,1,0:T(8,128)(2,1)S(1)} %get-tuple-element.53), channel_id=1, source_target_pairs={{0,4},{1,5},{2,6},{3,7},{4,0},{5,1},{6,2},{7,3},{8,12},{9,13},{10,... | collective-permute-start | bytes 208904 | tf_op jit(solution)/shard_map/ppermute | solution.py:484
  18.3 44.1 %collective-permute-start.19 = (bf16[16,256,128]{2,1,0:T(8,128)(2,1)}, bf16[16,256,128]{2,1,0:T(8,128)(2,1)S(1)}, u32[]{:S(2)}, u32[]{:S(2)}) collective-permute-start(bf16[16,256,128]{2,1,0:T(8,128)(2,1)} %refs_2_.1), channel_id=1, source_target_pairs={{0,12},{1,13},{2,14},{3,15},{4,8},{5,9},{6,10},{7,11},{8,4},{9,5},... | collective-permute-start | bytes 3145736 | tf_op jit(solution)/shard_map/ppermute | solution.py:484
  40.4 8.4 %collective-permute-start.6 = (bf16[1,32,16,256]{3,2,1,0:T(8,128)(2,1)S(1)}, bf16[1,32,16,256]{3,2,1,0:T(8,128)(2,1)S(1)}, u32[]{:S(2)}, u32[]{:S(2)}) collective-permute-start(bf16[1,32,16,256]{3,2,1,0:T(8,128)(2,1)S(1)} %get-tuple-element.66), channel_id=1, source_target_pairs={{0,2},{1,3},{2,0},{3,1},{4,6},{5,7},{6,4},{7,5},{8,10},{9,11},{10,... | collective-permute-start | bytes 786440 | tf_op jit(solution)/shard_map/ppermute | solution.py:484
  42.0 9.2 %collective-permute-start.8 = (bf16[1,32,16,256]{3,2,1,0:T(8,128)(2,1)S(1)}, bf16[1,32,16,256]{3,2,1,0:T(8,128)(2,1)S(1)}, u32[]{:S(2)}, u32[]{:S(2)}) collective-permute-start(bf16[1,32,16,256]{3,2,1,0:T(8,128)(2,1)S(1)} %get-tuple-element.69), channel_id=1, source_target_pairs={{0,4},{1,5},{2,6},{3,7},{4,0},{5,1},{6,2},{7,3},{8,12},{9,13},{10,... | collective-permute-start | bytes 786440 | tf_op jit(solution)/shard_map/ppermute | solution.py:484
  42.0 15.2 %collective-permute-start.10 = (bf16[1,32,16,256]{3,2,1,0:T(8,128)(2,1)S(1)}, bf16[1,32,16,256]{3,2,1,0:T(8,128)(2,1)S(1)}, u32[]{:S(2)}, u32[]{:S(2)}) collective-permute-start(bf16[1,32,16,256]{3,2,1,0:T(8,128)(2,1)S(1)} %get-tuple-element.72), channel_id=1, source_target_pairs={{0,6},{1,7},{2,4},{3,5},{4,2},{5,3},{6,0},{7,1},{8,14},{9,15},{10,... | collective-permute-start | bytes 786440 | tf_op jit(solution)/shard_map/ppermute | solution.py:484
  48.8 16.8 %collective-permute-start.7 = (bf16[1,32,16,256]{3,2,1,0:T(8,128)(2,1)S(1)}, bf16[1,32,16,256]{3,2,1,0:T(8,128)(2,1)S(1)}, u32[]{:S(2)}, u32[]{:S(2)}) collective-permute-start(bf16[1,32,16,256]{3,2,1,0:T(8,128)(2,1)S(1)} %get-tuple-element.68), channel_id=1, source_target_pairs={{0,2},{1,3},{2,0},{3,1},{4,6},{5,7},{6,4},{7,5},{8,10},{9,11},{10,... | collective-permute-start | bytes 786440 | tf_op jit(solution)/shard_map/ppermute | solution.py:484
  51.1 14.6 %collective-permute-start.9 = (bf16[1,32,16,256]{3,2,1,0:T(8,128)(2,1)S(1)}, bf16[1,32,16,256]{3,2,1,0:T(8,128)(2,1)S(1)}, u32[]{:S(2)}, u32[]{:S(2)}) collective-permute-start(bf16[1,32,16,256]{3,2,1,0:T(8,128)(2,1)S(1)} %get-tuple-element.71), channel_id=1, source_target_pairs={{0,4},{1,5},{2,6},{3,7},{4,0},{5,1},{6,2},{7,3},{8,12},{9,13},{10,... | collective-permute-start | bytes 786440 | tf_op jit(solution)/shard_map/ppermute | solution.py:484
  57.2 10.7 %collective-permute-start.11 = (bf16[1,32,16,256]{3,2,1,0:T(8,128)(2,1)S(1)}, bf16[1,32,16,256]{3,2,1,0:T(8,128)(2,1)S(1)}, u32[]{:S(2)}, u32[]{:S(2)}) collective-permute-start(bf16[1,32,16,256]{3,2,1,0:T(8,128)(2,1)S(1)} %get-tuple-element.74), channel_id=1, source_target_pairs={{0,6},{1,7},{2,4},{3,5},{4,2},{5,3},{6,0},{7,1},{8,14},{9,15},{10,... | collective-permute-start | bytes 786440 | tf_op jit(solution)/shard_map/ppermute | solution.py:484
  62.3 7.3 %collective-permute-start.12 = (bf16[1,32,16,256]{3,2,1,0:T(8,128)(2,1)S(1)}, bf16[1,32,16,256]{3,2,1,0:T(8,128)(2,1)S(1)}, u32[]{:S(2)}, u32[]{:S(2)}) collective-permute-start(bf16[1,32,16,256]{3,2,1,0:T(8,128)(2,1)S(1)} %get-tuple-element.78.refs_4_), channel_id=1, source_target_pairs={{0,1},{1,0},{2,3},{3,2},{4,5},{5,4},{6,7},{7,6},{8,9},{9,8},{10,11... | collective-permute-start | bytes 786440 | tf_op jit(solution)/shard_map/ppermute | solution.py:484
  62.4 7.4 %collective-permute-start.13 = (bf16[1,32,16,256]{3,2,1,0:T(8,128)(2,1)S(1)}, bf16[1,32,16,256]{3,2,1,0:T(8,128)(2,1)S(1)}, u32[]{:S(2)}, u32[]{:S(2)}) collective-permute-start(bf16[1,32,16,256]{3,2,1,0:T(8,128)(2,1)S(1)} %collective-permute-done.6.refs_5_), channel_id=1, source_target_pairs={{0,1},{1,0},{2,3},{3,2},{4,5},{5,4},{6,7},{7,6},{8,9},{9,8},{10,11... | collective-permute-start | bytes 786440 | tf_op jit(solution)/shard_map/ppermute | solution.py:484
  65.7 8.8 %collective-permute-start.20 = (bf16[1,32,16,256]{3,2,1,0:T(8,128)(2,1)S(1)}, bf16[1,32,16,256]{3,2,1,0:T(8,128)(2,1)S(1)}, u32[]{:S(2)}, u32[]{:S(2)}) collective-permute-start(bf16[1,32,16,256]{3,2,1,0:T(8,128)(2,1)S(1)} %get-tuple-element.90), channel_id=1, source_target_pairs={{0,2},{1,3},{2,0},{3,1},{4,6},{5,7},{6,4},{7,5},{8,10},{9,11},{10,... | collective-permute-start | bytes 786440 | tf_op jit(solution)/shard_map/ppermute | solution.py:484
  67.9 9.2 %collective-permute-start.21 = (bf16[1,32,16,256]{3,2,1,0:T(8,128)(2,1)S(1)}, bf16[1,32,16,256]{3,2,1,0:T(8,128)(2,1)S(1)}, u32[]{:S(2)}, u32[]{:S(2)}) collective-permute-start(bf16[1,32,16,256]{3,2,1,0:T(8,128)(2,1)S(1)} %get-tuple-element.92), channel_id=1, source_target_pairs={{0,4},{1,5},{2,6},{3,7},{4,0},{5,1},{6,2},{7,3},{8,12},{9,13},{10,... | collective-permute-start | bytes 786440 | tf_op jit(solution)/shard_map/ppermute | solution.py:484
  69.6 11.9 %collective-permute-start.22 = (bf16[1,32,16,256]{3,2,1,0:T(8,128)(2,1)S(1)}, bf16[1,32,16,256]{3,2,1,0:T(8,128)(2,1)S(1)}, u32[]{:S(2)}, u32[]{:S(2)}) collective-permute-start(bf16[1,32,16,256]{3,2,1,0:T(8,128)(2,1)S(1)} %get-tuple-element.94), channel_id=1, source_target_pairs={{0,6},{1,7},{2,4},{3,5},{4,2},{5,3},{6,0},{7,1},{8,14},{9,15},{10,... | collective-permute-start | bytes 786440 | tf_op jit(solution)/shard_map/ppermute | solution.py:484
  69.9 11.6 %collective-permute-start.15 = (bf16[1,32,16,256]{3,2,1,0:T(8,128)(2,1)S(1)}, bf16[1,32,16,256]{3,2,1,0:T(8,128)(2,1)S(1)}, u32[]{:S(2)}, u32[]{:S(2)}) collective-permute-start(bf16[1,32,16,256]{3,2,1,0:T(8,128)(2,1)S(1)} %collective-permute-done.10.refs_7_), channel_id=1, source_target_pairs={{0,1},{1,0},{2,3},{3,2},{4,5},{5,4},{6,7},{7,6},{8,9},{9,8},{10,11... | collective-permute-start | bytes 786440 | tf_op jit(solution)/shard_map/ppermute | solution.py:484
  69.9 14.2 %collective-permute-start.23 = (bf16[1,32,16,256]{3,2,1,0:T(8,128)(2,1)S(1)}, bf16[1,32,16,256]{3,2,1,0:T(8,128)(2,1)S(1)}, u32[]{:S(2)}, u32[]{:S(2)}) collective-permute-start(bf16[1,32,16,256]{3,2,1,0:T(8,128)(2,1)S(1)} %get-tuple-element.88.refs_4_), channel_id=1, source_target_pairs={{0,1},{1,0},{2,3},{3,2},{4,5},{5,4},{6,7},{7,6},{8,9},{9,8},{10,11... | collective-permute-start | bytes 786440 | tf_op jit(solution)/shard_map/ppermute | solution.py:484
  74.6 11.1 %collective-permute-start.24 = (bf16[1,32,16,256]{3,2,1,0:T(8,128)(2,1)S(1)}, bf16[1,32,16,256]{3,2,1,0:T(8,128)(2,1)S(1)}, u32[]{:S(2)}, u32[]{:S(2)}) collective-permute-start(bf16[1,32,16,256]{3,2,1,0:T(8,128)(2,1)S(1)} %collective-permute-done.20.refs_5_), channel_id=1, source_target_pairs={{0,1},{1,0},{2,3},{3,2},{4,5},{5,4},{6,7},{7,6},{8,9},{9,8},{10,11... | collective-permute-start | bytes 786440 | tf_op jit(solution)/shard_map/ppermute | solution.py:484
  77.0 8.9 %collective-permute-start.25 = (bf16[1,32,16,256]{3,2,1,0:T(8,128)(2,1)S(1)}, bf16[1,32,16,256]{3,2,1,0:T(8,128)(2,1)S(1)}, u32[]{:S(2)}, u32[]{:S(2)}) collective-permute-start(bf16[1,32,16,256]{3,2,1,0:T(8,128)(2,1)S(1)} %collective-permute-done.21.refs_6_), channel_id=1, source_target_pairs={{0,1},{1,0},{2,3},{3,2},{4,5},{5,4},{6,7},{7,6},{8,9},{9,8},{10,11... | collective-permute-start | bytes 786440 | tf_op jit(solution)/shard_map/ppermute | solution.py:484
  82.3 7.7 %collective-permute-start.16 = (bf16[1,32,16,128]{3,2,1,0:T(8,128)(2,1)S(1)}, bf16[1,32,16,128]{3,2,1,0:T(8,128)(2,1)S(1)}, u32[]{:S(2)}, u32[]{:S(2)}) collective-permute-start(bf16[1,32,16,128]{3,2,1,0:T(8,128)(2,1)S(1)} %get-tuple-element.83), channel_id=1, source_target_pairs={{0,2},{1,3},{2,0},{3,1},{4,6},{5,7},{6,4},{7,5},{8,10},{9,11},{10,... | collective-permute-start | bytes 393224 | tf_op jit(solution)/shard_map/ppermute | solution.py:484
  85.6 7.3 %collective-permute-start.18 = (bf16[1,32,16,128]{3,2,1,0:T(8,128)(2,1)S(1)}, bf16[1,32,16,128]{3,2,1,0:T(8,128)(2,1)S(1)}, u32[]{:S(2)}, u32[]{:S(2)}) collective-permute-start(bf16[1,32,16,128]{3,2,1,0:T(8,128)(2,1)S(1)} %get-tuple-element.85), channel_id=1, source_target_pairs={{0,6},{1,7},{2,4},{3,5},{4,2},{5,3},{6,0},{7,1},{8,14},{9,15},{10,... | collective-permute-start | bytes 393224 | tf_op jit(solution)/shard_map/ppermute | solution.py:484
  86.7 8.2 %collective-permute-start.27 = (bf16[1,32,16,128]{3,2,1,0:T(8,128)(2,1)S(1)}, bf16[1,32,16,128]{3,2,1,0:T(8,128)(2,1)S(1)}, u32[]{:S(2)}, u32[]{:S(2)}) collective-permute-start(bf16[1,32,16,128]{3,2,1,0:T(8,128)(2,1)S(1)} %get-tuple-element.96), channel_id=1, source_target_pairs={{0,2},{1,3},{2,0},{3,1},{4,6},{5,7},{6,4},{7,5},{8,10},{9,11},{10,... | collective-permute-start | bytes 393224 | tf_op jit(solution)/shard_map/ppermute | solution.py:484
  88.4 7.6 %collective-permute-start.28 = (bf16[1,32,16,128]{3,2,1,0:T(8,128)(2,1)S(1)}, bf16[1,32,16,128]{3,2,1,0:T(8,128)(2,1)S(1)}, u32[]{:S(2)}, u32[]{:S(2)}) collective-permute-start(bf16[1,32,16,128]{3,2,1,0:T(8,128)(2,1)S(1)} %get-tuple-element.97), channel_id=1, source_target_pairs={{0,4},{1,5},{2,6},{3,7},{4,0},{5,1},{6,2},{7,3},{8,12},{9,13},{10,... | collective-permute-start | bytes 393224 | tf_op jit(solution)/shard_map/ppermute | solution.py:484
  90.0 8.0 %collective-permute-start.29 = (bf16[1,32,16,128]{3,2,1,0:T(8,128)(2,1)S(1)}, bf16[1,32,16,128]{3,2,1,0:T(8,128)(2,1)S(1)}, u32[]{:S(2)}, u32[]{:S(2)}) collective-permute-start(bf16[1,32,16,128]{3,2,1,0:T(8,128)(2,1)S(1)} %get-tuple-element.98), channel_id=1, source_target_pairs={{0,6},{1,7},{2,4},{3,5},{4,2},{5,3},{6,0},{7,1},{8,14},{9,15},{10,... | collective-permute-start | bytes 393224 | tf_op jit(solution)/shard_map/ppermute | solution.py:484
  (16 other events, 66.2 us)

commit v4 on v3

--- a/solution.py
+++ b/solution.py
@@ -130,14 +130,17 @@
             pltpu.VMEM((rows * proj // 2, 2 * seqs), F32),
             pltpu.VMEM((rows, proj, seqs), F32),
         ],
-        12,
+        58,
         flops=4 * seqs * rows * breadth * proj,
         data=2 * seqs * rows * breadth,
         windows=True,
     )
 
 
-def weights_kernel(out_ref, in_ref, gate_ref, final_ref, out_t, in_t, gate_t, final_t, rows):
+def weights_kernel(
+    mirror, out_ref, in_ref, gate_ref, final_ref, obs_ref, seen_ref, *refs
+):
+    out_t, in_t, gate_t, final_t, own_ref, far_ref, rows = refs
     one = identity(LANES)
 
     def turned(value):
@@ -153,21 +156,29 @@
         in_t[cols] = turned(in_ref[:, cols])
     gate_t[...] = turned(gate_ref[...])
     final_t[...] = turned(final_ref[...])
-
-
-def weights_stage(w_out, w_in, w_gate, w_final):
+    me = lax.axis_index("row")
+    seen = seen_ref[...].astype(F32)
+    for device, ref in ((me, own_ref), (mirror(me), far_ref)):
+        for i in range(ref.shape[0]):
+            ref[i : i + 1] = seen * obs_ref[device * ref.shape[0] + i].astype(F32)
+
+
+def weights_stage(mirror, w_out, w_in, w_gate, w_final, obs, rows):
     depth, width = w_out.shape
     shapes = [w_out.shape[::-1], w_in.shape[::-1], w_gate.shape[::-1], w_final.shape[::-1]]
     return local_call(
         "weights_stage",
-        weights_kernel,
+        lambda *refs: weights_kernel(mirror, *refs),
         1,
-        [fixed(w_out), fixed(w_in), fixed(w_gate), fixed(w_final)],
-        [(shape, BF16, None, None) for shape in shapes],
+        [fixed(w_out), fixed(w_in), fixed(w_gate), fixed(w_final), scalars(obs)]
+        + [fixed(obs[None])],
+        [(shape, BF16, None, None) for shape in shapes]
+        + [((rows,) + obs.shape, F32, None, None)] * 2,
         [pltpu.VMEM((depth, width), F32)],
-        8,
+        58,
         flops=2 * LANES * LANES * LANES * 6,
         data=4 * depth * width,
+        windows=True,
     )
 
 
@@ -200,16 +211,15 @@
     ).astype(BF16)
     half = rows * proj
 
-    @pl.loop(0, slices - 1, unroll=4)
-    def _(t):
+    for t in range(slices - 1):
         both = lax.dot_general(
             both_left,
-            right[:, pl.ds(t, 1)].reshape(block, LANES),
+            right[:, t].reshape(block, LANES),
             NT,
             preferred_element_type=F32,
         ).astype(BF16)
         for e in range(2):
-            outer[:, pl.ds(pl.multiple_of((2 * t + e) * proj, proj), proj), :] = both[
+            outer[:, (2 * t + e) * proj : (2 * t + e + 1) * proj, :] = both[
                 e * half : (e + 1) * half
             ].reshape(rows, proj, block)
 
@@ -221,10 +231,6 @@
 
 def chip_here(split):
     return jnp.int32(0) if split == 1 else (lax.axis_index("row") // 2) & (split - 1)
-
-
-def observed(device, obs_ref, seen_ref, rows, i):
-    return seen_ref[...].astype(F32) * obs_ref[device * rows + i].astype(F32)
 
 
 def keep_sides(i, norm, w_in_ref, seen, sides_of, hidden):
@@ -256,10 +262,9 @@
 
 
 def pair_kernel(pieces, split, *refs):
-    left_ref, mask_ref, couple_ref, w_out_ref, w_in_ref, w_gate_ref, obs_ref, seen_ref = refs[:8]
-    right_refs, refs = refs[8 : 8 + pieces], refs[8 + pieces :]
-    pair_ref, gate_ref = refs[:2]
-    a_refs, b_refs, refs = refs[2 : 2 + split], refs[2 + split : 2 + 2 * split], refs[2 + 2 * split :]
+    left_ref, mask_ref, couple_ref, w_out_ref, w_in_ref, seen_ref = refs[:6]
+    right_refs, (pair_ref, *refs) = refs[6 : 6 + pieces], refs[6 + pieces :]
+    a_refs, b_refs, refs = refs[:split], refs[split : 2 * split], refs[2 * split :]
     if pieces > 1:
         right, refs = refs[0], refs[1:]
         order_right(right_refs, right)
@@ -273,9 +278,7 @@
         pair = couple_ref[i].astype(F32).T + row_update(i, w_out_ref, outer, scale)
         norm = standardize(pair, 0).astype(BF16)
         pair_ref[i] = pair
-        gate_ref[i] = sigmoid(jnp.dot(w_gate_ref[...], norm, preferred_element_type=F32))
-        seen = observed(lax.axis_index("row"), obs_ref, seen_ref, rows, i)
-        keep_sides(i, norm, w_in_ref, seen, (kept_a, kept_b), hidden)
+        keep_sides(i, norm, w_in_ref, seen_ref[i : i + 1], (kept_a, kept_b), hidden)
     write_sides(kept_b, b_refs, rows, hidden)
     write_sides(kept_a, a_refs, rows, hidden)
 
@@ -291,16 +294,14 @@
         update_ref[i] = row_update(i, w_out_ref, outer, scale)
 
 
-def mirror_kernel(mirror, update_ref, couple_ref, w_in_ref, obs_ref, seen_ref, *refs):
+def mirror_kernel(update_ref, couple_ref, w_in_ref, seen_ref, *refs):
     outs, kept = refs[:-1], refs[-1]
     rows = couple_ref.shape[0]
     hidden = w_in_ref.shape[0] // 4
     for i in range(rows):
         pair = couple_ref[i].astype(F32).T + update_ref[i]
-        device = mirror(lax.axis_index("row"))
-        seen = observed(device, obs_ref, seen_ref, rows, i)
         norm = standardize(pair, 0).astype(BF16)
-        keep_sides(i, norm, w_in_ref.at[2 * hidden :], seen, (kept,), hidden)
+        keep_sides(i, norm, w_in_ref.at[2 * hidden :], seen_ref[i : i + 1], (kept,), hidden)
     write_sides(kept, outs, rows, hidden)
 
 
@@ -320,11 +321,11 @@
     return value, None, None
 
 
-def pair_stage(left, right, mask, couple, w_out, w_in, w_gate, obs, parts, split):
+def pair_stage(left, right, mask, couple, w_out, w_in, seen, parts, split):
     rows, total, width = couple.shape
     hidden = w_in.shape[0] // 4
     piece = (parts // split, hidden // parts, rows, total)
-    outs = [last_out((rows, width, total), F32, BLOCK)] * 2
+    outs = [last_out((rows, width, total), F32, BLOCK)]
     outs += [last_out(piece, BF16, BLOCK)] * (2 * split)
     if len(right) > 1:
         outs += [((total // rows,) + right[0].shape[1:], BF16, None, None)]
@@ -333,7 +334,7 @@
         lambda *refs: pair_kernel(len(right), split, *refs),
         total // BLOCK,
         [fixed(left), fixed(mask), couple_input(couple), fixed(w_out), fixed(w_in)]
-        + [fixed(w_gate), scalars(obs), last(obs[None], BLOCK)]
+        + [last(seen, BLOCK)]
         + [right_input(value, total) for value in right],
         outs,
         [pltpu.VMEM((rows, w_out.shape[1], BLOCK), BF16)]
@@ -342,8 +343,30 @@
         24,
         flops=4 * rows * total * w_out.shape[1] * width,
         data=16 * rows * total * width,
-        special=3 * rows * total * hidden,
-    )
+        special=2 * rows * total * hidden,
+    )
+
+
+def gate_kernel(pair_ref, w_gate_ref, gate_ref):
+    for i in range(pair_ref.shape[0]):
+        norm = standardize(pair_ref[i], 0).astype(BF16)
+        gate_ref[i] = sigmoid(jnp.dot(w_gate_ref[...], norm, preferred_element_type=F32))
+
+
+def gate_stage(pair, w_gate):
+    rows, width, total = pair.shape
+    return local_call(
+        "gate_stage",
+        gate_kernel,
+        total // BLOCK,
+        [last(pair, BLOCK), fixed(w_gate)],
+        [last_out(pair.shape, F32, BLOCK)],
+        [],
+        16,
+        flops=2 * rows * total * width * width,
+        data=8 * rows * total * width,
+        special=rows * total * width,
+    )[0]
 
 
 def update_stage(left, right, mask, w_out, rows, total):
@@ -362,15 +385,14 @@
     )[0]
 
 
-def mirror_stage(mirror, update, couple, w_in, obs, parts, split):
+def mirror_stage(update, couple, w_in, seen, parts, split):
     rows, total, width = couple.shape
     hidden = w_in.shape[0] // 4
     return local_call(
         "mirror_stage",
-        lambda *refs: mirror_kernel(mirror, *refs),
+        mirror_kernel,
         total // BLOCK,
-        [last(update, BLOCK), couple_input(couple), fixed(w_in), scalars(obs)]
-        + [last(obs[None], BLOCK)],
+        [last(update, BLOCK), couple_input(couple), fixed(w_in), last(seen, BLOCK)],
         [last_out((parts // split, hidden // parts, rows, total), BF16, BLOCK)] * split,
         [kept_scratch(rows, hidden, BLOCK)],
         16,
@@ -425,52 +447,88 @@
     )
 
 
-def final_kernel(spans, split, pair_ref, gate_ref, w_ref, *refs):
-    out_ref, normed = refs[-2:]
-    rows, _, whole = pair_ref.shape
-    per, chans, _, block = refs[0].shape
-    parts = per * split
+def final_rows(tri, low, pair_ref, gate_ref, w_ref, normed, write):
+    rows = pair_ref.shape[0]
+    per, chans, _, block = tri[0].shape
+    parts = per * len(tri)
     hidden = chans * parts
     tiles = block // LANES
-    chip = chip_here(split)
-    for span in range(spans):
-        tri = refs[span * split : (span + 1) * split]
-        if spans == 1:
-            low = 0
-        else:
-            devs = lax.axis_size("row")
-            mine = lax.div(lax.axis_index("row"), devs // 2)
-            low = pl.multiple_of((mine ^ span) * block, block)
-        values = standardize(
-            jnp.concatenate([ref[slot] for ref in tri for slot in range(per)]).astype(F32), 0
-        )
-        for part in range(parts):
-            first = pl.multiple_of((chip ^ part) * (chans * rows), chans * rows)
-            for tile in range(tiles):
-                normed[tile, pl.ds(first, chans * rows), :] = values[
-                    part * chans : (part + 1) * chans, :, tile * LANES : (tile + 1) * LANES
-                ].reshape(chans * rows, LANES)
-        for i in range(rows):
-            columns = jnp.concatenate(
-                [normed[tile, pl.ds(i, hidden, stride=rows), :] for tile in range(tiles)], axis=1
-            ).astype(BF16)
-            update = jnp.dot(w_ref[...], columns, preferred_element_type=F32)
-            cols = pl.ds(low, block)
-            result = pair_ref[i, :, cols] + gate_ref[i, :, cols] * update
-            out_ref[i, cols, :] = result.T.astype(BF16)
-
-
-def final_stage(spans, pair, gate, weight):
+    chip = chip_here(len(tri))
+    values = standardize(
+        jnp.concatenate([ref[slot] for ref in tri for slot in range(per)]).astype(F32), 0
+    )
+    for part in range(parts):
+        first = pl.multiple_of((chip ^ part) * (chans * rows), chans * rows)
+        for tile in range(tiles):
+            normed[tile, pl.ds(first, chans * rows), :] = values[
+                part * chans : (part + 1) * chans, :, tile * LANES : (tile + 1) * LANES
+            ].reshape(chans * rows, LANES)
+    for i in range(rows):
+        columns = jnp.concatenate(
+            [normed[tile, pl.ds(i, hidden, stride=rows), :] for tile in range(tiles)], axis=1
+        ).astype(BF16)
+        update = jnp.dot(w_ref[...], columns, preferred_element_type=F32)
+        cols = pl.ds(low, block)
+        result = pair_ref[i, :, cols] + gate_ref[i, :, cols] * update
+        write(i, result.T.astype(BF16))
+
+
+def half_start(far, block):
+    mine = lax.div(lax.axis_index("row"), lax.axis_size("row") // 2)
+    return pl.multiple_of((mine ^ far) * block, block)
+
+
+def near_kernel(pair_ref, gate_ref, w_ref, *refs):
+    tri, (out_ref, normed) = refs[:-2], refs[-2:]
+
+    def write(i, result):
+        out_ref[i] = result
+
+    low = half_start(0, tri[0].shape[-1])
+    final_rows(tri, low, pair_ref, gate_ref, w_ref, normed, write)
+
+
+def near_stage(tri, pair, gate, weight):
+    rows, width, _ = pair.shape
+    hidden, block = weight.shape[1], tri[0].shape[-1]
+    return local_call(
+        "near_stage",
+        near_kernel,
+        1,
+        [fixed(pair), fixed(gate), fixed(weight)] + [fixed(value) for value in tri],
+        [((rows, block, width), BF16, None, None)],
+        [pltpu.VMEM((block // LANES, hidden * rows, LANES), F32)],
+        16,
+        flops=2 * rows * block * hidden * width,
+        data=12 * rows * block * width,
+    )[0]
+
+
+def final_kernel(split, pair_ref, gate_ref, w_ref, *refs):
+    out_ref, normed = refs[-2:]
+    tri, near = refs[:split], refs[split:-2]
+    block = tri[0].shape[-1]
+    low = half_start(1, block) if near else 0
+
+    def write(i, result):
+        out_ref[i, pl.ds(low, block), :] = result
+        if near:
+            out_ref[i, pl.ds(half_start(0, block), block), :] = near[0][i]
+
+    final_rows(tri, low, pair_ref, gate_ref, w_ref, normed, write)
+
+
+def final_stage(tri, near, pair, gate, weight):
     rows, width, total = pair.shape
-    hidden = weight.shape[1]
-    split = len(spans[0])
-    block = spans[0][0].shape[-1] if len(spans) > 1 else BLOCK
+    hidden, split = weight.shape[1], len(tri)
+    block = BLOCK if near is None else tri[0].shape[-1]
     return local_call(
         "final_stage",
-        lambda *refs: final_kernel(len(spans), split, *refs),
+        lambda *refs: final_kernel(split, *refs),
         total // BLOCK,
         [last(pair, BLOCK), last(gate, BLOCK), fixed(weight)]
-        + [last(value, block) for span in spans for value in span],
+        + [last(value, block) for value in tri]
+        + ([] if near is None else [fixed(near)]),
         [((rows, total, width), BF16, (rows, BLOCK, width), lambda j: (0, j, 0))],
         [pltpu.VMEM((block // LANES, hidden * rows, LANES), F32)],
         24,
@@ -532,7 +590,6 @@
     cores = 2 if hops else 1
     parts = half // cores
     split = parts if hops else 1
-    obs = observed_indicator
 
     def mirror(device):
         return device ^ 12 if hops else (device + half) % devs
@@ -547,10 +604,13 @@
         second_factor_matrix.T,
     )
     weights = weights_stage(
+        mirror,
         product_final_matrix,
         edge_projection_matrix,
         sigmoid_filter_matrix,
         multiplicative_final_matrix,
+        observed_indicator,
+        rows,
     )
     if hops:
         slices = block.shape[0]
@@ -567,38 +627,39 @@
         far_left = mirrored(left)
         far_couple = mirrored(couple_features)
         far_mask = right[0][mirror(me), -1]
-    w_out, w_in, w_gate, w_final = weights
-
-    pair, gate, *sides = pair_stage(
-        left, right, block[-1], couple_features, w_out, w_in, w_gate, obs, parts, split
+    w_out, w_in, w_gate, w_final, seen, far_seen = weights
+
+    pair, *sides = pair_stage(
+        left, right, block[-1], couple_features, w_out, w_in, seen, parts, split
     )
     a, b = list(sides[:split]), list(sides[split : 2 * split])
     ordered = sides[2 * split] if hops else right[0]
     b = exchange(b)
-    a = exchange(a, b)
     if hops:
         _, far_left = after(b[1], far_left)
     update = update_stage(far_left, ordered, far_mask, w_out, rows, total)
     if hops:
-        update, b = after(update, b)
+        update, a[2] = after(update, a[2])
+    a = exchange(a, b)
     near = tri_stage(a, with_other_core(b), cores, 0)
-    far_b = mirror_stage(mirror, update, far_couple, w_in, obs, parts, split)
-    far_b = with_other_core(exchange(far_b, a))
+    far_b = mirror_stage(update, far_couple, w_in, far_seen, parts, split)
+    far_b = exchange(far_b, a)
+    if hops:
+        near, pair = after(near, pair)
+    gate = gate_stage(pair, w_gate)
+    if hops:
+        (near, gate), far_b = after((near, gate), far_b)
     near = exchange(near)
-    far = exchange(tri_stage(a, far_b, cores, 2 if hops else 0))
+    far = exchange(tri_stage(a, with_other_core(far_b), cores, 2 if hops else 0))
     if hops:
-        spans = [near, far]
-    else:
-        lower = me < half
-        spans = [
-            [
-                jnp.concatenate(
-                    [jnp.where(lower, x, y), jnp.where(lower, y, x)], axis=-1
-                )
-                for x, y in zip(near, far)
-            ]
-        ]
-    return final_stage(spans, pair, gate, w_final)
+        done = near_stage(near, pair, gate, w_final)
+        return final_stage(far, done, pair, gate, w_final)
+    lower = me < half
+    tri = [
+        jnp.concatenate([jnp.where(lower, x, y), jnp.where(lower, y, x)], axis=-1)
+        for x, y in zip(near, far)
+    ]
+    return final_stage(tri, None, pair, gate, w_final)
 
 
 def solution(mesh):

time: 101 us -> 98.6 us (0.976)
  local copies, waits for them, and re-layouts: 7.32 us -> 0.02 us
  waiting for transfers between devices: 41 us -> 45 us
  starting transfers between devices: 28.4 us -> 32.2 us
  Pallas kernels: 23.9 us -> 21.1 us
    unnamed x20 -> x2, local copies, waits for them, and re-layouts: 7.31 us -> 0.01 us
    ppermute x30, waiting for transfers between devices: 41 us -> 45 us  [send(): return lax.ppermute(value, 'row', [(i, move(i)) for i in range(devs)])]
    ppermute x30, starting transfers between devices: 28.4 us -> 32.2 us  [send(): return lax.ppermute(value, 'row', [(i, move(i)) for i in range(devs)])]
    pallas_call x8 -> x10, Pallas kernels: 23.9 us -> 21.1 us  [local_call(): pl.pallas_call(kernel, grid=() if whole else (steps,), in_specs=in_specs,...]
  transfers between devices with their start and end apart: 30 -> 30, of which waited for: 14 -> 17; matrix products, arithmetic and copies ran while one was open for 0% -> 0% of each run, Pallas kernels for 20% -> 17%
where the time goes in v4:
time: 98.6 us; the launch traced here: 98.5 us
  waiting for transfers between devices  45 us (46%)
  starting transfers between devices  32.2 us (33%)
  Pallas kernels  21.1 us (21%)
    ppermute x30, waiting for transfers between devices, send(): return lax.ppermute(value, 'row', [(i, move(i)) for i in range(devs)])  45 us
    ppermute x30, starting transfers between devices, send(): return lax.ppermute(value, 'row', [(i, move(i)) for i in range(devs)])  32.2 us
    pallas_call x10, Pallas kernels, local_call(): pl.pallas_call(kernel, grid=() if whole else (steps,), in_specs=in_specs,...  21.1 us
  transfers between devices with their start and end apart: 30, of which 17 were waited for; matrix products, arithmetic and copies ran while one was open for 0% of the time, Pallas kernels for 17%

profile of v4, /device:TPU:0, one launch (start us, length us, event | category | flops | bytes accessed | tf_op | source)
XLA Modules:
  0.0 98.5 jit_solution(12209141441248089211)
XLA Ops:
  0.0 2.3 %msa_stage.1 = (bf16[17,16,128]{2,1,0:T(8,128)(2,1)S(1)}, bf16[256,128]{1,0:T(8,128)(2,1)S(1)}) custom-call(bf16[64,16,256]{2,1,0:T(8,128)(2,1)} %msa_ref.1, s32[16,64]{1,0:T(8,128)} %bitcast.20, bf16[32,256]{1,0:T(8,128)(2,1)} %bitcast.18, bf16[32,256]{1,0:T(8,128)(2,1)} %bitcast.19), custom_call_target="tpu_custom_call" | custom-call | flops 33554 | bytes 524 | tf_op jit(solution)/shard_map/msa_stage/pallas_call | solution.py:49
  2.4 5.1 %collective-permute-start.2 = (bf16[33,16,128]{2,1,0:T(8,128)(2,1)S(1)}, bf16[33,16,128]{2,1,0:T(8,128)(2,1)S(1)}, u32[]{:S(2)}, u32[]{:S(2)}) collective-permute-start(bf16[33,16,128]{2,1,0:T(8,128)(2,1)S(1)} %pad_maximum_fusion.1), channel_id=1, source_target_pairs={{0,12},{1,13},{2,14},{3,15},{4,8},{5,9},{6,10},{7,11},{8,4},{9,5},... | collective-permute-start | bytes 405512 | tf_op jit(solution)/shard_map/ppermute | solution.py:542
  8.1 1.7 %weights_stage.1 = (bf16[128,1024]{1,0:T(8,128)(2,1)S(1)}, bf16[512,128]{1,0:T(8,128)(2,1)S(1)}, bf16[128,128]{1,0:T(8,128)(2,1)S(1)}, bf16[128,128]{1,0:T(8,128...) custom-call(bf16[1024,128]{1,0:T(8,128)(2,1)} %refs_0_.1, bf16[128,512]{1,0:T(8,128)(2,1)} %refs_1_.1, ...), custom_call_target="tpu_custom_call" | custom-call | flops 25165 | bytes 524 | tf_op jit(solution)/shard_map/weights_stage/pallas_call | solution.py:49
  9.8 2.2 %collective-permute-done.2 = bf16[33,16,128]{2,1,0:T(8,128)(2,1)S(1)} collective-permute-done((bf16[33,16,128]{2,1,0:T(8,128)(2,1)S(1)}, bf16[33,16,128]{2,1,0:T(8,128)(2,1)S(1)}, u32[]{:S(2)}, u32[]{:S(2)}) %collective-permute-start.2) | collective-permute-done | bytes 135200 | tf_op jit(solution)/shard_map/ppermute | solution.py:542
  12.7 3.4 %collective-permute-done.1 = bf16[17,16,128]{2,1,0:T(8,128)(2,1)S(1)} collective-permute-done((bf16[17,16,128]{2,1,0:T(8,128)(2,1)S(1)}, bf16[17,16,128]{2,1,0:T(8,128)(2,1)S(1)}, u32[]{:S(2)}, u32[]{:S(2)}) %collective-permute-start.1) | collective-permute-done | bytes 69664 | tf_op jit(solution)/shard_map/ppermute | solution.py:542
  16.1 2.5 %collective-permute-start.16 = (bf16[16,256,128]{2,1,0:T(8,128)(2,1)}, bf16[16,256,128]{2,1,0:T(8,128)(2,1)S(1)}, u32[]{:S(2)}, u32[]{:S(2)}) collective-permute-start(bf16[16,256,128]{2,1,0:T(8,128)(2,1)} %refs_2_.3), channel_id=1, source_target_pairs={{0,12},{1,13},{2,14},{3,15},{4,8},{5,9},{6,10},{7,11},{8,4},{9,5},... | collective-permute-start | bytes 3145736 | tf_op jit(solution)/shard_map/ppermute | solution.py:542
  20.2 5.7 %collective-permute-done.3.refs_7_ = bf16[4,17,16,128]{3,2,1,0:T(8,128)(2,1)S(1)} collective-permute-done((bf16[4,17,16,128]{3,2,1,0:T(8,128)(2,1)S(1)}, bf16[4,17,16,128]{3,2,1,0:T(8,128)(2,1)S(1)}, u32[]{:S(2)}, u32[]{:S(2)}) %collective-permute-start.3) | collective-permute-done | bytes 278560 | tf_op jit(solution)/shard_map/ppermute | solution.py:542
  27.5 6.2 %pair_stage.1 = (f32[16,128,256]{2,1,0:T(8,128)S(1)}, bf16[1,32,16,256]{3,2,1,0:T(8,128)(2,1)S(1)}, bf16[1,32,16,256]{3,2,1,0:T(8,128)(2,1)S(1)}, bf16[1,32,16,2...) custom-call(bf16[256,128]{1,0:T(8,128)(2,1)S(1)} %get-tuple-element., ...), custom_call_target="tpu_custom_call" | custom-call | flops 2147483 | bytes 8388 | tf_op jit(solution)/shard_map/pair_stage/pallas_call | solution.py:49
  35.2 2.0 %collective-permute-start.8 = (bf16[1,32,16,256]{3,2,1,0:T(8,128)(2,1)S(1)}, bf16[1,32,16,256]{3,2,1,0:T(8,128)(2,1)S(1)}, u32[]{:S(2)}, u32[]{:S(2)}) collective-permute-start(bf16[1,32,16,256]{3,2,1,0:T(8,128)(2,1)S(1)} %get-tuple-element.82), channel_id=1, source_target_pairs={{0,4},{1,5},{2,6},{3,7},{4,0},{5,1},{6,2},{7,3},{8,12},{9,13},{10,... | collective-permute-start | bytes 786440 | tf_op jit(solution)/shard_map/ppermute | solution.py:542
  37.2 5.8 %collective-permute-done.6.refs_5_ = bf16[1,32,16,256]{3,2,1,0:T(8,128)(2,1)S(1)} collective-permute-done((bf16[1,32,16,256]{3,2,1,0:T(8,128)(2,1)S(1)}, bf16[1,32,16,256]{3,2,1,0:T(8,128)(2,1)S(1)}, u32[]{:S(2)}, u32[]{:S(2)}) %collective-permute-start.6) | collective-permute-done | bytes 262176 | tf_op jit(solution)/shard_map/ppermute | solution.py:542
  43.0 3.5 %update_stage.1.update_ref = f32[16,128,256]{2,1,0:T(8,128)S(1)} custom-call(bf16[256,128]{1,0:T(8,128)(2,1)S(1)} %bitcast.14, bf16[128,1024]{1,0:T(8,128)(2,1)S(1)} %get-tuple-element.74.refs_3_.w_out_ref, bf16[16,17,16,128]{3,2,1,0:T(8,128)(2,1)S(1)} %get-tuple-element.84.right), custom_call_target="tpu_custom_call" | custom-call | flops 2147483 | bytes 4194 | tf_op jit(solution)/shard_map/update_stage/pallas_call | solution.py:49
  46.5 2.4 %collective-permute-done.10.refs_7_ = bf16[1,32,16,256]{3,2,1,0:T(8,128)(2,1)S(1)} collective-permute-done((bf16[1,32,16,256]{3,2,1,0:T(8,128)(2,1)S(1)}, bf16[1,32,16,256]{3,2,1,0:T(8,128)(2,1)S(1)}, u32[]{:S(2)}, u32[]{:S(2)}) %collective-permute-start.10) | collective-permute-done | bytes 262176 | tf_op jit(solution)/shard_map/ppermute | solution.py:542
  48.9 2.6 %collective-permute-start.11 = (bf16[1,32,16,256]{3,2,1,0:T(8,128)(2,1)S(1)}, bf16[1,32,16,256]{3,2,1,0:T(8,128)(2,1)S(1)}, u32[]{:S(2)}, u32[]{:S(2)}) collective-permute-start(bf16[1,32,16,256]{3,2,1,0:T(8,128)(2,1)S(1)} %get-tuple-element.90), channel_id=1, source_target_pairs={{0,6},{1,7},{2,4},{3,5},{4,2},{5,3},{6,0},{7,1},{8,14},{9,15},{10,... | collective-permute-start | bytes 786440 | tf_op jit(solution)/shard_map/ppermute | solution.py:542
  51.6 2.2 %collective-permute-done.8.refs_6_ = bf16[1,32,16,256]{3,2,1,0:T(8,128)(2,1)S(1)} collective-permute-done((bf16[1,32,16,256]{3,2,1,0:T(8,128)(2,1)S(1)}, bf16[1,32,16,256]{3,2,1,0:T(8,128)(2,1)S(1)}, u32[]{:S(2)}, u32[]{:S(2)}) %collective-permute-start.8) | collective-permute-done | bytes 262176 | tf_op jit(solution)/shard_map/ppermute | solution.py:542
  53.8 2.5 %collective-permute-start.9 = (bf16[1,32,16,256]{3,2,1,0:T(8,128)(2,1)S(1)}, bf16[1,32,16,256]{3,2,1,0:T(8,128)(2,1)S(1)}, u32[]{:S(2)}, u32[]{:S(2)}) collective-permute-start(bf16[1,32,16,256]{3,2,1,0:T(8,128)(2,1)S(1)} %get-tuple-element.87), channel_id=1, source_target_pairs={{0,4},{1,5},{2,6},{3,7},{4,0},{5,1},{6,2},{7,3},{8,12},{9,13},{10,... | collective-permute-start | bytes 786440 | tf_op jit(solution)/shard_map/ppermute | solution.py:542
  58.3 1.9 %mirror_stage.1 = (bf16[1,32,16,256]{3,2,1,0:T(8,128)(2,1)S(1)}, bf16[1,32,16,256]{3,2,1,0:T(8,128)(2,1)S(1)}, bf16[1,32,16,256]{3,2,1,0:T(8,128)(2,1)S(1)}, bf16[1,32,16,256]{3,2,1,0:T(8,128)(2,1)S(1)}) custom-call(f32[16,128,256]{2,1,0:T(8,128)S(1)} %update_stage.1.update_ref, bf16[16,256,128]{2,1,0:T(8,128)(2,1)S(1)} %collective-permute-done.16.couple_ref, ...), custom_call_target="tpu_custom_call" | custom-call | flops 268435 | bytes 20971520 | tf_op jit(solution)/shard_map/mirror_stage/pallas_call | solution.py:49
  60.3 4.4 %collective-permute-done.9.refs_2_ = bf16[1,32,16,256]{3,2,1,0:T(8,128)(2,1)S(1)} collective-permute-done((bf16[1,32,16,256]{3,2,1,0:T(8,128)(2,1)S(1)}, bf16[1,32,16,256]{3,2,1,0:T(8,128)(2,1)S(1)}, u32[]{:S(2)}, u32[]{:S(2)}) %collective-permute-start.9) | collective-permute-done | bytes 262176 | tf_op jit(solution)/shard_map/ppermute | solution.py:542
  70.9 4.8 %collective-permute-done.19.refs_7_ = bf16[1,32,16,256]{3,2,1,0:T(8,128)(2,1)S(1)} collective-permute-done((bf16[1,32,16,256]{3,2,1,0:T(8,128)(2,1)S(1)}, bf16[1,32,16,256]{3,2,1,0:T(8,128)(2,1)S(1)}, u32[]{:S(2)}, u32[]{:S(2)}) %collective-permute-start.19) | collective-permute-done | bytes 262176 | tf_op jit(solution)/shard_map/ppermute | solution.py:542
  75.8 4.3 %collective-permute-done.18.refs_6_ = bf16[1,32,16,256]{3,2,1,0:T(8,128)(2,1)S(1)} collective-permute-done((bf16[1,32,16,256]{3,2,1,0:T(8,128)(2,1)S(1)}, bf16[1,32,16,256]{3,2,1,0:T(8,128)(2,1)S(1)}, u32[]{:S(2)}, u32[]{:S(2)}) %collective-permute-start.18) | collective-permute-done | bytes 262176 | tf_op jit(solution)/shard_map/ppermute | solution.py:542
  83.2 1.7 %collective-permute-start.29 = (bf16[1,32,16,128]{3,2,1,0:T(8,128)(2,1)S(1)}, bf16[1,32,16,128]{3,2,1,0:T(8,128)(2,1)S(1)}, u32[]{:S(2)}, u32[]{:S(2)}) collective-permute-start(bf16[1,32,16,128]{3,2,1,0:T(8,128)(2,1)S(1)} %get-tuple-element.126), channel_id=1, source_target_pairs={{0,6},{1,7},{2,4},{3,5},{4,2},{5,3},{6,0},{7,1},{8,14},{9,15},{10,... | collective-permute-start | bytes 393224 | tf_op jit(solution)/shard_map/ppermute | solution.py:542
  87.6 1.7 %collective-permute-start.26 = (bf16[1,32,16,128]{3,2,1,0:T(8,128)(2,1)S(1)}, bf16[1,32,16,128]{3,2,1,0:T(8,128)(2,1)S(1)}, u32[]{:S(2)}, u32[]{:S(2)}) collective-permute-start(bf16[1,32,16,128]{3,2,1,0:T(8,128)(2,1)S(1)} %get-tuple-element.122), channel_id=1, source_target_pairs={{0,6},{1,7},{2,4},{3,5},{4,2},{5,3},{6,0},{7,1},{8,14},{9,15},{10,... | collective-permute-start | bytes 393224 | tf_op jit(solution)/shard_map/ppermute | solution.py:542
  89.3 2.8 %collective-permute-done.29.refs_3_ = bf16[1,32,16,128]{3,2,1,0:T(8,128)(2,1)S(1)} collective-permute-done((bf16[1,32,16,128]{3,2,1,0:T(8,128)(2,1)S(1)}, bf16[1,32,16,128]{3,2,1,0:T(8,128)(2,1)S(1)}, u32[]{:S(2)}, u32[]{:S(2)}) %collective-permute-start.29) | collective-permute-done | bytes 131104 | tf_op jit(solution)/shard_map/ppermute | solution.py:542
  94.6 1.9 %collective-permute-done.26.refs_6_ = bf16[1,32,16,128]{3,2,1,0:T(8,128)(2,1)S(1)} collective-permute-done((bf16[1,32,16,128]{3,2,1,0:T(8,128)(2,1)S(1)}, bf16[1,32,16,128]{3,2,1,0:T(8,128)(2,1)S(1)}, u32[]{:S(2)}, u32[]{:S(2)}) %collective-permute-start.26) | collective-permute-done | bytes 131104 | tf_op jit(solution)/shard_map/ppermute | solution.py:542
  96.5 2.0 %final_stage.1 = bf16[16,256,128]{2,1,0:T(8,128)(2,1)} custom-call(f32[16,128,256]{2,1,0:T(8,128)S(1)} %get-tuple-element.97.pair_ref.refs_0_, f32[16,128,256]{2,1,0:T(8,128)S(1)} %gate_stage.1.gate_ref.refs_1_, bf16[128,128]{1,0:T(8,128)(2,1)S(1)} %get-tuple-element.114.w_ref.refs_2_, bf16[1,32,16,128]{3,2,1,0:T(8,128)(2,1)S(1)} %get-tuple-element.119.refs_3_, ...), custom_call_target="tpu_custom_call" | custom-call | flops 134217 | bytes 6291 | tf_op jit(solution)/shard_map/final_stage/pallas_call | solution.py:49
  (53 shorter events, 22.7 us)
Async XLA Ops:
  2.4 9.6 %collective-permute-start.2 = (bf16[33,16,128]{2,1,0:T(8,128)(2,1)S(1)}, bf16[33,16,128]{2,1,0:T(8,128)(2,1)S(1)}, u32[]{:S(2)}, u32[]{:S(2)}) collective-permute-start(bf16[33,16,128]{2,1,0:T(8,128)(2,1)S(1)} %pad_maximum_fusion.1), channel_id=1, source_target_pairs={{0,12},{1,13},{2,14},{3,15},{4,8},{5,9},{6,10},{7,11},{8,4},{9,5},... | collective-permute-start | bytes 405512 | tf_op jit(solution)/shard_map/ppermute | solution.py:542
  7.5 5.2 %collective-permute-start = (bf16[17,16,128]{2,1,0:T(8,128)(2,1)S(1)}, bf16[17,16,128]{2,1,0:T(8,128)(2,1)S(1)}, u32[]{:S(2)}, u32[]{:S(2)}) collective-permute-start(bf16[17,16,128]{2,1,0:T(8,128)(2,1)S(1)} %get-tuple-element.67), channel_id=1, source_target_pairs={{0,4},{1,5},{2,6},{3,7},{4,0},{5,1},{6,2},{7,3},{8,12},{9,13},{10,... | collective-permute-start | bytes 208904 | tf_op jit(solution)/shard_map/ppermute | solution.py:542
  7.5 8.6 %collective-permute-start.1 = (bf16[17,16,128]{2,1,0:T(8,128)(2,1)S(1)}, bf16[17,16,128]{2,1,0:T(8,128)(2,1)S(1)}, u32[]{:S(2)}, u32[]{:S(2)}) collective-permute-start(bf16[17,16,128]{2,1,0:T(8,128)(2,1)S(1)} %get-tuple-element.67), channel_id=1, source_target_pairs={{0,8},{1,9},{2,10},{3,11},{4,12},{5,13},{6,14},{7,15},{8,0},{9,1},... | collective-permute-start | bytes 208904 | tf_op jit(solution)/shard_map/ppermute | solution.py:542
  16.1 41.7 %collective-permute-start.16 = (bf16[16,256,128]{2,1,0:T(8,128)(2,1)}, bf16[16,256,128]{2,1,0:T(8,128)(2,1)S(1)}, u32[]{:S(2)}, u32[]{:S(2)}) collective-permute-start(bf16[16,256,128]{2,1,0:T(8,128)(2,1)} %refs_2_.3), channel_id=1, source_target_pairs={{0,12},{1,13},{2,14},{3,15},{4,8},{5,9},{6,10},{7,11},{8,4},{9,5},... | collective-permute-start | bytes 3145736 | tf_op jit(solution)/shard_map/ppermute | solution.py:542
  18.7 7.2 %collective-permute-start.3 = (bf16[4,17,16,128]{3,2,1,0:T(8,128)(2,1)S(1)}, bf16[4,17,16,128]{3,2,1,0:T(8,128)(2,1)S(1)}, u32[]{:S(2)}, u32[]{:S(2)}) collective-permute-start(bf16[4,17,16,128]{3,2,1,0:T(8,128)(2,1)S(1)} %pad_maximum_fusion.refs_6_), channel_id=1, source_target_pairs={{0,2},{1,3},{2,0},{3,1},{4,6},{5,7},{6,4},{7,5},{8,10},{9,11},{10,... | collective-permute-start | bytes 835592 | tf_op jit(solution)/shard_map/ppermute | solution.py:542
  20.2 5.7 %collective-permute-start.4 = (bf16[4,17,16,128]{3,2,1,0:T(8,128)(2,1)S(1)}, bf16[4,17,16,128]{3,2,1,0:T(8,128)(2,1)S(1)}, u32[]{:S(2)}, u32[]{:S(2)}) collective-permute-start(bf16[4,17,16,128]{3,2,1,0:T(8,128)(2,1)S(1)} %pad_maximum_fusion.refs_6_), channel_id=1, source_target_pairs={{0,1},{1,0},{2,3},{3,2},{4,5},{5,4},{6,7},{7,6},{8,9},{9,8},{10,11... | collective-permute-start | bytes 835592 | tf_op jit(solution)/shard_map/ppermute | solution.py:542
  33.7 9.4 %collective-permute-start.6 = (bf16[1,32,16,256]{3,2,1,0:T(8,128)(2,1)S(1)}, bf16[1,32,16,256]{3,2,1,0:T(8,128)(2,1)S(1)}, u32[]{:S(2)}, u32[]{:S(2)}) collective-permute-start(bf16[1,32,16,256]{3,2,1,0:T(8,128)(2,1)S(1)} %get-tuple-element.79), channel_id=1, source_target_pairs={{0,2},{1,3},{2,0},{3,1},{4,6},{5,7},{6,4},{7,5},{8,10},{9,11},{10,... | collective-permute-start | bytes 786440 | tf_op jit(solution)/shard_map/ppermute | solution.py:542
  35.2 13.7 %collective-permute-start.10 = (bf16[1,32,16,256]{3,2,1,0:T(8,128)(2,1)S(1)}, bf16[1,32,16,256]{3,2,1,0:T(8,128)(2,1)S(1)}, u32[]{:S(2)}, u32[]{:S(2)}) collective-permute-start(bf16[1,32,16,256]{3,2,1,0:T(8,128)(2,1)S(1)} %get-tuple-element.88), channel_id=1, source_target_pairs={{0,6},{1,7},{2,4},{3,5},{4,2},{5,3},{6,0},{7,1},{8,14},{9,15},{10,... | collective-permute-start | bytes 786440 | tf_op jit(solution)/shard_map/ppermute | solution.py:542
  35.2 18.5 %collective-permute-start.8 = (bf16[1,32,16,256]{3,2,1,0:T(8,128)(2,1)S(1)}, bf16[1,32,16,256]{3,2,1,0:T(8,128)(2,1)S(1)}, u32[]{:S(2)}, u32[]{:S(2)}) collective-permute-start(bf16[1,32,16,256]{3,2,1,0:T(8,128)(2,1)S(1)} %get-tuple-element.82), channel_id=1, source_target_pairs={{0,4},{1,5},{2,6},{3,7},{4,0},{5,1},{6,2},{7,3},{8,12},{9,13},{10,... | collective-permute-start | bytes 786440 | tf_op jit(solution)/shard_map/ppermute | solution.py:542
  48.9 11.3 %collective-permute-start.11 = (bf16[1,32,16,256]{3,2,1,0:T(8,128)(2,1)S(1)}, bf16[1,32,16,256]{3,2,1,0:T(8,128)(2,1)S(1)}, u32[]{:S(2)}, u32[]{:S(2)}) collective-permute-start(bf16[1,32,16,256]{3,2,1,0:T(8,128)(2,1)S(1)} %get-tuple-element.90), channel_id=1, source_target_pairs={{0,6},{1,7},{2,4},{3,5},{4,2},{5,3},{6,0},{7,1},{8,14},{9,15},{10,... | collective-permute-start | bytes 786440 | tf_op jit(solution)/shard_map/ppermute | solution.py:542
  53.8 11.0 %collective-permute-start.9 = (bf16[1,32,16,256]{3,2,1,0:T(8,128)(2,1)S(1)}, bf16[1,32,16,256]{3,2,1,0:T(8,128)(2,1)S(1)}, u32[]{:S(2)}, u32[]{:S(2)}) collective-permute-start(bf16[1,32,16,256]{3,2,1,0:T(8,128)(2,1)S(1)} %get-tuple-element.87), channel_id=1, source_target_pairs={{0,4},{1,5},{2,6},{3,7},{4,0},{5,1},{6,2},{7,3},{8,12},{9,13},{10,... | collective-permute-start | bytes 786440 | tf_op jit(solution)/shard_map/ppermute | solution.py:542
  56.3 9.4 %collective-permute-start.7 = (bf16[1,32,16,256]{3,2,1,0:T(8,128)(2,1)S(1)}, bf16[1,32,16,256]{3,2,1,0:T(8,128)(2,1)S(1)}, u32[]{:S(2)}, u32[]{:S(2)}) collective-permute-start(bf16[1,32,16,256]{3,2,1,0:T(8,128)(2,1)S(1)} %get-tuple-element.81), channel_id=1, source_target_pairs={{0,2},{1,3},{2,0},{3,1},{4,6},{5,7},{6,4},{7,5},{8,10},{9,11},{10,... | collective-permute-start | bytes 786440 | tf_op jit(solution)/shard_map/ppermute | solution.py:542
  57.8 8.6 %collective-permute-start.12 = (bf16[1,32,16,256]{3,2,1,0:T(8,128)(2,1)S(1)}, bf16[1,32,16,256]{3,2,1,0:T(8,128)(2,1)S(1)}, u32[]{:S(2)}, u32[]{:S(2)}) collective-permute-start(bf16[1,32,16,256]{3,2,1,0:T(8,128)(2,1)S(1)} %get-tuple-element.91.refs_4_), channel_id=1, source_target_pairs={{0,1},{1,0},{2,3},{3,2},{4,5},{5,4},{6,7},{7,6},{8,9},{9,8},{10,11... | collective-permute-start | bytes 786440 | tf_op jit(solution)/shard_map/ppermute | solution.py:542
  57.8 10.0 %collective-permute-start.13 = (bf16[1,32,16,256]{3,2,1,0:T(8,128)(2,1)S(1)}, bf16[1,32,16,256]{3,2,1,0:T(8,128)(2,1)S(1)}, u32[]{:S(2)}, u32[]{:S(2)}) collective-permute-start(bf16[1,32,16,256]{3,2,1,0:T(8,128)(2,1)S(1)} %collective-permute-done.6.refs_5_), channel_id=1, source_target_pairs={{0,1},{1,0},{2,3},{3,2},{4,5},{5,4},{6,7},{7,6},{8,9},{9,8},{10,11... | collective-permute-start | bytes 786440 | tf_op jit(solution)/shard_map/ppermute | solution.py:542
  60.2 8.9 %collective-permute-start.14 = (bf16[1,32,16,256]{3,2,1,0:T(8,128)(2,1)S(1)}, bf16[1,32,16,256]{3,2,1,0:T(8,128)(2,1)S(1)}, u32[]{:S(2)}, u32[]{:S(2)}) collective-permute-start(bf16[1,32,16,256]{3,2,1,0:T(8,128)(2,1)S(1)} %collective-permute-done.8.refs_6_), channel_id=1, source_target_pairs={{0,1},{1,0},{2,3},{3,2},{4,5},{5,4},{6,7},{7,6},{8,9},{9,8},{10,11... | collective-permute-start | bytes 786440 | tf_op jit(solution)/shard_map/ppermute | solution.py:542
  65.7 10.1 %collective-permute-start.19 = (bf16[1,32,16,256]{3,2,1,0:T(8,128)(2,1)S(1)}, bf16[1,32,16,256]{3,2,1,0:T(8,128)(2,1)S(1)}, u32[]{:S(2)}, u32[]{:S(2)}) collective-permute-start(bf16[1,32,16,256]{3,2,1,0:T(8,128)(2,1)S(1)} %get-tuple-element.112), channel_id=1, source_target_pairs={{0,6},{1,7},{2,4},{3,5},{4,2},{5,3},{6,0},{7,1},{8,14},{9,15},{10,... | collective-permute-start | bytes 786440 | tf_op jit(solution)/shard_map/ppermute | solution.py:542
  66.4 13.7 %collective-permute-start.18 = (bf16[1,32,16,256]{3,2,1,0:T(8,128)(2,1)S(1)}, bf16[1,32,16,256]{3,2,1,0:T(8,128)(2,1)S(1)}, u32[]{:S(2)}, u32[]{:S(2)}) collective-permute-start(bf16[1,32,16,256]{3,2,1,0:T(8,128)(2,1)S(1)} %get-tuple-element.110), channel_id=1, source_target_pairs={{0,4},{1,5},{2,6},{3,7},{4,0},{5,1},{6,2},{7,3},{8,12},{9,13},{10,... | collective-permute-start | bytes 786440 | tf_op jit(solution)/shard_map/ppermute | solution.py:542
  67.8 12.6 %collective-permute-start.17 = (bf16[1,32,16,256]{3,2,1,0:T(8,128)(2,1)S(1)}, bf16[1,32,16,256]{3,2,1,0:T(8,128)(2,1)S(1)}, u32[]{:S(2)}, u32[]{:S(2)}) collective-permute-start(bf16[1,32,16,256]{3,2,1,0:T(8,128)(2,1)S(1)} %get-tuple-element.108), channel_id=1, source_target_pairs={{0,2},{1,3},{2,0},{3,1},{4,6},{5,7},{6,4},{7,5},{8,10},{9,11},{10,... | collective-permute-start | bytes 786440 | tf_op jit(solution)/shard_map/ppermute | solution.py:542
  81.4 6.2 %collective-permute-start.27 = (bf16[1,32,16,128]{3,2,1,0:T(8,128)(2,1)S(1)}, bf16[1,32,16,128]{3,2,1,0:T(8,128)(2,1)S(1)}, u32[]{:S(2)}, u32[]{:S(2)}) collective-permute-start(bf16[1,32,16,128]{3,2,1,0:T(8,128)(2,1)S(1)} %get-tuple-element.124), channel_id=1, source_target_pairs={{0,2},{1,3},{2,0},{3,1},{4,6},{5,7},{6,4},{7,5},{8,10},{9,11},{10,... | collective-permute-start | bytes 393224 | tf_op jit(solution)/shard_map/ppermute | solution.py:542
  82.5 6.8 %collective-permute-start.28 = (bf16[1,32,16,128]{3,2,1,0:T(8,128)(2,1)S(1)}, bf16[1,32,16,128]{3,2,1,0:T(8,128)(2,1)S(1)}, u32[]{:S(2)}, u32[]{:S(2)}) collective-permute-start(bf16[1,32,16,128]{3,2,1,0:T(8,128)(2,1)S(1)} %get-tuple-element.125), channel_id=1, source_target_pairs={{0,4},{1,5},{2,6},{3,7},{4,0},{5,1},{6,2},{7,3},{8,12},{9,13},{10,... | collective-permute-start | bytes 393224 | tf_op jit(solution)/shard_map/ppermute | solution.py:542
  83.2 8.9 %collective-permute-start.29 = (bf16[1,32,16,128]{3,2,1,0:T(8,128)(2,1)S(1)}, bf16[1,32,16,128]{3,2,1,0:T(8,128)(2,1)S(1)}, u32[]{:S(2)}, u32[]{:S(2)}) collective-permute-start(bf16[1,32,16,128]{3,2,1,0:T(8,128)(2,1)S(1)} %get-tuple-element.126), channel_id=1, source_target_pairs={{0,6},{1,7},{2,4},{3,5},{4,2},{5,3},{6,0},{7,1},{8,14},{9,15},{10,... | collective-permute-start | bytes 393224 | tf_op jit(solution)/shard_map/ppermute | solution.py:542
  85.7 7.4 %collective-permute-start.24 = (bf16[1,32,16,128]{3,2,1,0:T(8,128)(2,1)S(1)}, bf16[1,32,16,128]{3,2,1,0:T(8,128)(2,1)S(1)}, u32[]{:S(2)}, u32[]{:S(2)}) collective-permute-start(bf16[1,32,16,128]{3,2,1,0:T(8,128)(2,1)S(1)} %get-tuple-element.120), channel_id=1, source_target_pairs={{0,2},{1,3},{2,0},{3,1},{4,6},{5,7},{6,4},{7,5},{8,10},{9,11},{10,... | collective-permute-start | bytes 393224 | tf_op jit(solution)/shard_map/ppermute | solution.py:542
  86.9 7.6 %collective-permute-start.25 = (bf16[1,32,16,128]{3,2,1,0:T(8,128)(2,1)S(1)}, bf16[1,32,16,128]{3,2,1,0:T(8,128)(2,1)S(1)}, u32[]{:S(2)}, u32[]{:S(2)}) collective-permute-start(bf16[1,32,16,128]{3,2,1,0:T(8,128)(2,1)S(1)} %get-tuple-element.121), channel_id=1, source_target_pairs={{0,4},{1,5},{2,6},{3,7},{4,0},{5,1},{6,2},{7,3},{8,12},{9,13},{10,... | collective-permute-start | bytes 393224 | tf_op jit(solution)/shard_map/ppermute | solution.py:542
  87.6 8.8 %collective-permute-start.26 = (bf16[1,32,16,128]{3,2,1,0:T(8,128)(2,1)S(1)}, bf16[1,32,16,128]{3,2,1,0:T(8,128)(2,1)S(1)}, u32[]{:S(2)}, u32[]{:S(2)}) collective-permute-start(bf16[1,32,16,128]{3,2,1,0:T(8,128)(2,1)S(1)} %get-tuple-element.122), channel_id=1, source_target_pairs={{0,6},{1,7},{2,4},{3,5},{4,2},{5,3},{6,0},{7,1},{8,14},{9,15},{10,... | collective-permute-start | bytes 393224 | tf_op jit(solution)/shard_map/ppermute | solution.py:542
  (7 other events, 46.4 us)

commit v5 on v4

--- a/solution.py
+++ b/solution.py
@@ -643,7 +643,11 @@
     a = exchange(a, b)
     near = tri_stage(a, with_other_core(b), cores, 0)
     far_b = mirror_stage(update, far_couple, w_in, far_seen, parts, split)
-    far_b = exchange(far_b, a)
+    if hops:
+        far_b = list(far_b)
+        _, far_b[1] = after(a[3], far_b[1])
+        _, far_b[2:] = after(a[1], far_b[2:])
+    far_b = exchange(far_b)
     if hops:
         near, pair = after(near, pair)
     gate = gate_stage(pair, w_gate)

time: 98.6 us -> 97.9 us (level)
  waiting for transfers between devices: 45 us -> 41.3 us
  starting transfers between devices: 32.2 us -> 35.2 us
    ppermute x30, waiting for transfers between devices: 45 us -> 41.3 us  [send(): return lax.ppermute(value, 'row', [(i, move(i)) for i in range(devs)])]
    ppermute x30, starting transfers between devices: 32.2 us -> 35.2 us  [send(): return lax.ppermute(value, 'row', [(i, move(i)) for i in range(devs)])]
  transfers between devices with their start and end apart: 30 -> 30, of which waited for: 17 -> 15; matrix products, arithmetic and copies ran while one was open for 0% -> 0% of each run, Pallas kernels for 17% -> 17%
where the time goes in v5:
time: 97.9 us; the launch traced here: 97.8 us
  waiting for transfers between devices  41.3 us (42%)
  starting transfers between devices  35.2 us (36%)
  Pallas kernels  21.2 us (22%)
    ppermute x30, waiting for transfers between devices, send(): return lax.ppermute(value, 'row', [(i, move(i)) for i in range(devs)])  41.3 us
    ppermute x30, starting transfers between devices, send(): return lax.ppermute(value, 'row', [(i, move(i)) for i in range(devs)])  35.2 us
    pallas_call x10, Pallas kernels, local_call(): pl.pallas_call(kernel, grid=() if whole else (steps,), in_specs=in_specs,...  21.2 us
  transfers between devices with their start and end apart: 30, of which 15 were waited for; matrix products, arithmetic and copies ran while one was open for 0% of the time, Pallas kernels for 17%

profile of v5, /device:TPU:0, one launch (start us, length us, event | category | flops | bytes accessed | tf_op | source)
XLA Modules:
  0.0 97.8 jit_solution(11200240228107932288)
XLA Ops:
  0.0 2.3 %msa_stage.1 = (bf16[17,16,128]{2,1,0:T(8,128)(2,1)S(1)}, bf16[256,128]{1,0:T(8,128)(2,1)S(1)}) custom-call(bf16[64,16,256]{2,1,0:T(8,128)(2,1)} %msa_ref.1, s32[16,64]{1,0:T(8,128)} %bitcast.20, bf16[32,256]{1,0:T(8,128)(2,1)} %bitcast.18, bf16[32,256]{1,0:T(8,128)(2,1)} %bitcast.19), custom_call_target="tpu_custom_call" | custom-call | flops 33554 | bytes 524 | tf_op jit(solution)/shard_map/msa_stage/pallas_call | solution.py:49
  2.4 5.1 %collective-permute-start.2 = (bf16[33,16,128]{2,1,0:T(8,128)(2,1)S(1)}, bf16[33,16,128]{2,1,0:T(8,128)(2,1)S(1)}, u32[]{:S(2)}, u32[]{:S(2)}) collective-permute-start(bf16[33,16,128]{2,1,0:T(8,128)(2,1)S(1)} %pad_maximum_fusion.1), channel_id=1, source_target_pairs={{0,12},{1,13},{2,14},{3,15},{4,8},{5,9},{6,10},{7,11},{8,4},{9,5},... | collective-permute-start | bytes 405512 | tf_op jit(solution)/shard_map/ppermute | solution.py:542
  8.1 1.7 %weights_stage.1 = (bf16[128,1024]{1,0:T(8,128)(2,1)S(1)}, bf16[512,128]{1,0:T(8,128)(2,1)S(1)}, bf16[128,128]{1,0:T(8,128)(2,1)S(1)}, bf16[128,128]{1,0:T(8,128...) custom-call(bf16[1024,128]{1,0:T(8,128)(2,1)} %refs_0_.1, bf16[128,512]{1,0:T(8,128)(2,1)} %refs_1_.1, ...), custom_call_target="tpu_custom_call" | custom-call | flops 25165 | bytes 524 | tf_op jit(solution)/shard_map/weights_stage/pallas_call | solution.py:49
  9.8 2.2 %collective-permute-done.2 = bf16[33,16,128]{2,1,0:T(8,128)(2,1)S(1)} collective-permute-done((bf16[33,16,128]{2,1,0:T(8,128)(2,1)S(1)}, bf16[33,16,128]{2,1,0:T(8,128)(2,1)S(1)}, u32[]{:S(2)}, u32[]{:S(2)}) %collective-permute-start.2) | collective-permute-done | bytes 135200 | tf_op jit(solution)/shard_map/ppermute | solution.py:542
  12.7 3.4 %collective-permute-done.1 = bf16[17,16,128]{2,1,0:T(8,128)(2,1)S(1)} collective-permute-done((bf16[17,16,128]{2,1,0:T(8,128)(2,1)S(1)}, bf16[17,16,128]{2,1,0:T(8,128)(2,1)S(1)}, u32[]{:S(2)}, u32[]{:S(2)}) %collective-permute-start.1) | collective-permute-done | bytes 69664 | tf_op jit(solution)/shard_map/ppermute | solution.py:542
  16.1 2.5 %collective-permute-start.16 = (bf16[16,256,128]{2,1,0:T(8,128)(2,1)}, bf16[16,256,128]{2,1,0:T(8,128)(2,1)S(1)}, u32[]{:S(2)}, u32[]{:S(2)}) collective-permute-start(bf16[16,256,128]{2,1,0:T(8,128)(2,1)} %refs_2_.3), channel_id=1, source_target_pairs={{0,12},{1,13},{2,14},{3,15},{4,8},{5,9},{6,10},{7,11},{8,4},{9,5},... | collective-permute-start | bytes 3145736 | tf_op jit(solution)/shard_map/ppermute | solution.py:542
  20.2 5.7 %collective-permute-done.3.refs_7_ = bf16[4,17,16,128]{3,2,1,0:T(8,128)(2,1)S(1)} collective-permute-done((bf16[4,17,16,128]{3,2,1,0:T(8,128)(2,1)S(1)}, bf16[4,17,16,128]{3,2,1,0:T(8,128)(2,1)S(1)}, u32[]{:S(2)}, u32[]{:S(2)}) %collective-permute-start.3) | collective-permute-done | bytes 278560 | tf_op jit(solution)/shard_map/ppermute | solution.py:542
  27.5 6.2 %pair_stage.1 = (f32[16,128,256]{2,1,0:T(8,128)S(1)}, bf16[1,32,16,256]{3,2,1,0:T(8,128)(2,1)S(1)}, bf16[1,32,16,256]{3,2,1,0:T(8,128)(2,1)S(1)}, bf16[1,32,16,2...) custom-call(bf16[256,128]{1,0:T(8,128)(2,1)S(1)} %get-tuple-element., ...), custom_call_target="tpu_custom_call" | custom-call | flops 2147483 | bytes 8388 | tf_op jit(solution)/shard_map/pair_stage/pallas_call | solution.py:49
  35.2 2.0 %collective-permute-start.8 = (bf16[1,32,16,256]{3,2,1,0:T(8,128)(2,1)S(1)}, bf16[1,32,16,256]{3,2,1,0:T(8,128)(2,1)S(1)}, u32[]{:S(2)}, u32[]{:S(2)}) collective-permute-start(bf16[1,32,16,256]{3,2,1,0:T(8,128)(2,1)S(1)} %get-tuple-element.82), channel_id=1, source_target_pairs={{0,4},{1,5},{2,6},{3,7},{4,0},{5,1},{6,2},{7,3},{8,12},{9,13},{10,... | collective-permute-start | bytes 786440 | tf_op jit(solution)/shard_map/ppermute | solution.py:542
  37.2 5.8 %collective-permute-done.6.refs_5_ = bf16[1,32,16,256]{3,2,1,0:T(8,128)(2,1)S(1)} collective-permute-done((bf16[1,32,16,256]{3,2,1,0:T(8,128)(2,1)S(1)}, bf16[1,32,16,256]{3,2,1,0:T(8,128)(2,1)S(1)}, u32[]{:S(2)}, u32[]{:S(2)}) %collective-permute-start.6) | collective-permute-done | bytes 262176 | tf_op jit(solution)/shard_map/ppermute | solution.py:542
  43.0 2.5 %collective-permute-start.7 = (bf16[1,32,16,256]{3,2,1,0:T(8,128)(2,1)S(1)}, bf16[1,32,16,256]{3,2,1,0:T(8,128)(2,1)S(1)}, u32[]{:S(2)}, u32[]{:S(2)}) collective-permute-start(bf16[1,32,16,256]{3,2,1,0:T(8,128)(2,1)S(1)} %get-tuple-element.81), channel_id=1, source_target_pairs={{0,2},{1,3},{2,0},{3,1},{4,6},{5,7},{6,4},{7,5},{8,10},{9,11},{10,... | collective-permute-start | bytes 786440 | tf_op jit(solution)/shard_map/ppermute | solution.py:542
  45.6 3.4 %collective-permute-done.10.refs_7_ = bf16[1,32,16,256]{3,2,1,0:T(8,128)(2,1)S(1)} collective-permute-done((bf16[1,32,16,256]{3,2,1,0:T(8,128)(2,1)S(1)}, bf16[1,32,16,256]{3,2,1,0:T(8,128)(2,1)S(1)}, u32[]{:S(2)}, u32[]{:S(2)}) %collective-permute-start.10) | collective-permute-done | bytes 262176 | tf_op jit(solution)/shard_map/ppermute | solution.py:542
  48.9 2.6 %collective-permute-start.11 = (bf16[1,32,16,256]{3,2,1,0:T(8,128)(2,1)S(1)}, bf16[1,32,16,256]{3,2,1,0:T(8,128)(2,1)S(1)}, u32[]{:S(2)}, u32[]{:S(2)}) collective-permute-start(bf16[1,32,16,256]{3,2,1,0:T(8,128)(2,1)S(1)} %get-tuple-element.90), channel_id=1, source_target_pairs={{0,6},{1,7},{2,4},{3,5},{4,2},{5,3},{6,0},{7,1},{8,14},{9,15},{10,... | collective-permute-start | bytes 786440 | tf_op jit(solution)/shard_map/ppermute | solution.py:542
  51.6 3.5 %update_stage.1.update_ref = f32[16,128,256]{2,1,0:T(8,128)S(1)} custom-call(bf16[256,128]{1,0:T(8,128)(2,1)S(1)} %bitcast.14, bf16[128,1024]{1,0:T(8,128)(2,1)S(1)} %get-tuple-element.74.refs_3_.w_out_ref, bf16[16,17,16,128]{3,2,1,0:T(8,128)(2,1)S(1)} %get-tuple-element.84.right), custom_call_target="tpu_custom_call" | custom-call | flops 2147483 | bytes 4194 | tf_op jit(solution)/shard_map/update_stage/pallas_call | solution.py:49
  56.3 1.9 %mirror_stage.1 = (bf16[1,32,16,256]{3,2,1,0:T(8,128)(2,1)S(1)}, bf16[1,32,16,256]{3,2,1,0:T(8,128)(2,1)S(1)}, bf16[1,32,16,256]{3,2,1,0:T(8,128)(2,1)S(1)}, bf16[1,32,16,256]{3,2,1,0:T(8,128)(2,1)S(1)}) custom-call(f32[16,128,256]{2,1,0:T(8,128)S(1)} %update_stage.1.update_ref, bf16[16,256,128]{2,1,0:T(8,128)(2,1)S(1)} %collective-permute-done.16.couple_ref, ...), custom_call_target="tpu_custom_call" | custom-call | flops 268435 | bytes 20971520 | tf_op jit(solution)/shard_map/mirror_stage/pallas_call | solution.py:49
  60.2 4.5 %collective-permute-start.18 = (bf16[1,32,16,256]{3,2,1,0:T(8,128)(2,1)S(1)}, bf16[1,32,16,256]{3,2,1,0:T(8,128)(2,1)S(1)}, u32[]{:S(2)}, u32[]{:S(2)}) collective-permute-start(bf16[1,32,16,256]{3,2,1,0:T(8,128)(2,1)S(1)} %get-tuple-element.111), channel_id=1, source_target_pairs={{0,4},{1,5},{2,6},{3,7},{4,0},{5,1},{6,2},{7,3},{8,12},{9,13},{10,... | collective-permute-start | bytes 786440 | tf_op jit(solution)/shard_map/ppermute | solution.py:542
  64.8 1.7 %collective-permute-start.19 = (bf16[1,32,16,256]{3,2,1,0:T(8,128)(2,1)S(1)}, bf16[1,32,16,256]{3,2,1,0:T(8,128)(2,1)S(1)}, u32[]{:S(2)}, u32[]{:S(2)}) collective-permute-start(bf16[1,32,16,256]{3,2,1,0:T(8,128)(2,1)S(1)} %get-tuple-element.112), channel_id=1, source_target_pairs={{0,6},{1,7},{2,4},{3,5},{4,2},{5,3},{6,0},{7,1},{8,14},{9,15},{10,... | collective-permute-start | bytes 786440 | tf_op jit(solution)/shard_map/ppermute | solution.py:542
  68.7 3.1 %collective-permute-done.18.refs_6_ = bf16[1,32,16,256]{3,2,1,0:T(8,128)(2,1)S(1)} collective-permute-done((bf16[1,32,16,256]{3,2,1,0:T(8,128)(2,1)S(1)}, bf16[1,32,16,256]{3,2,1,0:T(8,128)(2,1)S(1)}, u32[]{:S(2)}, u32[]{:S(2)}) %collective-permute-start.18) | collective-permute-done | bytes 262176 | tf_op jit(solution)/shard_map/ppermute | solution.py:542
  71.9 6.4 %collective-permute-done.19.refs_7_ = bf16[1,32,16,256]{3,2,1,0:T(8,128)(2,1)S(1)} collective-permute-done((bf16[1,32,16,256]{3,2,1,0:T(8,128)(2,1)S(1)}, bf16[1,32,16,256]{3,2,1,0:T(8,128)(2,1)S(1)}, u32[]{:S(2)}, u32[]{:S(2)}) %collective-permute-start.19) | collective-permute-done | bytes 262176 | tf_op jit(solution)/shard_map/ppermute | solution.py:542
  81.3 1.6 %collective-permute-start.28 = (bf16[1,32,16,128]{3,2,1,0:T(8,128)(2,1)S(1)}, bf16[1,32,16,128]{3,2,1,0:T(8,128)(2,1)S(1)}, u32[]{:S(2)}, u32[]{:S(2)}) collective-permute-start(bf16[1,32,16,128]{3,2,1,0:T(8,128)(2,1)S(1)} %get-tuple-element.125), channel_id=1, source_target_pairs={{0,4},{1,5},{2,6},{3,7},{4,0},{5,1},{6,2},{7,3},{8,12},{9,13},{10,... | collective-permute-start | bytes 393224 | tf_op jit(solution)/shard_map/ppermute | solution.py:542
  85.7 1.6 %collective-permute-start.25 = (bf16[1,32,16,128]{3,2,1,0:T(8,128)(2,1)S(1)}, bf16[1,32,16,128]{3,2,1,0:T(8,128)(2,1)S(1)}, u32[]{:S(2)}, u32[]{:S(2)}) collective-permute-start(bf16[1,32,16,128]{3,2,1,0:T(8,128)(2,1)S(1)} %get-tuple-element.121), channel_id=1, source_target_pairs={{0,4},{1,5},{2,6},{3,7},{4,0},{5,1},{6,2},{7,3},{8,12},{9,13},{10,... | collective-permute-start | bytes 393224 | tf_op jit(solution)/shard_map/ppermute | solution.py:542
  88.6 2.6 %collective-permute-done.29.refs_3_ = bf16[1,32,16,128]{3,2,1,0:T(8,128)(2,1)S(1)} collective-permute-done((bf16[1,32,16,128]{3,2,1,0:T(8,128)(2,1)S(1)}, bf16[1,32,16,128]{3,2,1,0:T(8,128)(2,1)S(1)}, u32[]{:S(2)}, u32[]{:S(2)}) %collective-permute-start.29) | collective-permute-done | bytes 131104 | tf_op jit(solution)/shard_map/ppermute | solution.py:542
  93.3 2.5 %collective-permute-done.26.refs_6_ = bf16[1,32,16,128]{3,2,1,0:T(8,128)(2,1)S(1)} collective-permute-done((bf16[1,32,16,128]{3,2,1,0:T(8,128)(2,1)S(1)}, bf16[1,32,16,128]{3,2,1,0:T(8,128)(2,1)S(1)}, u32[]{:S(2)}, u32[]{:S(2)}) %collective-permute-start.26) | collective-permute-done | bytes 131104 | tf_op jit(solution)/shard_map/ppermute | solution.py:542
  95.8 2.0 %final_stage.1 = bf16[16,256,128]{2,1,0:T(8,128)(2,1)} custom-call(f32[16,128,256]{2,1,0:T(8,128)S(1)} %get-tuple-element.97.pair_ref.refs_0_, f32[16,128,256]{2,1,0:T(8,128)S(1)} %gate_stage.1.gate_ref.refs_1_, bf16[128,128]{1,0:T(8,128)(2,1)S(1)} %get-tuple-element.114.w_ref.refs_2_, bf16[1,32,16,128]{3,2,1,0:T(8,128)(2,1)S(1)} %get-tuple-element.119.refs_3_, ...), custom_call_target="tpu_custom_call" | custom-call | flops 134217 | bytes 6291 | tf_op jit(solution)/shard_map/final_stage/pallas_call | solution.py:49
  (53 shorter events, 20.7 us)
Async XLA Ops:
  2.4 9.6 %collective-permute-start.2 = (bf16[33,16,128]{2,1,0:T(8,128)(2,1)S(1)}, bf16[33,16,128]{2,1,0:T(8,128)(2,1)S(1)}, u32[]{:S(2)}, u32[]{:S(2)}) collective-permute-start(bf16[33,16,128]{2,1,0:T(8,128)(2,1)S(1)} %pad_maximum_fusion.1), channel_id=1, source_target_pairs={{0,12},{1,13},{2,14},{3,15},{4,8},{5,9},{6,10},{7,11},{8,4},{9,5},... | collective-permute-start | bytes 405512 | tf_op jit(solution)/shard_map/ppermute | solution.py:542
  7.5 8.6 %collective-permute-start.1 = (bf16[17,16,128]{2,1,0:T(8,128)(2,1)S(1)}, bf16[17,16,128]{2,1,0:T(8,128)(2,1)S(1)}, u32[]{:S(2)}, u32[]{:S(2)}) collective-permute-start(bf16[17,16,128]{2,1,0:T(8,128)(2,1)S(1)} %get-tuple-element.67), channel_id=1, source_target_pairs={{0,8},{1,9},{2,10},{3,11},{4,12},{5,13},{6,14},{7,15},{8,0},{9,1},... | collective-permute-start | bytes 208904 | tf_op jit(solution)/shard_map/ppermute | solution.py:542
  16.1 40.2 %collective-permute-start.16 = (bf16[16,256,128]{2,1,0:T(8,128)(2,1)}, bf16[16,256,128]{2,1,0:T(8,128)(2,1)S(1)}, u32[]{:S(2)}, u32[]{:S(2)}) collective-permute-start(bf16[16,256,128]{2,1,0:T(8,128)(2,1)} %refs_2_.3), channel_id=1, source_target_pairs={{0,12},{1,13},{2,14},{3,15},{4,8},{5,9},{6,10},{7,11},{8,4},{9,5},... | collective-permute-start | bytes 3145736 | tf_op jit(solution)/shard_map/ppermute | solution.py:542
  18.7 7.2 %collective-permute-start.3 = (bf16[4,17,16,128]{3,2,1,0:T(8,128)(2,1)S(1)}, bf16[4,17,16,128]{3,2,1,0:T(8,128)(2,1)S(1)}, u32[]{:S(2)}, u32[]{:S(2)}) collective-permute-start(bf16[4,17,16,128]{3,2,1,0:T(8,128)(2,1)S(1)} %pad_maximum_fusion.refs_6_), channel_id=1, source_target_pairs={{0,2},{1,3},{2,0},{3,1},{4,6},{5,7},{6,4},{7,5},{8,10},{9,11},{10,... | collective-permute-start | bytes 835592 | tf_op jit(solution)/shard_map/ppermute | solution.py:542
  20.2 5.7 %collective-permute-start.4 = (bf16[4,17,16,128]{3,2,1,0:T(8,128)(2,1)S(1)}, bf16[4,17,16,128]{3,2,1,0:T(8,128)(2,1)S(1)}, u32[]{:S(2)}, u32[]{:S(2)}) collective-permute-start(bf16[4,17,16,128]{3,2,1,0:T(8,128)(2,1)S(1)} %pad_maximum_fusion.refs_6_), channel_id=1, source_target_pairs={{0,1},{1,0},{2,3},{3,2},{4,5},{5,4},{6,7},{7,6},{8,9},{9,8},{10,11... | collective-permute-start | bytes 835592 | tf_op jit(solution)/shard_map/ppermute | solution.py:542
  33.7 9.4 %collective-permute-start.6 = (bf16[1,32,16,256]{3,2,1,0:T(8,128)(2,1)S(1)}, bf16[1,32,16,256]{3,2,1,0:T(8,128)(2,1)S(1)}, u32[]{:S(2)}, u32[]{:S(2)}) collective-permute-start(bf16[1,32,16,256]{3,2,1,0:T(8,128)(2,1)S(1)} %get-tuple-element.79), channel_id=1, source_target_pairs={{0,2},{1,3},{2,0},{3,1},{4,6},{5,7},{6,4},{7,5},{8,10},{9,11},{10,... | collective-permute-start | bytes 786440 | tf_op jit(solution)/shard_map/ppermute | solution.py:542
  35.2 13.7 %collective-permute-start.10 = (bf16[1,32,16,256]{3,2,1,0:T(8,128)(2,1)S(1)}, bf16[1,32,16,256]{3,2,1,0:T(8,128)(2,1)S(1)}, u32[]{:S(2)}, u32[]{:S(2)}) collective-permute-start(bf16[1,32,16,256]{3,2,1,0:T(8,128)(2,1)S(1)} %get-tuple-element.88), channel_id=1, source_target_pairs={{0,6},{1,7},{2,4},{3,5},{4,2},{5,3},{6,0},{7,1},{8,14},{9,15},{10,... | collective-permute-start | bytes 786440 | tf_op jit(solution)/shard_map/ppermute | solution.py:542
  35.2 19.8 %collective-permute-start.8 = (bf16[1,32,16,256]{3,2,1,0:T(8,128)(2,1)S(1)}, bf16[1,32,16,256]{3,2,1,0:T(8,128)(2,1)S(1)}, u32[]{:S(2)}, u32[]{:S(2)}) collective-permute-start(bf16[1,32,16,256]{3,2,1,0:T(8,128)(2,1)S(1)} %get-tuple-element.82), channel_id=1, source_target_pairs={{0,4},{1,5},{2,6},{3,7},{4,0},{5,1},{6,2},{7,3},{8,12},{9,13},{10,... | collective-permute-start | bytes 786440 | tf_op jit(solution)/shard_map/ppermute | solution.py:542
  37.2 23.0 %collective-permute-start.12 = (bf16[1,32,16,256]{3,2,1,0:T(8,128)(2,1)S(1)}, bf16[1,32,16,256]{3,2,1,0:T(8,128)(2,1)S(1)}, u32[]{:S(2)}, u32[]{:S(2)}) collective-permute-start(bf16[1,32,16,256]{3,2,1,0:T(8,128)(2,1)S(1)} %get-tuple-element.91.refs_4_), channel_id=1, source_target_pairs={{0,1},{1,0},{2,3},{3,2},{4,5},{5,4},{6,7},{7,6},{8,9},{9,8},{10,11... | collective-permute-start | bytes 786440 | tf_op jit(solution)/shard_map/ppermute | solution.py:542
  43.0 15.2 %collective-permute-start.7 = (bf16[1,32,16,256]{3,2,1,0:T(8,128)(2,1)S(1)}, bf16[1,32,16,256]{3,2,1,0:T(8,128)(2,1)S(1)}, u32[]{:S(2)}, u32[]{:S(2)}) collective-permute-start(bf16[1,32,16,256]{3,2,1,0:T(8,128)(2,1)S(1)} %get-tuple-element.81), channel_id=1, source_target_pairs={{0,2},{1,3},{2,0},{3,1},{4,6},{5,7},{6,4},{7,5},{8,10},{9,11},{10,... | collective-permute-start | bytes 786440 | tf_op jit(solution)/shard_map/ppermute | solution.py:542
  48.9 11.2 %collective-permute-start.11 = (bf16[1,32,16,256]{3,2,1,0:T(8,128)(2,1)S(1)}, bf16[1,32,16,256]{3,2,1,0:T(8,128)(2,1)S(1)}, u32[]{:S(2)}, u32[]{:S(2)}) collective-permute-start(bf16[1,32,16,256]{3,2,1,0:T(8,128)(2,1)S(1)} %get-tuple-element.90), channel_id=1, source_target_pairs={{0,6},{1,7},{2,4},{3,5},{4,2},{5,3},{6,0},{7,1},{8,14},{9,15},{10,... | collective-permute-start | bytes 786440 | tf_op jit(solution)/shard_map/ppermute | solution.py:542
  55.1 9.7 %collective-permute-start.9 = (bf16[1,32,16,256]{3,2,1,0:T(8,128)(2,1)S(1)}, bf16[1,32,16,256]{3,2,1,0:T(8,128)(2,1)S(1)}, u32[]{:S(2)}, u32[]{:S(2)}) collective-permute-start(bf16[1,32,16,256]{3,2,1,0:T(8,128)(2,1)S(1)} %get-tuple-element.87), channel_id=1, source_target_pairs={{0,4},{1,5},{2,6},{3,7},{4,0},{5,1},{6,2},{7,3},{8,12},{9,13},{10,... | collective-permute-start | bytes 786440 | tf_op jit(solution)/shard_map/ppermute | solution.py:542
  56.3 10.1 %collective-permute-start.13 = (bf16[1,32,16,256]{3,2,1,0:T(8,128)(2,1)S(1)}, bf16[1,32,16,256]{3,2,1,0:T(8,128)(2,1)S(1)}, u32[]{:S(2)}, u32[]{:S(2)}) collective-permute-start(bf16[1,32,16,256]{3,2,1,0:T(8,128)(2,1)S(1)} %collective-permute-done.6.refs_5_), channel_id=1, source_target_pairs={{0,1},{1,0},{2,3},{3,2},{4,5},{5,4},{6,7},{7,6},{8,9},{9,8},{10,11... | collective-permute-start | bytes 786440 | tf_op jit(solution)/shard_map/ppermute | solution.py:542
  58.3 8.7 %collective-permute-start.14 = (bf16[1,32,16,256]{3,2,1,0:T(8,128)(2,1)S(1)}, bf16[1,32,16,256]{3,2,1,0:T(8,128)(2,1)S(1)}, u32[]{:S(2)}, u32[]{:S(2)}) collective-permute-start(bf16[1,32,16,256]{3,2,1,0:T(8,128)(2,1)S(1)} %collective-permute-done.8.refs_6_), channel_id=1, source_target_pairs={{0,1},{1,0},{2,3},{3,2},{4,5},{5,4},{6,7},{7,6},{8,9},{9,8},{10,11... | collective-permute-start | bytes 786440 | tf_op jit(solution)/shard_map/ppermute | solution.py:542
  60.2 6.8 %collective-permute-start.15 = (bf16[1,32,16,256]{3,2,1,0:T(8,128)(2,1)S(1)}, bf16[1,32,16,256]{3,2,1,0:T(8,128)(2,1)S(1)}, u32[]{:S(2)}, u32[]{:S(2)}) collective-permute-start(bf16[1,32,16,256]{3,2,1,0:T(8,128)(2,1)S(1)} %collective-permute-done.10.refs_7_), channel_id=1, source_target_pairs={{0,1},{1,0},{2,3},{3,2},{4,5},{5,4},{6,7},{7,6},{8,9},{9,8},{10,11... | collective-permute-start | bytes 786440 | tf_op jit(solution)/shard_map/ppermute | solution.py:542
  60.2 11.7 %collective-permute-start.18 = (bf16[1,32,16,256]{3,2,1,0:T(8,128)(2,1)S(1)}, bf16[1,32,16,256]{3,2,1,0:T(8,128)(2,1)S(1)}, u32[]{:S(2)}, u32[]{:S(2)}) collective-permute-start(bf16[1,32,16,256]{3,2,1,0:T(8,128)(2,1)S(1)} %get-tuple-element.111), channel_id=1, source_target_pairs={{0,4},{1,5},{2,6},{3,7},{4,0},{5,1},{6,2},{7,3},{8,12},{9,13},{10,... | collective-permute-start | bytes 786440 | tf_op jit(solution)/shard_map/ppermute | solution.py:542
  64.8 13.5 %collective-permute-start.19 = (bf16[1,32,16,256]{3,2,1,0:T(8,128)(2,1)S(1)}, bf16[1,32,16,256]{3,2,1,0:T(8,128)(2,1)S(1)}, u32[]{:S(2)}, u32[]{:S(2)}) collective-permute-start(bf16[1,32,16,256]{3,2,1,0:T(8,128)(2,1)S(1)} %get-tuple-element.112), channel_id=1, source_target_pairs={{0,6},{1,7},{2,4},{3,5},{4,2},{5,3},{6,0},{7,1},{8,14},{9,15},{10,... | collective-permute-start | bytes 786440 | tf_op jit(solution)/shard_map/ppermute | solution.py:542
  66.5 13.3 %collective-permute-start.17 = (bf16[1,32,16,256]{3,2,1,0:T(8,128)(2,1)S(1)}, bf16[1,32,16,256]{3,2,1,0:T(8,128)(2,1)S(1)}, u32[]{:S(2)}, u32[]{:S(2)}) collective-permute-start(bf16[1,32,16,256]{3,2,1,0:T(8,128)(2,1)S(1)} %get-tuple-element.108), channel_id=1, source_target_pairs={{0,2},{1,3},{2,0},{3,1},{4,6},{5,7},{6,4},{7,5},{8,10},{9,11},{10,... | collective-permute-start | bytes 786440 | tf_op jit(solution)/shard_map/ppermute | solution.py:542
  80.8 6.6 %collective-permute-start.27 = (bf16[1,32,16,128]{3,2,1,0:T(8,128)(2,1)S(1)}, bf16[1,32,16,128]{3,2,1,0:T(8,128)(2,1)S(1)}, u32[]{:S(2)}, u32[]{:S(2)}) collective-permute-start(bf16[1,32,16,128]{3,2,1,0:T(8,128)(2,1)S(1)} %get-tuple-element.124), channel_id=1, source_target_pairs={{0,2},{1,3},{2,0},{3,1},{4,6},{5,7},{6,4},{7,5},{8,10},{9,11},{10,... | collective-permute-start | bytes 393224 | tf_op jit(solution)/shard_map/ppermute | solution.py:542
  81.3 7.3 %collective-permute-start.28 = (bf16[1,32,16,128]{3,2,1,0:T(8,128)(2,1)S(1)}, bf16[1,32,16,128]{3,2,1,0:T(8,128)(2,1)S(1)}, u32[]{:S(2)}, u32[]{:S(2)}) collective-permute-start(bf16[1,32,16,128]{3,2,1,0:T(8,128)(2,1)S(1)} %get-tuple-element.125), channel_id=1, source_target_pairs={{0,4},{1,5},{2,6},{3,7},{4,0},{5,1},{6,2},{7,3},{8,12},{9,13},{10,... | collective-permute-start | bytes 393224 | tf_op jit(solution)/shard_map/ppermute | solution.py:542
  83.0 8.3 %collective-permute-start.29 = (bf16[1,32,16,128]{3,2,1,0:T(8,128)(2,1)S(1)}, bf16[1,32,16,128]{3,2,1,0:T(8,128)(2,1)S(1)}, u32[]{:S(2)}, u32[]{:S(2)}) collective-permute-start(bf16[1,32,16,128]{3,2,1,0:T(8,128)(2,1)S(1)} %get-tuple-element.126), channel_id=1, source_target_pairs={{0,6},{1,7},{2,4},{3,5},{4,2},{5,3},{6,0},{7,1},{8,14},{9,15},{10,... | collective-permute-start | bytes 393224 | tf_op jit(solution)/shard_map/ppermute | solution.py:542
  85.1 7.4 %collective-permute-start.24 = (bf16[1,32,16,128]{3,2,1,0:T(8,128)(2,1)S(1)}, bf16[1,32,16,128]{3,2,1,0:T(8,128)(2,1)S(1)}, u32[]{:S(2)}, u32[]{:S(2)}) collective-permute-start(bf16[1,32,16,128]{3,2,1,0:T(8,128)(2,1)S(1)} %get-tuple-element.120), channel_id=1, source_target_pairs={{0,2},{1,3},{2,0},{3,1},{4,6},{5,7},{6,4},{7,5},{8,10},{9,11},{10,... | collective-permute-start | bytes 393224 | tf_op jit(solution)/shard_map/ppermute | solution.py:542
  85.7 7.6 %collective-permute-start.25 = (bf16[1,32,16,128]{3,2,1,0:T(8,128)(2,1)S(1)}, bf16[1,32,16,128]{3,2,1,0:T(8,128)(2,1)S(1)}, u32[]{:S(2)}, u32[]{:S(2)}) collective-permute-start(bf16[1,32,16,128]{3,2,1,0:T(8,128)(2,1)S(1)} %get-tuple-element.121), channel_id=1, source_target_pairs={{0,4},{1,5},{2,6},{3,7},{4,0},{5,1},{6,2},{7,3},{8,12},{9,13},{10,... | collective-permute-start | bytes 393224 | tf_op jit(solution)/shard_map/ppermute | solution.py:542
  87.3 8.4 %collective-permute-start.26 = (bf16[1,32,16,128]{3,2,1,0:T(8,128)(2,1)S(1)}, bf16[1,32,16,128]{3,2,1,0:T(8,128)(2,1)S(1)}, u32[]{:S(2)}, u32[]{:S(2)}) collective-permute-start(bf16[1,32,16,128]{3,2,1,0:T(8,128)(2,1)S(1)} %get-tuple-element.122), channel_id=1, source_target_pairs={{0,6},{1,7},{2,4},{3,5},{4,2},{5,3},{6,0},{7,1},{8,14},{9,15},{10,... | collective-permute-start | bytes 393224 | tf_op jit(solution)/shard_map/ppermute | solution.py:542
  (7 other events, 47.1 us)

commit v6 on v5

--- a/solution.py
+++ b/solution.py
@@ -649,10 +649,10 @@
         _, far_b[2:] = after(a[1], far_b[2:])
     far_b = exchange(far_b)
     if hops:
-        near, pair = after(near, pair)
+        _, pair = after(far_b[1], pair)
     gate = gate_stage(pair, w_gate)
     if hops:
-        (near, gate), far_b = after((near, gate), far_b)
+        near, far_b = after(near, far_b)
     near = exchange(near)
     far = exchange(tri_stage(a, with_other_core(far_b), cores, 2 if hops else 0))
     if hops:

time: 97.9 us -> 97.9 us (level)
  no operation moved by 1% of the time
where the time goes in v6:
time: 97.9 us; the launch traced here: 97.8 us
  waiting for transfers between devices  41.3 us (42%)
  starting transfers between devices  35.2 us (36%)
  Pallas kernels  21.1 us (22%)
    ppermute x30, waiting for transfers between devices, send(): return lax.ppermute(value, 'row', [(i, move(i)) for i in range(devs)])  41.3 us
    ppermute x30, starting transfers between devices, send(): return lax.ppermute(value, 'row', [(i, move(i)) for i in range(devs)])  35.2 us
    pallas_call x10, Pallas kernels, local_call(): pl.pallas_call(kernel, grid=() if whole else (steps,), in_specs=in_specs,...  21.1 us
  transfers between devices with their start and end apart: 30, of which 15 were waited for; matrix products, arithmetic and copies ran while one was open for 0% of the time, Pallas kernels for 17%

profile of v6, /device:TPU:0, one launch (start us, length us, event | category | flops | bytes accessed | tf_op | source)
XLA Modules:
  0.0 97.8 jit_solution(1909283145190850484)
XLA Ops:
  0.0 2.3 %msa_stage.1 = (bf16[17,16,128]{2,1,0:T(8,128)(2,1)S(1)}, bf16[256,128]{1,0:T(8,128)(2,1)S(1)}) custom-call(bf16[64,16,256]{2,1,0:T(8,128)(2,1)} %msa_ref.1, s32[16,64]{1,0:T(8,128)} %bitcast.20, bf16[32,256]{1,0:T(8,128)(2,1)} %bitcast.18, bf16[32,256]{1,0:T(8,128)(2,1)} %bitcast.19), custom_call_target="tpu_custom_call" | custom-call | flops 33554 | bytes 524 | tf_op jit(solution)/shard_map/msa_stage/pallas_call | solution.py:49
  2.4 5.1 %collective-permute-start.2 = (bf16[33,16,128]{2,1,0:T(8,128)(2,1)S(1)}, bf16[33,16,128]{2,1,0:T(8,128)(2,1)S(1)}, u32[]{:S(2)}, u32[]{:S(2)}) collective-permute-start(bf16[33,16,128]{2,1,0:T(8,128)(2,1)S(1)} %pad_maximum_fusion.1), channel_id=1, source_target_pairs={{0,12},{1,13},{2,14},{3,15},{4,8},{5,9},{6,10},{7,11},{8,4},{9,5},... | collective-permute-start | bytes 405512 | tf_op jit(solution)/shard_map/ppermute | solution.py:542
  8.1 1.7 %weights_stage.1 = (bf16[128,1024]{1,0:T(8,128)(2,1)S(1)}, bf16[512,128]{1,0:T(8,128)(2,1)S(1)}, bf16[128,128]{1,0:T(8,128)(2,1)S(1)}, bf16[128,128]{1,0:T(8,128...) custom-call(bf16[1024,128]{1,0:T(8,128)(2,1)} %refs_0_.1, bf16[128,512]{1,0:T(8,128)(2,1)} %refs_1_.1, ...), custom_call_target="tpu_custom_call" | custom-call | flops 25165 | bytes 524 | tf_op jit(solution)/shard_map/weights_stage/pallas_call | solution.py:49
  9.8 2.2 %collective-permute-done.2 = bf16[33,16,128]{2,1,0:T(8,128)(2,1)S(1)} collective-permute-done((bf16[33,16,128]{2,1,0:T(8,128)(2,1)S(1)}, bf16[33,16,128]{2,1,0:T(8,128)(2,1)S(1)}, u32[]{:S(2)}, u32[]{:S(2)}) %collective-permute-start.2) | collective-permute-done | bytes 135200 | tf_op jit(solution)/shard_map/ppermute | solution.py:542
  12.7 3.4 %collective-permute-done.1 = bf16[17,16,128]{2,1,0:T(8,128)(2,1)S(1)} collective-permute-done((bf16[17,16,128]{2,1,0:T(8,128)(2,1)S(1)}, bf16[17,16,128]{2,1,0:T(8,128)(2,1)S(1)}, u32[]{:S(2)}, u32[]{:S(2)}) %collective-permute-start.1) | collective-permute-done | bytes 69664 | tf_op jit(solution)/shard_map/ppermute | solution.py:542
  16.1 2.5 %collective-permute-start.9 = (bf16[16,256,128]{2,1,0:T(8,128)(2,1)}, bf16[16,256,128]{2,1,0:T(8,128)(2,1)S(1)}, u32[]{:S(2)}, u32[]{:S(2)}) collective-permute-start(bf16[16,256,128]{2,1,0:T(8,128)(2,1)} %refs_2_.3), channel_id=1, source_target_pairs={{0,12},{1,13},{2,14},{3,15},{4,8},{5,9},{6,10},{7,11},{8,4},{9,5},... | collective-permute-start | bytes 3145736 | tf_op jit(solution)/shard_map/ppermute | solution.py:542
  20.2 5.7 %collective-permute-done.3.refs_7_ = bf16[4,17,16,128]{3,2,1,0:T(8,128)(2,1)S(1)} collective-permute-done((bf16[4,17,16,128]{3,2,1,0:T(8,128)(2,1)S(1)}, bf16[4,17,16,128]{3,2,1,0:T(8,128)(2,1)S(1)}, u32[]{:S(2)}, u32[]{:S(2)}) %collective-permute-start.3) | collective-permute-done | bytes 278560 | tf_op jit(solution)/shard_map/ppermute | solution.py:542
  27.5 6.2 %pair_stage.1 = (f32[16,128,256]{2,1,0:T(8,128)S(1)}, bf16[1,32,16,256]{3,2,1,0:T(8,128)(2,1)S(1)}, bf16[1,32,16,256]{3,2,1,0:T(8,128)(2,1)S(1)}, bf16[1,32,16,2...) custom-call(bf16[256,128]{1,0:T(8,128)(2,1)S(1)} %get-tuple-element., ...), custom_call_target="tpu_custom_call" | custom-call | flops 2147483 | bytes 8388 | tf_op jit(solution)/shard_map/pair_stage/pallas_call | solution.py:49
  35.2 2.0 %collective-permute-start.12 = (bf16[1,32,16,256]{3,2,1,0:T(8,128)(2,1)S(1)}, bf16[1,32,16,256]{3,2,1,0:T(8,128)(2,1)S(1)}, u32[]{:S(2)}, u32[]{:S(2)}) collective-permute-start(bf16[1,32,16,256]{3,2,1,0:T(8,128)(2,1)S(1)} %get-tuple-element.92), channel_id=1, source_target_pairs={{0,4},{1,5},{2,6},{3,7},{4,0},{5,1},{6,2},{7,3},{8,12},{9,13},{10,... | collective-permute-start | bytes 786440 | tf_op jit(solution)/shard_map/ppermute | solution.py:542
  37.2 5.8 %collective-permute-done.8.refs_5_ = bf16[1,32,16,256]{3,2,1,0:T(8,128)(2,1)S(1)} collective-permute-done((bf16[1,32,16,256]{3,2,1,0:T(8,128)(2,1)S(1)}, bf16[1,32,16,256]{3,2,1,0:T(8,128)(2,1)S(1)}, u32[]{:S(2)}, u32[]{:S(2)}) %collective-permute-start.8) | collective-permute-done | bytes 262176 | tf_op jit(solution)/shard_map/ppermute | solution.py:542
  43.0 2.5 %collective-permute-start.11 = (bf16[1,32,16,256]{3,2,1,0:T(8,128)(2,1)S(1)}, bf16[1,32,16,256]{3,2,1,0:T(8,128)(2,1)S(1)}, u32[]{:S(2)}, u32[]{:S(2)}) collective-permute-start(bf16[1,32,16,256]{3,2,1,0:T(8,128)(2,1)S(1)} %get-tuple-element.91), channel_id=1, source_target_pairs={{0,2},{1,3},{2,0},{3,1},{4,6},{5,7},{6,4},{7,5},{8,10},{9,11},{10,... | collective-permute-start | bytes 786440 | tf_op jit(solution)/shard_map/ppermute | solution.py:542
  45.6 3.4 %collective-permute-done.6.refs_7_ = bf16[1,32,16,256]{3,2,1,0:T(8,128)(2,1)S(1)} collective-permute-done((bf16[1,32,16,256]{3,2,1,0:T(8,128)(2,1)S(1)}, bf16[1,32,16,256]{3,2,1,0:T(8,128)(2,1)S(1)}, u32[]{:S(2)}, u32[]{:S(2)}) %collective-permute-start.6) | collective-permute-done | bytes 262176 | tf_op jit(solution)/shard_map/ppermute | solution.py:542
  48.9 2.6 %collective-permute-start.7 = (bf16[1,32,16,256]{3,2,1,0:T(8,128)(2,1)S(1)}, bf16[1,32,16,256]{3,2,1,0:T(8,128)(2,1)S(1)}, u32[]{:S(2)}, u32[]{:S(2)}) collective-permute-start(bf16[1,32,16,256]{3,2,1,0:T(8,128)(2,1)S(1)} %get-tuple-element.75), channel_id=1, source_target_pairs={{0,6},{1,7},{2,4},{3,5},{4,2},{5,3},{6,0},{7,1},{8,14},{9,15},{10,... | collective-permute-start | bytes 786440 | tf_op jit(solution)/shard_map/ppermute | solution.py:542
  51.6 3.5 %update_stage.1.update_ref = f32[16,128,256]{2,1,0:T(8,128)S(1)} custom-call(bf16[256,128]{1,0:T(8,128)(2,1)S(1)} %bitcast.14, bf16[128,1024]{1,0:T(8,128)(2,1)S(1)} %get-tuple-element.69.refs_3_.w_out_ref, bf16[16,17,16,128]{3,2,1,0:T(8,128)(2,1)S(1)} %get-tuple-element.78.right), custom_call_target="tpu_custom_call" | custom-call | flops 2147483 | bytes 4194 | tf_op jit(solution)/shard_map/update_stage/pallas_call | solution.py:49
  56.3 1.9 %mirror_stage.1 = (bf16[1,32,16,256]{3,2,1,0:T(8,128)(2,1)S(1)}, bf16[1,32,16,256]{3,2,1,0:T(8,128)(2,1)S(1)}, bf16[1,32,16,256]{3,2,1,0:T(8,128)(2,1)S(1)}, bf16[1,32,16,256]{3,2,1,0:T(8,128)(2,1)S(1)}) custom-call(f32[16,128,256]{2,1,0:T(8,128)S(1)} %update_stage.1.update_ref, bf16[16,256,128]{2,1,0:T(8,128)(2,1)S(1)} %collective-permute-done.9.couple_ref, ...), custom_call_target="tpu_custom_call" | custom-call | flops 268435 | bytes 20971520 | tf_op jit(solution)/shard_map/mirror_stage/pallas_call | solution.py:49
  60.2 4.5 %collective-permute-start.18 = (bf16[1,32,16,256]{3,2,1,0:T(8,128)(2,1)S(1)}, bf16[1,32,16,256]{3,2,1,0:T(8,128)(2,1)S(1)}, u32[]{:S(2)}, u32[]{:S(2)}) collective-permute-start(bf16[1,32,16,256]{3,2,1,0:T(8,128)(2,1)S(1)} %get-tuple-element.103), channel_id=1, source_target_pairs={{0,4},{1,5},{2,6},{3,7},{4,0},{5,1},{6,2},{7,3},{8,12},{9,13},{10,... | collective-permute-start | bytes 786440 | tf_op jit(solution)/shard_map/ppermute | solution.py:542
  64.8 1.7 %collective-permute-start.19 = (bf16[1,32,16,256]{3,2,1,0:T(8,128)(2,1)S(1)}, bf16[1,32,16,256]{3,2,1,0:T(8,128)(2,1)S(1)}, u32[]{:S(2)}, u32[]{:S(2)}) collective-permute-start(bf16[1,32,16,256]{3,2,1,0:T(8,128)(2,1)S(1)} %get-tuple-element.104), channel_id=1, source_target_pairs={{0,6},{1,7},{2,4},{3,5},{4,2},{5,3},{6,0},{7,1},{8,14},{9,15},{10,... | collective-permute-start | bytes 786440 | tf_op jit(solution)/shard_map/ppermute | solution.py:542
  67.8 4.1 %collective-permute-done.18.refs_6_ = bf16[1,32,16,256]{3,2,1,0:T(8,128)(2,1)S(1)} collective-permute-done((bf16[1,32,16,256]{3,2,1,0:T(8,128)(2,1)S(1)}, bf16[1,32,16,256]{3,2,1,0:T(8,128)(2,1)S(1)}, u32[]{:S(2)}, u32[]{:S(2)}) %collective-permute-start.18) | collective-permute-done | bytes 262176 | tf_op jit(solution)/shard_map/ppermute | solution.py:542
  71.9 6.4 %collective-permute-done.19.refs_7_ = bf16[1,32,16,256]{3,2,1,0:T(8,128)(2,1)S(1)} collective-permute-done((bf16[1,32,16,256]{3,2,1,0:T(8,128)(2,1)S(1)}, bf16[1,32,16,256]{3,2,1,0:T(8,128)(2,1)S(1)}, u32[]{:S(2)}, u32[]{:S(2)}) %collective-permute-start.19) | collective-permute-done | bytes 262176 | tf_op jit(solution)/shard_map/ppermute | solution.py:542
  81.3 1.6 %collective-permute-start.28 = (bf16[1,32,16,128]{3,2,1,0:T(8,128)(2,1)S(1)}, bf16[1,32,16,128]{3,2,1,0:T(8,128)(2,1)S(1)}, u32[]{:S(2)}, u32[]{:S(2)}) collective-permute-start(bf16[1,32,16,128]{3,2,1,0:T(8,128)(2,1)S(1)} %get-tuple-element.115), channel_id=1, source_target_pairs={{0,4},{1,5},{2,6},{3,7},{4,0},{5,1},{6,2},{7,3},{8,12},{9,13},{10,... | collective-permute-start | bytes 393224 | tf_op jit(solution)/shard_map/ppermute | solution.py:542
  85.7 1.6 %collective-permute-start.25 = (bf16[1,32,16,128]{3,2,1,0:T(8,128)(2,1)S(1)}, bf16[1,32,16,128]{3,2,1,0:T(8,128)(2,1)S(1)}, u32[]{:S(2)}, u32[]{:S(2)}) collective-permute-start(bf16[1,32,16,128]{3,2,1,0:T(8,128)(2,1)S(1)} %get-tuple-element.111), channel_id=1, source_target_pairs={{0,4},{1,5},{2,6},{3,7},{4,0},{5,1},{6,2},{7,3},{8,12},{9,13},{10,... | collective-permute-start | bytes 393224 | tf_op jit(solution)/shard_map/ppermute | solution.py:542
  89.6 1.7 %collective-permute-done.29.refs_3_ = bf16[1,32,16,128]{3,2,1,0:T(8,128)(2,1)S(1)} collective-permute-done((bf16[1,32,16,128]{3,2,1,0:T(8,128)(2,1)S(1)}, bf16[1,32,16,128]{3,2,1,0:T(8,128)(2,1)S(1)}, u32[]{:S(2)}, u32[]{:S(2)}) %collective-permute-start.29) | collective-permute-done | bytes 131104 | tf_op jit(solution)/shard_map/ppermute | solution.py:542
  93.3 2.5 %collective-permute-done.26.refs_6_ = bf16[1,32,16,128]{3,2,1,0:T(8,128)(2,1)S(1)} collective-permute-done((bf16[1,32,16,128]{3,2,1,0:T(8,128)(2,1)S(1)}, bf16[1,32,16,128]{3,2,1,0:T(8,128)(2,1)S(1)}, u32[]{:S(2)}, u32[]{:S(2)}) %collective-permute-start.26) | collective-permute-done | bytes 131104 | tf_op jit(solution)/shard_map/ppermute | solution.py:542
  95.8 2.0 %final_stage.1 = bf16[16,256,128]{2,1,0:T(8,128)(2,1)} custom-call(f32[16,128,256]{2,1,0:T(8,128)S(1)} %get-tuple-element.86.pair_ref.refs_0_, f32[16,128,256]{2,1,0:T(8,128)S(1)} %gate_stage.1.gate_ref.refs_1_, bf16[128,128]{1,0:T(8,128)(2,1)S(1)} %get-tuple-element.88.w_ref.refs_2_, bf16[1,32,16,128]{3,2,1,0:T(8,128)(2,1)S(1)} %get-tuple-element.109.refs_3_, ...), custom_call_target="tpu_custom_call" | custom-call | flops 134217 | bytes 6291 | tf_op jit(solution)/shard_map/final_stage/pallas_call | solution.py:49
  (53 shorter events, 20.7 us)
Async XLA Ops:
  2.4 9.6 %collective-permute-start.2 = (bf16[33,16,128]{2,1,0:T(8,128)(2,1)S(1)}, bf16[33,16,128]{2,1,0:T(8,128)(2,1)S(1)}, u32[]{:S(2)}, u32[]{:S(2)}) collective-permute-start(bf16[33,16,128]{2,1,0:T(8,128)(2,1)S(1)} %pad_maximum_fusion.1), channel_id=1, source_target_pairs={{0,12},{1,13},{2,14},{3,15},{4,8},{5,9},{6,10},{7,11},{8,4},{9,5},... | collective-permute-start | bytes 405512 | tf_op jit(solution)/shard_map/ppermute | solution.py:542
  7.5 8.6 %collective-permute-start.1 = (bf16[17,16,128]{2,1,0:T(8,128)(2,1)S(1)}, bf16[17,16,128]{2,1,0:T(8,128)(2,1)S(1)}, u32[]{:S(2)}, u32[]{:S(2)}) collective-permute-start(bf16[17,16,128]{2,1,0:T(8,128)(2,1)S(1)} %get-tuple-element.62), channel_id=1, source_target_pairs={{0,8},{1,9},{2,10},{3,11},{4,12},{5,13},{6,14},{7,15},{8,0},{9,1},... | collective-permute-start | bytes 208904 | tf_op jit(solution)/shard_map/ppermute | solution.py:542
  16.1 40.2 %collective-permute-start.9 = (bf16[16,256,128]{2,1,0:T(8,128)(2,1)}, bf16[16,256,128]{2,1,0:T(8,128)(2,1)S(1)}, u32[]{:S(2)}, u32[]{:S(2)}) collective-permute-start(bf16[16,256,128]{2,1,0:T(8,128)(2,1)} %refs_2_.3), channel_id=1, source_target_pairs={{0,12},{1,13},{2,14},{3,15},{4,8},{5,9},{6,10},{7,11},{8,4},{9,5},... | collective-permute-start | bytes 3145736 | tf_op jit(solution)/shard_map/ppermute | solution.py:542
  18.7 7.2 %collective-permute-start.3 = (bf16[4,17,16,128]{3,2,1,0:T(8,128)(2,1)S(1)}, bf16[4,17,16,128]{3,2,1,0:T(8,128)(2,1)S(1)}, u32[]{:S(2)}, u32[]{:S(2)}) collective-permute-start(bf16[4,17,16,128]{3,2,1,0:T(8,128)(2,1)S(1)} %pad_maximum_fusion.refs_6_), channel_id=1, source_target_pairs={{0,2},{1,3},{2,0},{3,1},{4,6},{5,7},{6,4},{7,5},{8,10},{9,11},{10,... | collective-permute-start | bytes 835592 | tf_op jit(solution)/shard_map/ppermute | solution.py:542
  20.2 5.7 %collective-permute-start.4 = (bf16[4,17,16,128]{3,2,1,0:T(8,128)(2,1)S(1)}, bf16[4,17,16,128]{3,2,1,0:T(8,128)(2,1)S(1)}, u32[]{:S(2)}, u32[]{:S(2)}) collective-permute-start(bf16[4,17,16,128]{3,2,1,0:T(8,128)(2,1)S(1)} %pad_maximum_fusion.refs_6_), channel_id=1, source_target_pairs={{0,1},{1,0},{2,3},{3,2},{4,5},{5,4},{6,7},{7,6},{8,9},{9,8},{10,11... | collective-permute-start | bytes 835592 | tf_op jit(solution)/shard_map/ppermute | solution.py:542
  33.7 9.4 %collective-permute-start.8 = (bf16[1,32,16,256]{3,2,1,0:T(8,128)(2,1)S(1)}, bf16[1,32,16,256]{3,2,1,0:T(8,128)(2,1)S(1)}, u32[]{:S(2)}, u32[]{:S(2)}) collective-permute-start(bf16[1,32,16,256]{3,2,1,0:T(8,128)(2,1)S(1)} %get-tuple-element.76), channel_id=1, source_target_pairs={{0,2},{1,3},{2,0},{3,1},{4,6},{5,7},{6,4},{7,5},{8,10},{9,11},{10,... | collective-permute-start | bytes 786440 | tf_op jit(solution)/shard_map/ppermute | solution.py:542
  35.2 13.7 %collective-permute-start.6 = (bf16[1,32,16,256]{3,2,1,0:T(8,128)(2,1)S(1)}, bf16[1,32,16,256]{3,2,1,0:T(8,128)(2,1)S(1)}, u32[]{:S(2)}, u32[]{:S(2)}) collective-permute-start(bf16[1,32,16,256]{3,2,1,0:T(8,128)(2,1)S(1)} %get-tuple-element.73), channel_id=1, source_target_pairs={{0,6},{1,7},{2,4},{3,5},{4,2},{5,3},{6,0},{7,1},{8,14},{9,15},{10,... | collective-permute-start | bytes 786440 | tf_op jit(solution)/shard_map/ppermute | solution.py:542
  35.2 19.8 %collective-permute-start.12 = (bf16[1,32,16,256]{3,2,1,0:T(8,128)(2,1)S(1)}, bf16[1,32,16,256]{3,2,1,0:T(8,128)(2,1)S(1)}, u32[]{:S(2)}, u32[]{:S(2)}) collective-permute-start(bf16[1,32,16,256]{3,2,1,0:T(8,128)(2,1)S(1)} %get-tuple-element.92), channel_id=1, source_target_pairs={{0,4},{1,5},{2,6},{3,7},{4,0},{5,1},{6,2},{7,3},{8,12},{9,13},{10,... | collective-permute-start | bytes 786440 | tf_op jit(solution)/shard_map/ppermute | solution.py:542
  37.2 23.0 %collective-permute-start.14 = (bf16[1,32,16,256]{3,2,1,0:T(8,128)(2,1)S(1)}, bf16[1,32,16,256]{3,2,1,0:T(8,128)(2,1)S(1)}, u32[]{:S(2)}, u32[]{:S(2)}) collective-permute-start(bf16[1,32,16,256]{3,2,1,0:T(8,128)(2,1)S(1)} %get-tuple-element.95.refs_4_), channel_id=1, source_target_pairs={{0,1},{1,0},{2,3},{3,2},{4,5},{5,4},{6,7},{7,6},{8,9},{9,8},{10,11... | collective-permute-start | bytes 786440 | tf_op jit(solution)/shard_map/ppermute | solution.py:542
  43.0 15.2 %collective-permute-start.11 = (bf16[1,32,16,256]{3,2,1,0:T(8,128)(2,1)S(1)}, bf16[1,32,16,256]{3,2,1,0:T(8,128)(2,1)S(1)}, u32[]{:S(2)}, u32[]{:S(2)}) collective-permute-start(bf16[1,32,16,256]{3,2,1,0:T(8,128)(2,1)S(1)} %get-tuple-element.91), channel_id=1, source_target_pairs={{0,2},{1,3},{2,0},{3,1},{4,6},{5,7},{6,4},{7,5},{8,10},{9,11},{10,... | collective-permute-start | bytes 786440 | tf_op jit(solution)/shard_map/ppermute | solution.py:542
  48.9 11.2 %collective-permute-start.7 = (bf16[1,32,16,256]{3,2,1,0:T(8,128)(2,1)S(1)}, bf16[1,32,16,256]{3,2,1,0:T(8,128)(2,1)S(1)}, u32[]{:S(2)}, u32[]{:S(2)}) collective-permute-start(bf16[1,32,16,256]{3,2,1,0:T(8,128)(2,1)S(1)} %get-tuple-element.75), channel_id=1, source_target_pairs={{0,6},{1,7},{2,4},{3,5},{4,2},{5,3},{6,0},{7,1},{8,14},{9,15},{10,... | collective-permute-start | bytes 786440 | tf_op jit(solution)/shard_map/ppermute | solution.py:542
  55.1 9.7 %collective-permute-start.13 = (bf16[1,32,16,256]{3,2,1,0:T(8,128)(2,1)S(1)}, bf16[1,32,16,256]{3,2,1,0:T(8,128)(2,1)S(1)}, u32[]{:S(2)}, u32[]{:S(2)}) collective-permute-start(bf16[1,32,16,256]{3,2,1,0:T(8,128)(2,1)S(1)} %get-tuple-element.94), channel_id=1, source_target_pairs={{0,4},{1,5},{2,6},{3,7},{4,0},{5,1},{6,2},{7,3},{8,12},{9,13},{10,... | collective-permute-start | bytes 786440 | tf_op jit(solution)/shard_map/ppermute | solution.py:542
  56.3 10.1 %collective-permute-start.15 = (bf16[1,32,16,256]{3,2,1,0:T(8,128)(2,1)S(1)}, bf16[1,32,16,256]{3,2,1,0:T(8,128)(2,1)S(1)}, u32[]{:S(2)}, u32[]{:S(2)}) collective-permute-start(bf16[1,32,16,256]{3,2,1,0:T(8,128)(2,1)S(1)} %collective-permute-done.8.refs_5_), channel_id=1, source_target_pairs={{0,1},{1,0},{2,3},{3,2},{4,5},{5,4},{6,7},{7,6},{8,9},{9,8},{10,11... | collective-permute-start | bytes 786440 | tf_op jit(solution)/shard_map/ppermute | solution.py:542
  58.3 8.7 %collective-permute-start.16 = (bf16[1,32,16,256]{3,2,1,0:T(8,128)(2,1)S(1)}, bf16[1,32,16,256]{3,2,1,0:T(8,128)(2,1)S(1)}, u32[]{:S(2)}, u32[]{:S(2)}) collective-permute-start(bf16[1,32,16,256]{3,2,1,0:T(8,128)(2,1)S(1)} %collective-permute-done.12.refs_6_), channel_id=1, source_target_pairs={{0,1},{1,0},{2,3},{3,2},{4,5},{5,4},{6,7},{7,6},{8,9},{9,8},{10,11... | collective-permute-start | bytes 786440 | tf_op jit(solution)/shard_map/ppermute | solution.py:542
  60.2 6.8 %collective-permute-start.17 = (bf16[1,32,16,256]{3,2,1,0:T(8,128)(2,1)S(1)}, bf16[1,32,16,256]{3,2,1,0:T(8,128)(2,1)S(1)}, u32[]{:S(2)}, u32[]{:S(2)}) collective-permute-start(bf16[1,32,16,256]{3,2,1,0:T(8,128)(2,1)S(1)} %collective-permute-done.6.refs_7_), channel_id=1, source_target_pairs={{0,1},{1,0},{2,3},{3,2},{4,5},{5,4},{6,7},{7,6},{8,9},{9,8},{10,11... | collective-permute-start | bytes 786440 | tf_op jit(solution)/shard_map/ppermute | solution.py:542
  60.2 11.7 %collective-permute-start.18 = (bf16[1,32,16,256]{3,2,1,0:T(8,128)(2,1)S(1)}, bf16[1,32,16,256]{3,2,1,0:T(8,128)(2,1)S(1)}, u32[]{:S(2)}, u32[]{:S(2)}) collective-permute-start(bf16[1,32,16,256]{3,2,1,0:T(8,128)(2,1)S(1)} %get-tuple-element.103), channel_id=1, source_target_pairs={{0,4},{1,5},{2,6},{3,7},{4,0},{5,1},{6,2},{7,3},{8,12},{9,13},{10,... | collective-permute-start | bytes 786440 | tf_op jit(solution)/shard_map/ppermute | solution.py:542
  64.8 13.5 %collective-permute-start.19 = (bf16[1,32,16,256]{3,2,1,0:T(8,128)(2,1)S(1)}, bf16[1,32,16,256]{3,2,1,0:T(8,128)(2,1)S(1)}, u32[]{:S(2)}, u32[]{:S(2)}) collective-permute-start(bf16[1,32,16,256]{3,2,1,0:T(8,128)(2,1)S(1)} %get-tuple-element.104), channel_id=1, source_target_pairs={{0,6},{1,7},{2,4},{3,5},{4,2},{5,3},{6,0},{7,1},{8,14},{9,15},{10,... | collective-permute-start | bytes 786440 | tf_op jit(solution)/shard_map/ppermute | solution.py:542
  66.5 13.3 %collective-permute-start.10 = (bf16[1,32,16,256]{3,2,1,0:T(8,128)(2,1)S(1)}, bf16[1,32,16,256]{3,2,1,0:T(8,128)(2,1)S(1)}, u32[]{:S(2)}, u32[]{:S(2)}) collective-permute-start(bf16[1,32,16,256]{3,2,1,0:T(8,128)(2,1)S(1)} %get-tuple-element.84), channel_id=1, source_target_pairs={{0,2},{1,3},{2,0},{3,1},{4,6},{5,7},{6,4},{7,5},{8,10},{9,11},{10,... | collective-permute-start | bytes 786440 | tf_op jit(solution)/shard_map/ppermute | solution.py:542
  80.8 6.6 %collective-permute-start.27 = (bf16[1,32,16,128]{3,2,1,0:T(8,128)(2,1)S(1)}, bf16[1,32,16,128]{3,2,1,0:T(8,128)(2,1)S(1)}, u32[]{:S(2)}, u32[]{:S(2)}) collective-permute-start(bf16[1,32,16,128]{3,2,1,0:T(8,128)(2,1)S(1)} %get-tuple-element.114), channel_id=1, source_target_pairs={{0,2},{1,3},{2,0},{3,1},{4,6},{5,7},{6,4},{7,5},{8,10},{9,11},{10,... | collective-permute-start | bytes 393224 | tf_op jit(solution)/shard_map/ppermute | solution.py:542
  81.3 8.2 %collective-permute-start.28 = (bf16[1,32,16,128]{3,2,1,0:T(8,128)(2,1)S(1)}, bf16[1,32,16,128]{3,2,1,0:T(8,128)(2,1)S(1)}, u32[]{:S(2)}, u32[]{:S(2)}) collective-permute-start(bf16[1,32,16,128]{3,2,1,0:T(8,128)(2,1)S(1)} %get-tuple-element.115), channel_id=1, source_target_pairs={{0,4},{1,5},{2,6},{3,7},{4,0},{5,1},{6,2},{7,3},{8,12},{9,13},{10,... | collective-permute-start | bytes 393224 | tf_op jit(solution)/shard_map/ppermute | solution.py:542
  83.0 8.3 %collective-permute-start.29 = (bf16[1,32,16,128]{3,2,1,0:T(8,128)(2,1)S(1)}, bf16[1,32,16,128]{3,2,1,0:T(8,128)(2,1)S(1)}, u32[]{:S(2)}, u32[]{:S(2)}) collective-permute-start(bf16[1,32,16,128]{3,2,1,0:T(8,128)(2,1)S(1)} %get-tuple-element.116), channel_id=1, source_target_pairs={{0,6},{1,7},{2,4},{3,5},{4,2},{5,3},{6,0},{7,1},{8,14},{9,15},{10,... | collective-permute-start | bytes 393224 | tf_op jit(solution)/shard_map/ppermute | solution.py:542
  85.1 7.4 %collective-permute-start.24 = (bf16[1,32,16,128]{3,2,1,0:T(8,128)(2,1)S(1)}, bf16[1,32,16,128]{3,2,1,0:T(8,128)(2,1)S(1)}, u32[]{:S(2)}, u32[]{:S(2)}) collective-permute-start(bf16[1,32,16,128]{3,2,1,0:T(8,128)(2,1)S(1)} %get-tuple-element.110), channel_id=1, source_target_pairs={{0,2},{1,3},{2,0},{3,1},{4,6},{5,7},{6,4},{7,5},{8,10},{9,11},{10,... | collective-permute-start | bytes 393224 | tf_op jit(solution)/shard_map/ppermute | solution.py:542
  85.7 7.6 %collective-permute-start.25 = (bf16[1,32,16,128]{3,2,1,0:T(8,128)(2,1)S(1)}, bf16[1,32,16,128]{3,2,1,0:T(8,128)(2,1)S(1)}, u32[]{:S(2)}, u32[]{:S(2)}) collective-permute-start(bf16[1,32,16,128]{3,2,1,0:T(8,128)(2,1)S(1)} %get-tuple-element.111), channel_id=1, source_target_pairs={{0,4},{1,5},{2,6},{3,7},{4,0},{5,1},{6,2},{7,3},{8,12},{9,13},{10,... | collective-permute-start | bytes 393224 | tf_op jit(solution)/shard_map/ppermute | solution.py:542
  87.3 8.4 %collective-permute-start.26 = (bf16[1,32,16,128]{3,2,1,0:T(8,128)(2,1)S(1)}, bf16[1,32,16,128]{3,2,1,0:T(8,128)(2,1)S(1)}, u32[]{:S(2)}, u32[]{:S(2)}) collective-permute-start(bf16[1,32,16,128]{3,2,1,0:T(8,128)(2,1)S(1)} %get-tuple-element.112), channel_id=1, source_target_pairs={{0,6},{1,7},{2,4},{3,5},{4,2},{5,3},{6,0},{7,1},{8,14},{9,15},{10,... | collective-permute-start | bytes 393224 | tf_op jit(solution)/shard_map/ppermute | solution.py:542
  (7 other events, 47.1 us)
